TPU v7x, 1024 devices: a whole 8x8x8 slice. The times are simulated.
1024 devices in a mesh: expert: 8 (over x), tensor: 16 (over y, core), dp: 8 (over z).
Axes of the slice: x: 8, y: 8, z: 8, core: 2. Of those that a mesh axis runs over, the one named last changes fastest.
Arguments:
- tokens: bfloat16 [512, 6144], P(('expert', 'tensor'), 'dp'), may hold values from -6 to 6
- grad_output: bfloat16 [512, 6144], P(('expert', 'tensor'), 'dp'), may hold values from -6 to 6
- expert_ids: int32 [512, 4], P(('expert', 'tensor')), may hold values from 0 to 7, all different within a row; in each aligned block of 4 rows (0 to 3, 4 to 7, ...) at most 3 rows name the same one
- gate_weights: bfloat16 [512, 4], P(('expert', 'tensor')), may hold values from 0.099609375 to 1
- w_in: bfloat16 [8, 6144, 12288], P('expert', 'dp', 'tensor'), may hold values from -0.078125 to 0.078125
- scale_in: bfloat16 [8, 12288], P('expert', 'tensor'), may hold values from 1.3953799e-05 to 8.685528e-05, as said below
- w_out: bfloat16 [8, 6144, 6144], P('expert', 'tensor', 'dp'), may hold values from -0.078125 to 0.078125
- scale_out: bfloat16 [8, 6144], P('expert', 'dp'), may hold values from 1.3953799e-05 to 8.685528e-05, as said below
Outputs:
- grad_tokens: bfloat16 [512, 6144], P(('expert', 'tensor'), 'dp')
- grad_in: bfloat16 [8, 6144, 12288], P('expert', 'dp', 'tensor')
- grad_out: bfloat16 [8, 6144, 6144], P('expert', 'tensor', 'dp')
Inputs may be any that keep to these rules, and one draw needn't show every extreme that they name: `expert_ids`: each row names 4 different experts; within each aligned block of 4 tokens no expert is named by more than 3 tokens, a bound that some block reaches. `scale_in`: positive per-column scales. `scale_out`: positive per-column scales.
All inputs are finite; a program needn't handle non-finite values.
Results may differ from a plain program's by a relative error of at most 0.01.
Values may be sent and summed in bfloat16 or wider, within the bound.
No kernel may reach another device: no remote copies, remote signals or barrier semaphores. Data moves between devices by JAX's collectives and lax.ppermute only.
A program may use at most 32 MiB of HBM per device.

v0:
```python
import jax
import jax.numpy as jnp
from jax import lax
from jax.sharding import PartitionSpec as P

CAP = 3


def clip_only(weights, scales):
    bound = 448.0 * scales.astype(jnp.float32)
    return jnp.clip(weights.astype(jnp.float32), -bound, bound).astype(jnp.bfloat16)


def keep_mask(weights, scales):
    return (jnp.abs(weights.astype(jnp.float32)) <= 448.0 * scales.astype(jnp.float32)).astype(
        jnp.float32
    )


def activate(pre_sum, back_sum, gate_rows, unit_share):
    gate_pre = pre_sum[..., :unit_share]
    up_pre = pre_sum[..., unit_share:]
    d_act = gate_rows * back_sum
    sigmoid_gate = jax.nn.sigmoid(gate_pre)
    silu_gate = gate_pre * sigmoid_gate
    slope = sigmoid_gate * (1.0 + gate_pre * (1.0 - sigmoid_gate))
    scaled_act = (gate_rows * silu_gate * up_pre).astype(jnp.bfloat16)
    d_hidden = jnp.concatenate([d_act * up_pre * slope, d_act * silu_gate], axis=-1).astype(
        jnp.bfloat16
    )
    return (d_hidden, scaled_act)


def per_device(tokens, grad_output, expert_ids, gate_weights, w_in, scale_in, w_out, scale_out):
    n_expert = lax.axis_size("expert")
    n_tensor = lax.axis_size("tensor")
    tok_rows, slice_width = tokens.shape
    top_count = expert_ids.shape[1]
    local_count = w_in.shape[0]
    expert_count = local_count * n_expert
    unit_share = w_out.shape[1]
    capacity = CAP
    assigned = tok_rows * top_count
    flat_ids = expert_ids.reshape(assigned)
    matches = (flat_ids[:, None] == jnp.arange(expert_count, dtype=jnp.int32)[None, :]).astype(
        jnp.int32
    )
    ranking = jnp.sum((jnp.cumsum(matches, axis=0) - 1) * matches, axis=1)
    target = flat_ids * capacity + ranking
    placer = (
        jnp.arange(expert_count * capacity, dtype=jnp.int32)[:, None] == target[None, :]
    ).astype(jnp.bfloat16)

    def to_slots(rows):
        spread = jnp.repeat(rows, top_count, axis=0)
        placed = jnp.dot(placer, spread, preferred_element_type=jnp.float32)
        return placed.astype(jnp.bfloat16).reshape(expert_count, capacity, rows.shape[1])

    feature_slots = to_slots(tokens)
    cotan_slots = to_slots(grad_output)
    gate_slots = jnp.dot(placer, gate_weights.reshape(assigned), preferred_element_type=jnp.float32)
    gate_slots = gate_slots.astype(jnp.bfloat16).reshape(expert_count, capacity)
    recv_x, recv_dy, recv_gate = (
        lax.all_to_all(feature_slots, "expert", split_axis=0, concat_axis=0, tiled=True),
        lax.all_to_all(cotan_slots, "expert", split_axis=0, concat_axis=0, tiled=True),
        lax.all_to_all(gate_slots, "expert", split_axis=0, concat_axis=0, tiled=True),
    )
    full_x, full_dy, full_gate = (
        lax.all_gather(recv_x, "tensor", axis=1, tiled=True),
        lax.all_gather(recv_dy, "tensor", axis=1, tiled=True),
        lax.all_gather(recv_gate, "tensor", axis=1, tiled=True),
    )
    routed = n_tensor * capacity
    full_x = full_x.reshape(n_expert, local_count, routed, slice_width)
    full_dy = full_dy.reshape(n_expert, local_count, routed, slice_width)
    gate_local = full_gate.reshape(n_expert, local_count, routed).astype(jnp.float32)[..., None]
    wq_in = clip_only(w_in, scale_in[:, None, :])
    wq_out = clip_only(w_out, scale_out[:, None, :])
    pre_part = jnp.einsum("slrd,ldf->slrf", full_x, wq_in, preferred_element_type=jnp.float32)
    back_part = jnp.einsum("slrd,lfd->slrf", full_dy, wq_out, preferred_element_type=jnp.float32)
    pre_full, back_full = lax.psum((pre_part, back_part), "dp")
    d_hidden, scaled_act = activate(pre_full, back_full, gate_local, unit_share)
    dx_part = jnp.einsum("slrf,ldf->slrd", d_hidden, wq_in, preferred_element_type=jnp.float32)
    dx_share = lax.psum_scatter(dx_part, "tensor", scatter_dimension=2, tiled=True)
    dx_share = dx_share.reshape(n_expert * local_count, capacity, slice_width)
    returned = lax.all_to_all(dx_share, "expert", split_axis=0, concat_axis=0, tiled=True)
    returned = returned.reshape(expert_count * capacity, slice_width)
    dx_assign = jnp.dot(placer.astype(jnp.float32).T, returned, precision=lax.Precision.HIGHEST)
    grad_tokens = jnp.sum(dx_assign.reshape(tok_rows, top_count, slice_width), axis=1).astype(
        jnp.bfloat16
    )
    sum_in = jnp.einsum("slrd,slrf->ldf", full_x, d_hidden, preferred_element_type=jnp.float32)
    sum_out = jnp.einsum("slrf,slrd->lfd", scaled_act, full_dy, preferred_element_type=jnp.float32)
    grad_in = (sum_in * keep_mask(w_in, scale_in[:, None, :])).astype(jnp.bfloat16)
    grad_out = (sum_out * keep_mask(w_out, scale_out[:, None, :])).astype(jnp.bfloat16)
    return (grad_tokens, grad_in, grad_out)


def solution(mesh):
    placed = (
        P(("expert", "tensor"), "dp"),
        P(("expert", "tensor"), "dp"),
        P(("expert", "tensor"), None),
        P(("expert", "tensor"), None),
        P("expert", "dp", "tensor"),
        P("expert", "tensor"),
        P("expert", "tensor", "dp"),
        P("expert", "dp"),
    )
    return jax.shard_map(
        per_device,
        mesh=mesh,
        in_specs=placed,
        out_specs=(
            P(("expert", "tensor"), "dp"),
            P("expert", "dp", "tensor"),
            P("expert", "tensor", "dp"),
        ),
        check_vma=False,
    )
```

profile of v0, /device:TPU:2, one launch (start us, length us, event | category | flops | bytes accessed | tf_op | source)
XLA Modules:
  0.0 260.1 jit_solution(12312718387646152822)
XLA Ops:
  7.2 0.8 reshape.159
  7.9 0.1 fusion.28
  8.0 0.2 select_reduce_fusion
  8.2 0.7 broadcast_in_dim.4
  9.0 0.1 convolution_convert_fusion.1
  9.1 0.6 reshape.164
  9.7 16.4 %all-to-all-start.1 = ((bf16[8,3,768]{2,1,0:T(4,128)(2,1)}), bf16[8,3,768]{2,1,0:T(4,128)(2,1)S(1)}, u32[]{:S(2)}, u32[]{:S(2)}) async-start(bf16[8,3,768]{2,1,0:T(4,128)(2,1)} %reshape.164), calls=%async_computation.1 | async-start | bytes 98304 | tf_op jit(solution)/shard_map/all_to_all | solution.py:65
  26.2 0.7 multiply_reduce_fusion.1
  26.9 0.7 broadcast_in_dim.5
  27.6 0.1 convolution_convert_fusion
  27.7 0.7 multiply_reduce_fusion
  28.4 0.6 reshape.166
  29.1 4.1 %all-to-all-done.1 = bf16[8,3,768]{2,1,0:T(4,128)(2,1)S(1)} async-done(((bf16[8,3,768]{2,1,0:T(4,128)(2,1)}), bf16[8,3,768]{2,1,0:T(4,128)(2,1)S(1)}, u32[]{:S(2)}, u32[]{:S(2)}) %all-to-all-start.1) | async-done | bytes 36896 | tf_op jit(solution)/shard_map/all_to_all | solution.py:65
  33.2 4.7 %all-to-all-start.2 = ((bf16[8,3,768]{2,1,0:T(4,128)(2,1)}), bf16[8,3,768]{2,1,0:T(4,128)(2,1)S(1)}, u32[]{:S(2)}, u32[]{:S(2)}) async-start(bf16[8,3,768]{2,1,0:T(4,128)(2,1)} %reshape.166), calls=%async_computation.2 | async-start | bytes 98304 | tf_op jit(solution)/shard_map/all_to_all | solution.py:64
  37.9 0.0 all-reduce.3.cloned.1.call-start
  37.9 16.0 %all_gather.10 = bf16[8,48,768]{2,0,1:T(8,128)(2,1)S(1)} all-gather(bf16[8,3,768]{2,0,1:T(8,128)(2,1)S(1)} %copy.25), channel_id=1, replica_groups=mesh['expert'=8,'tensor'=16,'dp'=8] {'tensor'}, dimensions={1}, use_global_device_ids=true | all-gather | bytes 626688 | tf_op jit(solution)/shard_map/all_gather | solution.py:70
  53.9 0.0 all-to-all-done.2
  53.9 17.5 %all_gather.11 = bf16[8,48,768]{2,0,1:T(8,128)(2,1)S(1)} all-gather(bf16[8,3,768]{2,0,1:T(8,128)(2,1)S(1)} %copy.27), channel_id=1, replica_groups=mesh['expert'=8,'tensor'=16,'dp'=8] {'tensor'}, dimensions={1}, use_global_device_ids=true | all-gather | bytes 626688 | tf_op jit(solution)/shard_map/all_gather | solution.py:69
  71.4 0.0 copy-start.1
  71.4 2.5 convolution_bitcast_fusion.3
  73.9 0.0 copy-done.1
  73.9 1.7 convolution_bitcast_fusion.1
  75.6 0.0 copy-start.2
  75.6 0.0 all-reduce.3.cloned.1.call-update
  75.6 0.0 reduce-scatter.2.cloned.1.call-start
  75.7 0.6 copy-done.2
  76.3 0.1 reshape.172
  76.4 0.1 fusion.10
  76.5 0.1 all_to_all.23
  76.6 13.2 %all_to_all.28 = bf16[8,1,3]{2,1,0:T(2,128)(2,1)S(1)} all-to-all(bf16[8,1,3]{2,1,0:T(2,128)(2,1)S(1)} %all_to_all.23), channel_id=1, replica_groups=mesh['expert'=8,'tensor'=16,'dp'=8] {'expert'}, dimensions={0} | all-to-all | bytes 96 | tf_op jit(solution)/shard_map/all_to_all | solution.py:66
  89.8 0.1 copy.23
  89.9 14.4 %all-gather = bf16[8,1,48]{0,1,2:T(2,128)(2,1)S(1)} all-gather(bf16[8,1,3]{0,1,2:T(2,128)(2,1)S(1)} %copy.23), channel_id=2, replica_groups=mesh['expert'=8,'tensor'=16,'dp'=8] {'tensor'}, dimensions={2}, use_global_device_ids=true | all-gather | bytes 816 | tf_op jit(solution)/shard_map/all_gather | solution.py:71
  104.3 0.1 copy.24
  104.4 66.5 %all-reduce.3.cloned.1.call-done = (f32[8,1,48,384]{3,2,0,1:T(8,128)}, f32[8,1,48,768]{3,2,0,1:T(8,128)}) async-done(((f32[8,1,48,384]{3,2,0,1:T(8,128)}, f32[8,1,48,768]{3,2,0,1:T(8,128)}), (f32[8,1,48,384]{3,2,0,1:T(8,128)}, f32[8,1,48,768]{3,2,0,1:T(8,128)})) %all-reduce.3.cloned.1.call-update) | async-done | bytes 1769488 | tf_op jit(solution)/shard_map/psum | solution.py:81
  170.9 1.7 fusion.26
  172.6 0.7 convolution_bitcast_fusion
  173.3 1.7 copy.29
  175.1 0.0 reduce-scatter.2.cloned.1.call-update
  175.1 0.1 iota_compare_fusion.5
  175.2 0.0 copy-start
  175.2 1.9 fusion.3
  177.1 59.3 %reduce-scatter.2.cloned.1.call-done = f32[8,1,3,768]{3,0,1,2:T(8,128)} async-done(((f32[8,1,48,768]{3,0,1,2:T(8,128)}), f32[8,1,3,768]{3,0,1,2:T(8,128)}) %reduce-scatter.2.cloned.1.call-update) | async-done | bytes 73744 | tf_op jit(solution)/shard_map/reduce_scatter | solution.py:84
  236.4 1.6 copy.30
  238.0 7.2 %all-to-all-start.3 = ((f32[8,3,768]{2,1,0:T(4,128)}), f32[8,3,768]{2,1,0:T(4,128)S(1)}, u32[]{:S(2)}, u32[]{:S(2)}) async-start(f32[8,3,768]{2,1,0:T(4,128)} %copy.30), calls=%async_computation.4 | async-start | bytes 196608 | tf_op jit(solution)/shard_map/all_to_all | solution.py:86
  245.2 0.0 copy-done
  245.2 2.6 fusion.5
  247.7 4.7 %all-to-all-done.3 = f32[8,3,768]{2,1,0:T(4,128)S(1)} async-done(((f32[8,3,768]{2,1,0:T(4,128)}), f32[8,3,768]{2,1,0:T(4,128)S(1)}, u32[]{:S(2)}, u32[]{:S(2)}) %all-to-all-start.3) | async-done | bytes 73760 | tf_op jit(solution)/shard_map/all_to_all | solution.py:86
  252.5 0.8 convolution_reduce_fusion
  (11 shorter events, 0.2 us)
Async XLA Ops:
  9.7 23.5 %all-to-all-start.1 = ((bf16[8,3,768]{2,1,0:T(4,128)(2,1)}), bf16[8,3,768]{2,1,0:T(4,128)(2,1)S(1)}, u32[]{:S(2)}, u32[]{:S(2)}) async-start(bf16[8,3,768]{2,1,0:T(4,128)(2,1)} %reshape.164), calls=%async_computation.1 | async-start | bytes 98304 | tf_op jit(solution)/shard_map/all_to_all | solution.py:65
  33.2 20.7 %all-to-all-start.2 = ((bf16[8,3,768]{2,1,0:T(4,128)(2,1)}), bf16[8,3,768]{2,1,0:T(4,128)(2,1)S(1)}, u32[]{:S(2)}, u32[]{:S(2)}) async-start(bf16[8,3,768]{2,1,0:T(4,128)(2,1)} %reshape.166), calls=%async_computation.2 | async-start | bytes 98304 | tf_op jit(solution)/shard_map/all_to_all | solution.py:64
  37.9 133.0 %all-reduce.3.cloned.1.call-start = ((), (), s32[]{:S(2)}) async-start(), calls=%async_computation.6 | async-start | bytes 3538944 | tf_op jit(solution)/shard_map/psum | solution.py:81
  71.4 2.5 copy-start.1
  75.6 0.7 copy-start.2
  75.6 160.8 %reduce-scatter.2.cloned.1.call-start = ((), (), s32[]{:S(2)}) async-start(), calls=%async_computation.5 | async-start | bytes 1253376 | tf_op jit(solution)/shard_map/reduce_scatter | solution.py:84
  175.2 70.0 %copy-start = (f32[8,1,48,768]{3,2,0,1:T(8,128)S(1)}, f32[8,1,48,768]{3,2,0,1:T(8,128)}, u32[]{:S(2)}) copy-start(f32[8,1,48,768]{3,2,0,1:T(8,128)} %get-tuple-element.4) | copy-start | bytes 3538948
  238.0 14.5 %all-to-all-start.3 = ((f32[8,3,768]{2,1,0:T(4,128)}), f32[8,3,768]{2,1,0:T(4,128)S(1)}, u32[]{:S(2)}, u32[]{:S(2)}) async-start(f32[8,3,768]{2,1,0:T(4,128)} %copy.30), calls=%async_computation.4 | async-start | bytes 196608 | tf_op jit(solution)/shard_map/all_to_all | solution.py:86
Sparse Core Ops, SparseCore 0:
  75.7 95.1 all-reduce.2
  175.2 61.1 reduce-scatter.1
where the time goes:
time: 261 us; the launch traced here: 260 us
  waiting for transfers between devices  135 us (52%)
  blocking collectives  61.1 us (23%)
  starting transfers between devices  28.4 us (11%)
  between operations  14.1 us (5%)
  matrix products  10.4 us (4%)
  local copies, waits for them, and re-layouts  7.78 us (3%)
  other arithmetic  3.59 us (1%)
    psum x1, waiting for transfers between devices, per_device(): pre_full, back_full = lax.psum((pre_part, back_part), 'dp')  66.5 us
    reduce_scatter x1, waiting for transfers between devices, per_device(): lax.psum_scatter(dx_part, 'tensor', scatter_dimension=2, tiled=True)  59.3 us
    all_gather x1, blocking collectives, per_device(): lax.all_gather(recv_x, 'tensor', axis=1, tiled=True)  17.5 us
    all_to_all x1, starting transfers between devices, per_device(): lax.all_to_all(cotan_slots, 'expert', split_axis=0, concat_axis=0, tiled=...  16.4 us
    all_gather x1, blocking collectives, per_device(): lax.all_gather(recv_dy, 'tensor', axis=1, tiled=True)  16 us
    all_gather x1, blocking collectives, per_device(): lax.all_gather(recv_gate, 'tensor', axis=1, tiled=True)  14.4 us
    all_to_all x1, blocking collectives, per_device(): lax.all_to_all(gate_slots, 'expert', split_axis=0, concat_axis=0, tiled=T...  13.2 us
    all_to_all x1, starting transfers between devices, per_device(): lax.all_to_all(dx_share, 'expert', split_axis=0, concat_axis=0, tiled=True)  7.2 us
  transfers between devices with their start and end apart: 5, of which 4 were waited for; matrix products, arithmetic and copies ran while one was open for 3% of the time, Pallas kernels for 0%

commit v1 on v0

v1 whole, which is shorter than its diff:
```python
import jax
import jax.numpy as jnp
from jax import lax
from jax.sharding import Mesh, PartitionSpec as P

CAP = 3
CORES = 2
LANE = 128


def clip_only(weights, scales):
    bound = 448.0 * scales.astype(jnp.float32)
    return jnp.clip(weights.astype(jnp.float32), -bound, bound).astype(jnp.bfloat16)


def keep_mask(weights, scales):
    return jnp.abs(weights.astype(jnp.float32)) <= 448.0 * scales.astype(jnp.float32)


def swap(x):
    return lax.ppermute(x, "core", [(0, 1), (1, 0)])


def exchange(x, axes):
    return lax.all_to_all(x, axes, split_axis=0, concat_axis=0, tiled=True)


def dot(a, b, dims):
    return lax.dot_general(a, b, (dims, ((), ())), preferred_element_type=jnp.float32)


def per_device(tokens, grad_output, expert_ids, gate_weights, w_in, scale_in, w_out, scale_out):
    n_expert = lax.axis_size("expert")
    n_y = lax.axis_size("y")
    n_dp = lax.axis_size("dp")
    tok_rows, width = tokens.shape
    units = w_out.shape[1]
    hidden = 2 * units
    bf16 = jnp.bfloat16
    w_in, w_out = w_in[0], w_out[0]
    parties = n_expert * n_y
    rows = parties * CAP
    share = rows // n_dp

    wq_in = clip_only(w_in, scale_in)
    wq_out = clip_only(w_out, scale_out)
    other = swap(jnp.concatenate([wq_in, wq_out], axis=0))
    wo_in, wo_out = other[:width], other[width:]

    experts = jnp.arange(n_expert, dtype=jnp.int32)
    named = expert_ids[:, :, None] == experts[None, None, :]
    matched = jnp.any(named, axis=1)
    gate_of = jnp.sum(jnp.where(named, gate_weights.astype(jnp.float32)[:, :, None], 0.0), axis=1)
    rank = jnp.cumsum(matched.astype(jnp.int32), axis=0) - 1
    place = matched[:, :, None] & (rank[:, :, None] == jnp.arange(CAP, dtype=jnp.int32))
    place = place.astype(jnp.float32).reshape(tok_rows, n_expert * CAP)
    gates = jnp.sum(place.reshape(tok_rows, n_expert, CAP) * gate_of[:, :, None], axis=0)
    packed = jnp.concatenate([tokens, grad_output], axis=1)
    slots = dot(place.astype(bf16), packed, ((0,), (0,))).astype(bf16)
    slots = slots.reshape(n_expert, CAP, 2 * width)
    gate_cols = jnp.broadcast_to(gates.astype(bf16)[..., None], (n_expert, CAP, LANE))
    slots = jnp.concatenate([slots, gate_cols], axis=2)
    slots = jnp.broadcast_to(slots[:, None], (n_expert, n_y, CAP, 2 * width + LANE))
    got = exchange(slots.reshape(parties, CAP, 2 * width + LANE), ("expert", "y"))
    got = got.reshape(rows, 2 * width + LANE)
    x, dy = got[:, :width], got[:, width : 2 * width]
    gate_rows = got[:, 2 * width : 2 * width + 1]

    part = jnp.concatenate(
        [
            dot(x, wq_in, ((1,), (0,))).astype(bf16),
            dot(x, wo_in, ((1,), (0,))).astype(bf16),
            dot(dy, wq_out, ((1,), (1,))).astype(bf16),
            dot(dy, wo_out, ((1,), (1,))).astype(bf16),
        ],
        axis=1,
    )
    parts = exchange(part.reshape(n_dp, share, 3 * hidden), "dp")
    total = jnp.sum(parts.astype(jnp.float32), axis=0)

    z = lax.axis_index("dp")
    gate = lax.dynamic_slice_in_dim(gate_rows, z * share, share, 0).astype(jnp.float32)

    def activate(pre, back):
        gate_pre, up_pre = pre[:, :units], pre[:, units:]
        d_act = gate * back
        sigmoid_gate = jax.nn.sigmoid(gate_pre)
        silu_gate = gate_pre * sigmoid_gate
        slope = sigmoid_gate * (1.0 + gate_pre * (1.0 - sigmoid_gate))
        act = gate * silu_gate * up_pre
        return d_act * up_pre * slope, d_act * silu_gate, act

    own = activate(total[:, :hidden], total[:, 2 * hidden : 2 * hidden + units])
    oth = activate(total[:, hidden : 2 * hidden], total[:, 2 * hidden + units :])
    mine = jnp.concatenate([own[0], own[1], own[2], oth[0], oth[1], oth[2]], axis=1).astype(bf16)
    copies = jnp.broadcast_to(mine[None], (n_dp, share, 3 * hidden))
    full = exchange(copies, "dp").reshape(rows, 3 * hidden)
    half = hidden + units
    dh_own, act_own = full[:, :hidden], full[:, hidden:half]
    dh_oth = full[:, half : half + hidden]

    dx = dot(dh_own, wq_in, ((1,), (1,))) + dot(dh_oth, wo_in, ((1,), (1,)))
    back = exchange(dx.astype(bf16).reshape(parties, CAP, width), ("expert", "y"))
    spread = place.reshape(tok_rows, n_expert, 1, CAP)
    spread = jnp.broadcast_to(spread, (tok_rows, n_expert, n_y, CAP)).reshape(tok_rows, rows)
    grad_tokens = dot(spread.astype(bf16), back.reshape(rows, width), ((1,), (0,))).astype(bf16)

    got_r = swap(got)
    full_r = swap(full[:, half:])
    x_r, dy_r = got_r[:, :width], got_r[:, width : 2 * width]
    dh_r, act_r = full_r[:, :hidden], full_r[:, hidden:]
    sum_in = dot(x, dh_own, ((0,), (0,))) + dot(x_r, dh_r, ((0,), (0,)))
    sum_out = dot(act_own, dy, ((0,), (0,))) + dot(act_r, dy_r, ((0,), (0,)))
    grad_in = jnp.where(keep_mask(w_in, scale_in), sum_in, 0.0).astype(bf16)
    grad_out = jnp.where(keep_mask(w_out, scale_out), sum_out, 0.0).astype(bf16)
    return grad_tokens, grad_in[None], grad_out[None]


def solution(mesh):
    names = ("expert", "y", "core", "dp")
    n_expert, n_tensor, n_dp = (mesh.shape[a] for a in ("expert", "tensor", "dp"))
    fine = Mesh(mesh.devices.reshape(n_expert, n_tensor // CORES, CORES, n_dp), names)
    tensor = ("y", "core")
    block = ("expert", "y", "core")
    placed = (
        P(block, "dp"),
        P(block, "dp"),
        P(block, None),
        P(block, None),
        P("expert", "dp", tensor),
        P("expert", tensor),
        P("expert", tensor, "dp"),
        P("expert", "dp"),
    )
    return jax.shard_map(
        per_device,
        mesh=fine,
        in_specs=placed,
        out_specs=(P(block, "dp"), P("expert", "dp", tensor), P("expert", tensor, "dp")),
        check_vma=False,
    )
```

time: 261 us -> 150 us (0.57)
  the two profiles are of different devices: /device:TPU:2 before, /device:TPU:4 now
where the time goes in v1:
time: 150 us; the launch traced here: 149 us
  waiting for transfers between devices  66.9 us (45%)
  starting transfers between devices  56.2 us (37%)
  matrix products  13.6 us (9%)
  other arithmetic  6.07 us (4%)
  local copies, waits for them, and re-layouts  5.55 us (4%)
    all_to_all x4, waiting for transfers between devices, exchange(): return lax.all_to_all(x, axes, split_axis=0, concat_axis=0, tiled=True)  66.1 us
    all_to_all x4, starting transfers between devices, exchange(): return lax.all_to_all(x, axes, split_axis=0, concat_axis=0, tiled=True)  50.3 us
    dot_general x12, matrix products, dot(): lax.dot_general(a, b, (dims, ((), ())), preferred_element_type=jnp.float32)  13.6 us
    ppermute x3, starting transfers between devices, swap(): return lax.ppermute(x, 'core', [(0, 1), (1, 0)])  5.88 us
  transfers between devices with their start and end apart: 7, of which 5 were waited for; matrix products, arithmetic and copies ran while one was open for 9% of the time, Pallas kernels for 0%

profile of v1, /device:TPU:4, one launch (start us, length us, event | category | flops | bytes accessed | tf_op | source)
XLA Modules:
  0.0 149.3 jit_solution(7926865290891040654)
XLA Ops:
  0.7 0.9 fusion.43
  1.6 0.7 convert_element_type.108
  2.3 0.8 select_reduce_fusion.1
  3.1 0.1 and.20
  3.2 0.1 select_reduce_fusion
  3.4 0.1 eq.47
  3.5 0.1 eq.49
  3.5 0.9 convolution_convert_fusion
  4.7 1.1 broadcast_in_dim.60
  5.8 18.2 %all-to-all-start = ((bf16[64,3,1664]{2,1,0:T(4,128)(2,1)}), bf16[64,3,1664]{2,1,0:T(4,128)(2,1)}, u32[]{:S(2)}, u32[]{:S(2)}) async-start(bf16[64,3,1664]{2,1,0:T(4,128)(2,1)} %bitcast), calls=%async_computation | async-start | bytes 1703936 | tf_op jit(solution)/shard_map/all_to_all | solution.py:25
  24.1 0.3 fusion.1
  24.4 0.1 fusion.9
  24.5 1.3 pad_maximum_fusion
  25.9 1.9 %collective-permute-start = (bf16[1152,768]{1,0:T(8,128)(2,1)}, bf16[1152,768]{1,0:T(8,128)(2,1)}, u32[]{:S(2)}, u32[]{:S(2)}) collective-permute-start(bf16[1152,768]{1,0:T(8,128)(2,1)} %pad_maximum_fusion), channel_id=1, source_target_pairs={{0,8},{8,0},{1,9},{9,1},{2,10},{10,2},{3,11},{11,3},{4,12},{12,4},... | collective-permute-start | bytes 5308424 | tf_op jit(solution)/shard_map/ppermute | solution.py:21
  27.8 18.1 %all-to-all-done = bf16[64,3,1664]{2,1,0:T(4,128)(2,1)} async-done(((bf16[64,3,1664]{2,1,0:T(4,128)(2,1)}), bf16[64,3,1664]{2,1,0:T(4,128)(2,1)}, u32[]{:S(2)}, u32[]{:S(2)}) %all-to-all-start) | async-done | bytes 639008 | tf_op jit(solution)/shard_map/all_to_all | solution.py:25
  45.9 1.6 %reshape.104 = bf16[192,1664]{1,0:T(8,128)(2,1)S(1)} reshape(bf16[64,3,1664]{2,1,0:T(4,128)(2,1)} %all-to-all-done) | data formatting | bytes 1277952 | tf_op jit(solution)/shard_map/reshape | solution.py:65
  47.5 0.4 convolution_convert_fusion.4
  47.8 0.4 convolution_convert_fusion.2
  48.3 1.4 convolution_convert_fusion.3
  49.7 1.7 %convolution_convert_fusion.1 = bf16[192,768]{1,0:T(8,128)(2,1)S(1)} fusion(bf16[1152,768]{1,0:T(8,128)(2,1)} %collective-permute-done, bf16[192,1664]{1,0:T(8,128)(2,1)S(1)} %reshape.104), kind=kOutput, calls=%fused_computation.18 | convolution fusion | flops 226639872 | bytes 1769472 | tf_op jit(solution)/shard_map/dot_general | solution.py:29
  51.4 1.0 pad_maximum_fusion.1
  52.4 16.7 %all-to-all-start.1 = ((bf16[8,24,2304]{2,1,0:T(8,128)(2,1)}), bf16[8,24,2304]{2,1,0:T(8,128)(2,1)S(1)}, u32[]{:S(2)}, u32[]{:S(2)}) async-start(bf16[8,24,2304]{2,1,0:T(8,128)(2,1)} %bitcast.3), calls=%async_computation.1 | async-start | bytes 1769472 | tf_op jit(solution)/shard_map/all_to_all | solution.py:25
  69.0 0.1 convert_reduce_fusion.1
  69.2 22.2 %all-to-all-done.1 = bf16[8,24,2304]{2,1,0:T(8,128)(2,1)S(1)} async-done(((bf16[8,24,2304]{2,1,0:T(8,128)(2,1)}), bf16[8,24,2304]{2,1,0:T(8,128)(2,1)S(1)}, u32[]{:S(2)}, u32[]{:S(2)}) %all-to-all-start.1) | async-done | bytes 884768 | tf_op jit(solution)/shard_map/all_to_all | solution.py:25
  91.3 0.1 convert_reduce_fusion
  91.5 0.1 fusion.34
  91.6 0.1 fusion.35
  91.7 0.1 fusion.36
  91.8 0.1 fusion.37
  91.8 0.1 fusion.38
  91.9 1.0 broadcast_in_dim.61
  92.9 3.6 %all-to-all-start.2 = ((bf16[8,24,2304]{2,1,0:T(8,128)(2,1)}), bf16[8,24,2304]{2,1,0:T(8,128)(2,1)S(1)}, u32[]{:S(2)}, u32[]{:S(2)}) async-start(bf16[8,24,2304]{2,1,0:T(8,128)(2,1)} %broadcast_in_dim.61), calls=%async_computation.2 | async-start | bytes 1769472 | tf_op jit(solution)/shard_map/all_to_all | solution.py:25
  96.5 0.1 convert_element_type.104
  96.7 1.9 %collective-permute-start.1 = (bf16[192,1664]{1,0:T(8,128)(2,1)S(1)}, bf16[192,1664]{1,0:T(8,128)(2,1)}, u32[]{:S(2)}, u32[]{:S(2)}) collective-permute-start(bf16[192,1664]{1,0:T(8,128)(2,1)S(1)} %reshape.104), channel_id=1, source_target_pairs={{0,8},{8,0},{1,9},{9,1},{2,10},{10,2},{3,11},{11,3},{4,12},{12,4},... | collective-permute-start | bytes 1916936 | tf_op jit(solution)/shard_map/ppermute | solution.py:21
  98.6 19.8 %all-to-all-done.2 = bf16[8,24,2304]{2,1,0:T(8,128)(2,1)S(1)} async-done(((bf16[8,24,2304]{2,1,0:T(8,128)(2,1)}), bf16[8,24,2304]{2,1,0:T(8,128)(2,1)S(1)}, u32[]{:S(2)}, u32[]{:S(2)}) %all-to-all-start.2) | async-done | bytes 884768 | tf_op jit(solution)/shard_map/all_to_all | solution.py:25
  118.4 0.6 fusion.20
  119.0 1.8 %fusion.7 = bf16[192,768]{1,0:T(8,128)(2,1)S(1)} fusion(f32[192,768]{1,0:T(8,128)S(1)} %fusion.20, bf16[1152,768]{1,0:T(8,128)(2,1)} %collective-permute-done, bf16[192,2304]{1,0:T(8,128)(2,1)S(1)} %bitcast.23), kind=kOutput, calls=%fused_computation.17 | convolution fusion | flops 226787328 | bytes 2359296 | tf_op jit(solution)/shard_map/dot_general | solution.py:29
  120.8 0.9 reshape.107
  121.7 11.9 %all-to-all-start.3 = ((bf16[64,3,768]{2,1,0:T(4,128)(2,1)}), bf16[64,3,768]{2,1,0:T(4,128)(2,1)S(1)}, u32[]{:S(2)}, u32[]{:S(2)}) async-start(bf16[64,3,768]{2,1,0:T(4,128)(2,1)} %reshape.107), calls=%async_computation.3 | async-start | bytes 786432 | tf_op jit(solution)/shard_map/all_to_all | solution.py:25
  133.6 2.1 %collective-permute-start.2 = (bf16[192,1152]{1,0:T(8,128)(2,1)S(1)}, bf16[192,1152]{1,0:T(8,128)(2,1)S(1)}, u32[]{:S(2)}, u32[]{:S(2)}) collective-permute-start(bf16[192,1152]{1,0:T(8,128)(2,1)S(1)} %slice.96), channel_id=1, source_target_pairs={{0,8},{8,0},{1,9},{9,1},{2,10},{10,2},{3,11},{11,3},{4,12},{12,4},... | collective-permute-start | bytes 1327112 | tf_op jit(solution)/shard_map/ppermute | solution.py:21
  135.7 0.5 fusion.18
  136.2 0.4 fusion.22
  136.6 0.9 collective-permute-done.2
  137.4 2.2 %fusion.6 = bf16[1,384,768]{2,1,0:T(8,128)(2,1)} fusion(f32[384,768]{1,0:T(8,128)S(1)} %fusion.22, bf16[1,384,768]{2,1,0:T(8,128)(2,1)S(1)} %copy-done.3, f32[768]{0:T(1024)S(1)} %get-tuple-element.3, bf16[192,1664]{1,0:T(8,128)(2,1)} %collective-permute-done.1, bf16[192,1152]{1,0:T(8,128)(2,1)S(1)} %collective-permute-done.2), kind=kOutput, calls=%fused_computation.16 | convolution fusion | flops 115015680 | bytes 2805760 | tf_op jit(solution)/shard_map/dot_general | solution.py:29
  139.6 2.6 %fusion.4 = bf16[1,768,768]{2,1,0:T(8,128)(2,1)} fusion(f32[768,768]{1,0:T(8,128)S(1)} %fusion.18, bf16[1,768,768]{2,1,0:T(8,128)(2,1)S(1)} %copy-done.1, f32[768]{0:T(1024)S(1)} %get-tuple-element.5, bf16[192,1152]{1,0:T(8,128)(2,1)S(1)} %collective-permute-done.2, bf16[192,1664]{1,0:T(8,128)(2,1)} %collective-permute-done.1), kind=kOutput, calls=%fused_computation.13 | convolution fusion | flops 230031360 | bytes 5312512 | tf_op jit(solution)/shard_map/dot_general | solution.py:29
  142.3 6.0 %all-to-all-done.3 = bf16[64,3,768]{2,1,0:T(4,128)(2,1)S(1)} async-done(((bf16[64,3,768]{2,1,0:T(4,128)(2,1)}), bf16[64,3,768]{2,1,0:T(4,128)(2,1)S(1)}, u32[]{:S(2)}, u32[]{:S(2)}) %all-to-all-start.3) | async-done | bytes 294944 | tf_op jit(solution)/shard_map/all_to_all | solution.py:25
  148.3 0.2 reshape.108
  148.6 0.8 convolution_convert_fusion.5
  (30 shorter events, 0.7 us)
Async XLA Ops:
  0.6 23.4 %copy-start.4 = (bf16[1,768]{1,0:T(2,128)(2,1)S(1)}, bf16[1,768]{1,0:T(2,128)(2,1)}, u32[]{:S(2)}) copy-start(bf16[1,768]{1,0:T(2,128)(2,1)} %param.13) | copy-start | bytes 4612
  0.6 23.4 %copy-start.5 = (bf16[1,768]{1,0:T(2,128)(2,1)S(1)}, bf16[1,768]{1,0:T(2,128)(2,1)}, u32[]{:S(2)}) copy-start(bf16[1,768]{1,0:T(2,128)(2,1)} %param.15) | copy-start | bytes 4612
  0.7 23.5 %copy-start = (bf16[1,768,768]{2,1,0:T(8,128)(2,1)S(1)}, bf16[1,768,768]{2,1,0:T(8,128)(2,1)}, u32[]{:S(2)}) copy-start(bf16[1,768,768]{2,1,0:T(8,128)(2,1)} %param.12) | copy-start | bytes 3538948
  5.8 18.6 %copy-start.2 = (bf16[1,384,768]{2,1,0:T(8,128)(2,1)S(1)}, bf16[1,384,768]{2,1,0:T(8,128)(2,1)}, u32[]{:S(2)}) copy-start(bf16[1,384,768]{2,1,0:T(8,128)(2,1)} %param.14) | copy-start | bytes 1769476
  5.8 40.1 %all-to-all-start = ((bf16[64,3,1664]{2,1,0:T(4,128)(2,1)}), bf16[64,3,1664]{2,1,0:T(4,128)(2,1)}, u32[]{:S(2)}, u32[]{:S(2)}) async-start(bf16[64,3,1664]{2,1,0:T(4,128)(2,1)} %bitcast), calls=%async_computation | async-start | bytes 1703936 | tf_op jit(solution)/shard_map/all_to_all | solution.py:25
  25.9 22.4 %collective-permute-start = (bf16[1152,768]{1,0:T(8,128)(2,1)}, bf16[1152,768]{1,0:T(8,128)(2,1)}, u32[]{:S(2)}, u32[]{:S(2)}) collective-permute-start(bf16[1152,768]{1,0:T(8,128)(2,1)} %pad_maximum_fusion), channel_id=1, source_target_pairs={{0,8},{8,0},{1,9},{9,1},{2,10},{10,2},{3,11},{11,3},{4,12},{12,4},... | collective-permute-start | bytes 5308424 | tf_op jit(solution)/shard_map/ppermute | solution.py:21
  52.4 38.9 %all-to-all-start.1 = ((bf16[8,24,2304]{2,1,0:T(8,128)(2,1)}), bf16[8,24,2304]{2,1,0:T(8,128)(2,1)S(1)}, u32[]{:S(2)}, u32[]{:S(2)}) async-start(bf16[8,24,2304]{2,1,0:T(8,128)(2,1)} %bitcast.3), calls=%async_computation.1 | async-start | bytes 1769472 | tf_op jit(solution)/shard_map/all_to_all | solution.py:25
  92.9 25.5 %all-to-all-start.2 = ((bf16[8,24,2304]{2,1,0:T(8,128)(2,1)}), bf16[8,24,2304]{2,1,0:T(8,128)(2,1)S(1)}, u32[]{:S(2)}, u32[]{:S(2)}) async-start(bf16[8,24,2304]{2,1,0:T(8,128)(2,1)} %broadcast_in_dim.61), calls=%async_computation.2 | async-start | bytes 1769472 | tf_op jit(solution)/shard_map/all_to_all | solution.py:25
  96.7 39.9 %collective-permute-start.1 = (bf16[192,1664]{1,0:T(8,128)(2,1)S(1)}, bf16[192,1664]{1,0:T(8,128)(2,1)}, u32[]{:S(2)}, u32[]{:S(2)}) collective-permute-start(bf16[192,1664]{1,0:T(8,128)(2,1)S(1)} %reshape.104), channel_id=1, source_target_pairs={{0,8},{8,0},{1,9},{9,1},{2,10},{10,2},{3,11},{11,3},{4,12},{12,4},... | collective-permute-start | bytes 1916936 | tf_op jit(solution)/shard_map/ppermute | solution.py:21
  121.7 26.6 %all-to-all-start.3 = ((bf16[64,3,768]{2,1,0:T(4,128)(2,1)}), bf16[64,3,768]{2,1,0:T(4,128)(2,1)S(1)}, u32[]{:S(2)}, u32[]{:S(2)}) async-start(bf16[64,3,768]{2,1,0:T(4,128)(2,1)} %reshape.107), calls=%async_computation.3 | async-start | bytes 786432 | tf_op jit(solution)/shard_map/all_to_all | solution.py:25
  133.6 3.8 %copy-start.3 = (bf16[1,384,768]{2,1,0:T(8,128)(2,1)S(1)}, bf16[1,384,768]{2,1,0:T(8,128)(2,1)}, u32[]{:S(2)}) copy-start(bf16[1,384,768]{2,1,0:T(8,128)(2,1)} %param.14) | copy-start | bytes 1769476
  133.6 3.8 %collective-permute-start.2 = (bf16[192,1152]{1,0:T(8,128)(2,1)S(1)}, bf16[192,1152]{1,0:T(8,128)(2,1)S(1)}, u32[]{:S(2)}, u32[]{:S(2)}) collective-permute-start(bf16[192,1152]{1,0:T(8,128)(2,1)S(1)} %slice.96), channel_id=1, source_target_pairs={{0,8},{8,0},{1,9},{9,1},{2,10},{10,2},{3,11},{11,3},{4,12},{12,4},... | collective-permute-start | bytes 1327112 | tf_op jit(solution)/shard_map/ppermute | solution.py:21
  136.6 3.1 %copy-start.1 = (bf16[1,768,768]{2,1,0:T(8,128)(2,1)S(1)}, bf16[1,768,768]{2,1,0:T(8,128)(2,1)}, u32[]{:S(2)}) copy-start(bf16[1,768,768]{2,1,0:T(8,128)(2,1)} %param.12) | copy-start | bytes 3538948

commit v2 on v1

v2 whole, which is shorter than its diff:
```python
import functools
import jax
import jax.numpy as jnp
from jax import lax
from jax.experimental import pallas as pl
from jax.experimental.pallas import tpu as pltpu
from jax.sharding import Mesh, PartitionSpec as P

CAP = 3
CORES = 2
LANE = 128
VMEM_LIMIT = 24 * 1024 * 1024
F32 = jnp.float32
BF16 = jnp.bfloat16


def clip_only(weights, scales):
    bound = 448.0 * scales.astype(F32)
    return jnp.clip(weights.astype(F32), -bound, bound).astype(BF16)


def keep_mask(weights, scales):
    return jnp.abs(weights.astype(F32)) <= 448.0 * scales.astype(F32)


def swap(x):
    return lax.ppermute(x, "core", [(0, 1), (1, 0)])


def exchange(x, axes):
    return lax.all_to_all(x, axes, split_axis=0, concat_axis=0, tiled=True)


def dot(a, b, dims):
    return lax.dot_general(a, b, (dims, ((), ())), preferred_element_type=F32)


def up(n, m):
    return -(-n // m) * m


def routing(ids, n_expert):
    tok_rows, top = ids.shape
    at = lax.broadcasted_iota(jnp.int32, (n_expert, LANE), 0)
    seen = jnp.zeros((n_expert, LANE), jnp.int32)
    masks, named = [], []
    for i in range(tok_rows):
        hits = [jnp.broadcast_to(ids[i : i + 1, k : k + 1], at.shape) == at for k in range(top)]
        any_hit = functools.reduce(jnp.logical_or, hits)
        masks.append([any_hit & (seen == j) for j in range(CAP)])
        named.append(hits)
        seen = seen + any_hit.astype(jnp.int32)
    return masks, named


def slots_kernel(n_expert, n_y, size, ids_ref, gates_ref, tok_ref, cot_ref, out_ref, wide):
    tok_rows, width = tok_ref.shape
    tiles = width // LANE
    masks, named = routing(ids_ref[...], n_expert)
    gates = gates_ref[...].astype(F32)
    lane = lax.broadcasted_iota(jnp.int32, (n_expert, LANE), 1)
    wide[...] = jnp.zeros_like(wide)
    gate_row = jnp.zeros((n_expert, LANE), F32)
    for i in range(tok_rows):
        weight = jnp.zeros((n_expert, LANE), F32)
        for k, hit in enumerate(named[i]):
            weight = jnp.where(hit, jnp.broadcast_to(gates[i : i + 1, k : k + 1], hit.shape), weight)
        for j in range(CAP):
            gate_row = jnp.where(masks[i][j] & (lane == j), weight, gate_row)
    wide[pl.ds(2 * tiles * CAP, n_expert, stride=size), :] = gate_row
    both = [tok_ref[...].astype(F32), cot_ref[...].astype(F32)]
    for k in range(2 * tiles):
        at = (k % tiles) * LANE
        cols = both[k // tiles][:, at : at + LANE]
        for j in range(CAP):
            value = jnp.zeros((n_expert, LANE), F32)
            for i in range(tok_rows):
                value = jnp.where(masks[i][j], jnp.broadcast_to(cols[i : i + 1], value.shape), value)
            wide[pl.ds(j * 2 * tiles + k, n_expert, stride=size), :] = value
    for e in range(n_expert):
        message = wide[e * size : (e + 1) * size, :].astype(BF16)
        for y in range(n_y):
            out_ref[e * n_y + y] = message


def gather_kernel(parties, size, got_ref, own_ref, oth_ref, part_ref, rows_ref, gate_ref, got, wide, own, oth, sems):
    width = own.shape[1]
    hidden = width
    units = own.shape[0] - width
    tiles = width // LANE
    copies = [
        pltpu.make_async_copy(src, dst, sems.at[n])
        for n, (src, dst) in enumerate([(got_ref, got), (own_ref, own), (oth_ref, oth)])
    ]
    for c in copies:
        c.start()
    copies[0].wait()
    wide[...] = got[...].astype(F32)
    gates = wide[pl.ds(2 * tiles * CAP, parties, stride=size), :]
    for j in range(CAP):
        at = slice(j * parties, (j + 1) * parties)
        gate_ref[at, :] = jnp.broadcast_to(gates[:, j : j + 1], (parties, LANE))
        for k in range(2 * tiles):
            value = wide[pl.ds(j * 2 * tiles + k, parties, stride=size), :]
            rows_ref[at, k * LANE : (k + 1) * LANE] = value.astype(BF16)
    for n, weights in enumerate((own, oth)):
        copies[n + 1].wait()
        pre = dot(rows_ref[:, :width], weights[:width, :], ((1,), (0,)))
        part_ref[:, n * hidden : (n + 1) * hidden] = pre.astype(BF16)
        back = dot(rows_ref[:, width:], weights[width:, :], ((1,), (1,)))
        start = 2 * hidden + n * units
        part_ref[:, start : start + units] = back.astype(BF16)


def scatter_kernel(parties, size, offset, full_ref, own_ref, oth_ref, out_ref, dh, own, oth, wide, sems):
    width = own.shape[0]
    hidden = own.shape[1]
    tiles = width // LANE
    pairs = [
        (full_ref.at[:, 0:hidden], dh.at[0]),
        (own_ref.at[0:width, :], own),
        (full_ref.at[:, offset : offset + hidden], dh.at[1]),
        (oth_ref.at[0:width, :], oth),
    ]
    copies = [pltpu.make_async_copy(src, dst, sems.at[n]) for n, (src, dst) in enumerate(pairs)]
    for c in copies:
        c.start()
    wide[...] = jnp.zeros_like(wide)
    copies[0].wait()
    copies[1].wait()
    dx = dot(dh[0], own[...], ((1,), (1,)))
    copies[2].wait()
    copies[3].wait()
    dx = dx + dot(dh[1], oth[...], ((1,), (1,)))
    for j in range(CAP):
        for k in range(tiles):
            value = dx[j * parties : (j + 1) * parties, k * LANE : (k + 1) * LANE]
            wide[pl.ds(j * tiles + k, parties, stride=size), :] = value
    out_ref[...] = wide[...].astype(BF16)


def combine_kernel(n_expert, n_y, size, ids_ref, back_ref, out_ref, wide):
    tok_rows, width = out_ref.shape
    tiles = width // LANE
    parties = n_expert * n_y
    masks, _ = routing(ids_ref[...], n_expert)
    wide[...] = back_ref[...].astype(F32)
    for k in range(tiles):
        totals = [jnp.zeros((1, LANE), F32) for _ in range(tok_rows)]
        for j in range(CAP):
            value = wide[pl.ds(j * tiles + k, parties, stride=size), :]
            value = jnp.sum(value.reshape(n_expert, n_y, LANE), axis=1)
            for i in range(tok_rows):
                totals[i] = totals[i] + jnp.sum(jnp.where(masks[i][j], value, 0.0), axis=0, keepdims=True)
        out_ref[:, k * LANE : (k + 1) * LANE] = jnp.concatenate(totals, axis=0).astype(BF16)


def call(kernel, out_shape, in_specs, out_specs, scratch, flops, moved):
    return pl.pallas_call(
        kernel,
        out_shape=out_shape,
        in_specs=in_specs,
        out_specs=out_specs,
        scratch_shapes=scratch,
        compiler_params=pltpu.CompilerParams(vmem_limit_bytes=VMEM_LIMIT),
        cost_estimate=pl.CostEstimate(flops=flops, bytes_accessed=moved, transcendentals=0),
    )


VM = pl.BlockSpec(memory_space=pltpu.VMEM)
ANY = pl.BlockSpec(memory_space=pl.ANY)


def make_slots(ids, gates, tokens, cotangents, n_expert, n_y):
    width = tokens.shape[1]
    size = up(2 * CAP * width // LANE + 1, 8)
    shape = jax.ShapeDtypeStruct((n_expert * n_y, size, LANE), BF16)
    scratch = [pltpu.VMEM((n_expert * size, LANE), F32)]
    kernel = functools.partial(slots_kernel, n_expert, n_y, size)
    return call(kernel, shape, [VM] * 4, VM, scratch, 1 << 20, 1 << 20)(ids, gates, tokens, cotangents)


def gather(got, own, oth):
    parties, size, _ = got.shape
    width = own.shape[1]
    rows = parties * CAP
    shapes = (
        jax.ShapeDtypeStruct((rows, 2 * own.shape[0]), BF16),
        jax.ShapeDtypeStruct((rows, 2 * width), BF16),
        jax.ShapeDtypeStruct((rows, LANE), F32),
    )
    scratch = [
        pltpu.VMEM((parties * size, LANE), BF16),
        pltpu.VMEM((parties * size, LANE), F32),
        pltpu.VMEM(own.shape, BF16),
        pltpu.VMEM(own.shape, BF16),
        pltpu.SemaphoreType.DMA((3,)),
    ]
    kernel = functools.partial(gather_kernel, parties, size)
    moved = 4 * own.size + 6 * got.size
    return call(kernel, shapes, [ANY] * 3, (VM,) * 3, scratch, 4 * rows * own.size, moved)(
        got.reshape(parties * size, LANE), own, oth
    )


def scatter(full, own, oth, parties):
    rows = full.shape[0]
    width = own.shape[1]
    hidden = width
    size = up(CAP * width // LANE, 8)
    shape = jax.ShapeDtypeStruct((parties * size, LANE), BF16)
    scratch = [
        pltpu.VMEM((2, rows, hidden), BF16),
        pltpu.VMEM((width, hidden), BF16),
        pltpu.VMEM((width, hidden), BF16),
        pltpu.VMEM((parties * size, LANE), F32),
        pltpu.SemaphoreType.DMA((4,)),
    ]
    kernel = functools.partial(scatter_kernel, parties, size, own.shape[0])
    out = call(kernel, shape, [ANY] * 3, VM, scratch, 4 * rows * width * hidden, 4 * own.size)(full, own, oth)
    return out.reshape(parties, size, LANE)


def combine(ids, back, tok_rows, width, n_expert, n_y):
    parties, size, _ = back.shape
    shape = jax.ShapeDtypeStruct((tok_rows, width), BF16)
    scratch = [pltpu.VMEM((parties * size, LANE), F32)]
    kernel = functools.partial(combine_kernel, n_expert, n_y, size)
    return call(kernel, shape, [VM] * 2, VM, scratch, 1 << 20, 1 << 20)(ids, back.reshape(parties * size, LANE))


def per_device(tokens, grad_output, expert_ids, gate_weights, w_in, scale_in, w_out, scale_out):
    n_expert = lax.axis_size("expert")
    n_y = lax.axis_size("y")
    n_dp = lax.axis_size("dp")
    tok_rows, width = tokens.shape
    units = w_out.shape[1]
    hidden = 2 * units
    w_in, w_out = w_in[0], w_out[0]
    parties = n_expert * n_y
    rows = parties * CAP
    share = rows // n_dp

    messages = make_slots(expert_ids, gate_weights, tokens, grad_output, n_expert, n_y)
    got = exchange(messages, ("expert", "y"))

    own = jnp.concatenate([clip_only(w_in, scale_in), clip_only(w_out, scale_out)], axis=0)
    oth = swap(own)

    part, xdy, gate_rows = gather(got, own, oth)
    parts = exchange(part.reshape(n_dp, share, 3 * hidden), "dp")
    total = jnp.sum(parts.astype(F32), axis=0)

    z = lax.axis_index("dp")
    gate = lax.dynamic_slice_in_dim(gate_rows, z * share, share, 0)[:, :1]

    def activate(pre, back):
        gate_pre, up_pre = pre[:, :units], pre[:, units:]
        d_act = gate * back
        sigmoid_gate = jax.nn.sigmoid(gate_pre)
        silu_gate = gate_pre * sigmoid_gate
        slope = sigmoid_gate * (1.0 + gate_pre * (1.0 - sigmoid_gate))
        act = gate * silu_gate * up_pre
        return d_act * up_pre * slope, d_act * silu_gate, act

    first = activate(total[:, :hidden], total[:, 2 * hidden : 2 * hidden + units])
    second = activate(total[:, hidden : 2 * hidden], total[:, 2 * hidden + units :])
    mine = jnp.concatenate([*first, *second], axis=1).astype(BF16)
    copies = jnp.broadcast_to(mine[None], (n_dp, share, 3 * hidden))
    full = exchange(copies, "dp").reshape(rows, 3 * hidden)
    half = hidden + units

    back = exchange(scatter(full, own, oth, parties), ("expert", "y"))
    grad_tokens = combine(expert_ids, back, tok_rows, width, n_expert, n_y)

    xdy_r = swap(xdy)
    full_r = swap(full[:, half:])
    x, dy = xdy[:, :width], xdy[:, width:]
    x_r, dy_r = xdy_r[:, :width], xdy_r[:, width:]
    dh, act = full[:, :hidden], full[:, hidden:half]
    dh_r, act_r = full_r[:, :hidden], full_r[:, hidden:]
    sum_in = dot(x, dh, ((0,), (0,))) + dot(x_r, dh_r, ((0,), (0,)))
    sum_out = dot(act, dy, ((0,), (0,))) + dot(act_r, dy_r, ((0,), (0,)))
    grad_in = jnp.where(keep_mask(w_in, scale_in), sum_in, 0.0).astype(BF16)
    grad_out = jnp.where(keep_mask(w_out, scale_out), sum_out, 0.0).astype(BF16)
    return grad_tokens, grad_in[None], grad_out[None]


def solution(mesh):
    names = ("expert", "y", "core", "dp")
    n_expert, n_tensor, n_dp = (mesh.shape[a] for a in ("expert", "tensor", "dp"))
    fine = Mesh(mesh.devices.reshape(n_expert, n_tensor // CORES, CORES, n_dp), names)
    tensor = ("y", "core")
    block = ("expert", "y", "core")
    placed = (
        P(block, "dp"),
        P(block, "dp"),
        P(block, None),
        P(block, None),
        P("expert", "dp", tensor),
        P("expert", tensor),
        P("expert", tensor, "dp"),
        P("expert", "dp"),
    )
    return jax.shard_map(
        per_device,
        mesh=fine,
        in_specs=placed,
        out_specs=(P(block, "dp"), P("expert", "dp", tensor), P("expert", tensor, "dp")),
        check_vma=False,
    )
```

time: 150 us -> 150 us (level)
  blocking collectives: 0 us -> 39.6 us
  starting transfers between devices: 56.2 us -> 31.7 us
  waiting for transfers between devices: 66.9 us -> 56.3 us
  matrix products: 13.6 us -> 6.01 us
  Pallas kernels: 0 us -> 6.99 us
  local copies, waits for them, and re-layouts: 5.55 us -> 3.39 us
    all_to_all x0 -> x1, blocking collectives: none -> 39.6 us  [exchange(): return lax.all_to_all(x, axes, split_axis=0, concat_axis=0, tiled=True)]
    all_to_all x4 -> x3, starting transfers between devices: 50.3 us -> 25.9 us  [exchange(): return lax.all_to_all(x, axes, split_axis=0, concat_axis=0, tiled=True)]
    all_to_all x4 -> x3, waiting for transfers between devices: 66.1 us -> 56.3 us  [exchange(): return lax.all_to_all(x, axes, split_axis=0, concat_axis=0, tiled=True)]
    dot_general x12 -> x4, matrix products: 13.6 us -> 6.01 us  [dot(): return lax.dot_general(a, b, (dims, ((), ())), preferred_element_type=F32)]
    pallas_call x0 -> x4, Pallas kernels: none -> 6.99 us  [the longest x1 3.5 us: gather(): call(kernel, shapes, [ANY] * 3, (VM,) * 3, scratch, 4 * rows * own.size,...]
    reshape x4 -> x0, local copies, waits for them, and re-layouts: 2.75 us -> none  [the longest x1 1.57 us: per_device(): got = got.reshape(rows, 2 * width + LANE)]
    concatenate x4 -> x2, other arithmetic: 2.42 us -> 0.2 us  [the longest x1 0.12 us: per_device(): jnp.concatenate([clip_only(w_in, scale_in), clip_only(w_out, scale_out)],...]
  transfers between devices with their start and end apart: 7 -> 6, of which waited for: 5 -> 3; matrix products, arithmetic and copies ran while one was open for 9% -> 5% of each run, Pallas kernels for 0% -> 2%
where the time goes in v2:
time: 150 us
  waiting for transfers between devices  56.3 us (38%)
  blocking collectives  39.6 us (26%)
  starting transfers between devices  31.7 us (21%)
  Pallas kernels  6.99 us (5%)
  matrix products  6.01 us (4%)
  other arithmetic  4.9 us (3%)
  local copies, waits for them, and re-layouts  3.39 us (2%)
    all_to_all x3, waiting for transfers between devices, exchange(): return lax.all_to_all(x, axes, split_axis=0, concat_axis=0, tiled=True)  56.3 us
    all_to_all x1, blocking collectives, exchange(): return lax.all_to_all(x, axes, split_axis=0, concat_axis=0, tiled=True)  39.6 us
    all_to_all x3, starting transfers between devices, exchange(): return lax.all_to_all(x, axes, split_axis=0, concat_axis=0, tiled=True)  25.9 us
    dot_general x4, matrix products, dot(): return lax.dot_general(a, b, (dims, ((), ())), preferred_element_type=F32)  6.01 us
    ppermute x3, starting transfers between devices, swap(): return lax.ppermute(x, 'core', [(0, 1), (1, 0)])  5.75 us
    pallas_call x1, Pallas kernels, gather(): call(kernel, shapes, [ANY] * 3, (VM,) * 3, scratch, 4 * rows * own.size,...  3.5 us
  transfers between devices with their start and end apart: 6, of which 3 were waited for; matrix products, arithmetic and copies ran while one was open for 5% of the time, Pallas kernels for 2%

profile of v2, /device:TPU:4, one launch (start us, length us, event | category | flops | bytes accessed | tf_op | source)
XLA Modules:
  0.0 149.7 jit_solution(16633167568083120899)
XLA Ops:
  0.6 0.0 copy-start.6
  0.6 0.8 fusion.29
  1.4 0.7 fusion.28
  2.2 1.2 fusion.8
  3.4 0.0 copy-done.6
  3.4 0.3 fusion.1
  3.7 0.0 copy-start.2
  3.7 0.0 copy-start.3
  3.7 0.0 copy-start.4
  3.7 0.0 copy-start.5
  3.7 0.1 pad_maximum_fusion.own_ref
  3.8 1.9 %collective-permute-start = (bf16[1152,768]{1,0:T(8,128)(2,1)S(1)}, bf16[1152,768]{1,0:T(8,128)(2,1)S(1)}, u32[]{:S(2)}, u32[]{:S(2)}) collective-permute-start(bf16[1152,768]{1,0:T(8,128)(2,1)S(1)} %pad_maximum_fusion.own_ref), channel_id=1, source_target_pairs={{0,8},{8,0},{1,9},{9,1},{2,10},{10,2},{3,11},{11,3},{4,12},{12,4},... | collective-permute-start | bytes 5308424 | tf_op jit(solution)/shard_map/ppermute | solution.py:27
  5.8 0.0 copy-done.2
  5.8 0.0 copy-done.3
  5.8 0.0 copy-done.4
  5.8 0.2 shard_map.103
  6.0 39.6 %all_to_all.20 = bf16[64,40,128]{2,1,0:T(8,128)(2,1)S(1)} all-to-all(bf16[64,40,128]{2,1,0:T(8,128)(2,1)S(1)} %shard_map.103), channel_id=1, replica_groups=mesh['expert'=8,'y'=8,'core'=2,'dp'=8] {'expert','y'}, dimensions={0} | all-to-all | bytes 1310720 | tf_op jit(solution)/shard_map/all_to_all | solution.py:31
  45.6 0.0 collective-permute-done.oth_ref
  45.6 3.5 %shard_map.104 = (bf16[192,2304]{1,0:T(8,128)(2,1)}, bf16[192,1536]{1,0:T(8,128)(2,1)S(1)}, f32[192,128]{1,0:T(8,128)S(1)}) custom-call(bf16[2560,128]{1,0:T(8,128)(2,1)S(1)} %bitcast.21, bf16[1152,768]{1,0:T(8,128)(2,1)S(1)} %pad_maximum_fusion.own_ref, bf16[1152,768]{1,0:T(8,128)(2,1)S(1)} %collective-permute-done.oth_ref), custom_call_target="tpu_custom_call" | custom-call | flops 679477248 | bytes 5505024 | tf_op jit(solution)/shard_map/pallas_call | solution.py:201
  49.1 0.0 copy-done
  49.1 13.2 %all-to-all-start.1 = ((bf16[8,24,2304]{2,1,0:T(8,128)(2,1)}), bf16[8,24,2304]{2,1,0:T(8,128)(2,1)}, u32[]{:S(2)}, u32[]{:S(2)}) async-start(bf16[8,24,2304]{2,1,0:T(8,128)(2,1)} %bitcast.3), calls=%async_computation.1 | async-start | bytes 1769472 | tf_op jit(solution)/shard_map/all_to_all | solution.py:31
  62.4 0.1 dynamic-slice_reduce_fusion
  62.5 23.5 %all-to-all-done.1 = bf16[8,24,2304]{2,1,0:T(8,128)(2,1)} async-done(((bf16[8,24,2304]{2,1,0:T(8,128)(2,1)}), bf16[8,24,2304]{2,1,0:T(8,128)(2,1)}, u32[]{:S(2)}, u32[]{:S(2)}) %all-to-all-start.1) | async-done | bytes 884768 | tf_op jit(solution)/shard_map/all_to_all | solution.py:31
  86.0 1.3 convert_reduce_fusion
  87.3 0.1 fusion.22
  87.4 0.1 fusion.23
  87.5 0.1 fusion.24
  87.5 0.1 fusion.25
  87.6 0.1 fusion.26
  87.7 0.1 fusion.27
  87.8 1.0 broadcast_in_dim.20
  88.8 3.6 %all-to-all-start.2 = ((bf16[8,24,2304]{2,1,0:T(8,128)(2,1)}), bf16[8,24,2304]{2,1,0:T(8,128)(2,1)S(1)}, u32[]{:S(2)}, u32[]{:S(2)}) async-start(bf16[8,24,2304]{2,1,0:T(8,128)(2,1)} %broadcast_in_dim.20), calls=%async_computation.2 | async-start | bytes 1769472 | tf_op jit(solution)/shard_map/all_to_all | solution.py:31
  92.3 1.9 %collective-permute-start.1 = (bf16[192,1536]{1,0:T(8,128)(2,1)S(1)}, bf16[192,1536]{1,0:T(8,128)(2,1)}, u32[]{:S(2)}, u32[]{:S(2)}) collective-permute-start(bf16[192,1536]{1,0:T(8,128)(2,1)S(1)} %get-tuple-element.8), channel_id=1, source_target_pairs={{0,8},{8,0},{1,9},{9,1},{2,10},{10,2},{3,11},{11,3},{4,12},{12,4},... | collective-permute-start | bytes 1769480 | tf_op jit(solution)/shard_map/ppermute | solution.py:27
  94.2 21.5 %all-to-all-done.2 = bf16[8,24,2304]{2,1,0:T(8,128)(2,1)S(1)} async-done(((bf16[8,24,2304]{2,1,0:T(8,128)(2,1)}), bf16[8,24,2304]{2,1,0:T(8,128)(2,1)S(1)}, u32[]{:S(2)}, u32[]{:S(2)}) %all-to-all-start.2) | async-done | bytes 884768 | tf_op jit(solution)/shard_map/all_to_all | solution.py:31
  115.7 0.8 slice.78
  116.5 1.9 %collective-permute-start.2 = (bf16[192,1152]{1,0:T(8,128)(2,1)}, bf16[192,1152]{1,0:T(8,128)(2,1)}, u32[]{:S(2)}, u32[]{:S(2)}) collective-permute-start(bf16[192,1152]{1,0:T(8,128)(2,1)} %slice.78), channel_id=1, source_target_pairs={{0,8},{8,0},{1,9},{9,1},{2,10},{10,2},{3,11},{11,3},{4,12},{12,4},... | collective-permute-start | bytes 1327112 | tf_op jit(solution)/shard_map/ppermute | solution.py:27
  118.5 1.5 copy-done.1
  119.9 2.4 %shard_map.105 = bf16[1536,128]{1,0:T(8,128)(2,1)} custom-call(bf16[192,2304]{1,0:T(8,128)(2,1)S(1)} %bitcast.18, bf16[1152,768]{1,0:T(8,128)(2,1)S(1)} %pad_maximum_fusion.own_ref, bf16[1152,768]{1,0:T(8,128)(2,1)S(1)} %copy-done.1), custom_call_target="tpu_custom_call" | custom-call | flops 452984832 | bytes 3538944 | tf_op jit(solution)/shard_map/pallas_call | solution.py:220
  122.3 9.1 %all-to-all-start.3 = ((bf16[64,24,128]{2,1,0:T(8,128)(2,1)}), bf16[64,24,128]{2,1,0:T(8,128)(2,1)S(1)}, u32[]{:S(2)}, u32[]{:S(2)}) async-start(bf16[64,24,128]{2,1,0:T(8,128)(2,1)} %bitcast.5), calls=%async_computation.3 | async-start | bytes 786432 | tf_op jit(solution)/shard_map/all_to_all | solution.py:31
  131.5 0.0 copy-start.8
  131.5 0.0 collective-permute-done.1
  131.5 0.0 collective-permute-done.2
  131.5 1.5 fusion.10
  133.0 1.2 fusion.6
  134.2 1.7 %fusion.12 = f32[768,768]{1,0:T(8,128)S(1)} fusion(bf16[192,1152]{1,0:T(8,128)(2,1)} %collective-permute-done.2, bf16[192,1536]{1,0:T(8,128)(2,1)} %collective-permute-done.1), kind=kOutput, calls=%fused_computation.20 | convolution fusion | flops 226492416 | bytes 2949120 | tf_op jit(solution)/shard_map/dot_general | solution.py:35
  135.9 1.7 %fusion.4 = bf16[1,768,768]{2,1,0:T(8,128)(2,1)} fusion(f32[768,768]{1,0:T(8,128)S(1)} %fusion.12, bf16[1,768,768]{2,1,0:T(8,128)(2,1)S(1)} %copy-done.7, f32[768]{0:T(1024)S(1)} %get-tuple-element.9, bf16[192,2304]{1,0:T(8,128)(2,1)S(1)} %bitcast.20, bf16[192,1536]{1,0:T(8,128)(2,1)S(1)} %get-tuple-element.8), kind=kOutput, calls=%fused_computation.12 | convolution fusion | flops 230031360 | bytes 5312512 | tf_op jit(solution)/shard_map/dot_general | solution.py:35
  137.6 11.3 %all-to-all-done.3 = bf16[64,24,128]{2,1,0:T(8,128)(2,1)S(1)} async-done(((bf16[64,24,128]{2,1,0:T(8,128)(2,1)}), bf16[64,24,128]{2,1,0:T(8,128)(2,1)S(1)}, u32[]{:S(2)}, u32[]{:S(2)}) %all-to-all-start.3) | async-done | bytes 393248 | tf_op jit(solution)/shard_map/all_to_all | solution.py:31
  148.8 0.9 shard_map.106
  (6 shorter events, 0.0 us)
Async XLA Ops:
  0.6 2.7 %copy-start.6 = (bf16[1,768,768]{2,1,0:T(8,128)(2,1)S(1)}, bf16[1,768,768]{2,1,0:T(8,128)(2,1)}, u32[]{:S(2)}) copy-start(bf16[1,768,768]{2,1,0:T(8,128)(2,1)} %param.12) | copy-start | bytes 3538948
  3.7 2.1 %copy-start.2 = (s32[4,4]{1,0:T(4,128)S(1)}, s32[4,4]{1,0:T(4,128)}, u32[]{:S(2)}) copy-start(s32[4,4]{1,0:T(4,128)} %ids_ref.3) | copy-start | bytes 196
  3.7 2.1 %copy-start.3 = (bf16[4,768]{1,0:T(4,128)(2,1)S(1)}, bf16[4,768]{1,0:T(4,128)(2,1)}, u32[]{:S(2)}) copy-start(bf16[4,768]{1,0:T(4,128)(2,1)} %tok_ref.1) | copy-start | bytes 18436
  3.7 2.1 %copy-start.4 = (bf16[4,768]{1,0:T(4,128)(2,1)S(1)}, bf16[4,768]{1,0:T(4,128)(2,1)}, u32[]{:S(2)}) copy-start(bf16[4,768]{1,0:T(4,128)(2,1)} %cot_ref.1) | copy-start | bytes 18436
  3.7 2.1 %copy-start.5 = (bf16[4,4]{1,0:T(4,128)(2,1)S(1)}, bf16[4,4]{1,0:T(4,128)(2,1)}, u32[]{:S(2)}) copy-start(bf16[4,4]{1,0:T(4,128)(2,1)} %gates_ref.1) | copy-start | bytes 100
  3.8 41.8 %collective-permute-start = (bf16[1152,768]{1,0:T(8,128)(2,1)S(1)}, bf16[1152,768]{1,0:T(8,128)(2,1)S(1)}, u32[]{:S(2)}, u32[]{:S(2)}) collective-permute-start(bf16[1152,768]{1,0:T(8,128)(2,1)S(1)} %pad_maximum_fusion.own_ref), channel_id=1, source_target_pairs={{0,8},{8,0},{1,9},{9,1},{2,10},{10,2},{3,11},{11,3},{4,12},{12,4},... | collective-permute-start | bytes 5308424 | tf_op jit(solution)/shard_map/ppermute | solution.py:27
  45.6 3.5 %copy-start = (bf16[1152,768]{1,0:T(8,128)(2,1)}, bf16[1152,768]{1,0:T(8,128)(2,1)S(1)}, u32[]{:S(2)}) copy-start(bf16[1152,768]{1,0:T(8,128)(2,1)S(1)} %collective-permute-done.oth_ref) | copy-start | bytes 5308420
  49.1 36.9 %all-to-all-start.1 = ((bf16[8,24,2304]{2,1,0:T(8,128)(2,1)}), bf16[8,24,2304]{2,1,0:T(8,128)(2,1)}, u32[]{:S(2)}, u32[]{:S(2)}) async-start(bf16[8,24,2304]{2,1,0:T(8,128)(2,1)} %bitcast.3), calls=%async_computation.1 | async-start | bytes 1769472 | tf_op jit(solution)/shard_map/all_to_all | solution.py:31
  88.8 27.0 %all-to-all-start.2 = ((bf16[8,24,2304]{2,1,0:T(8,128)(2,1)}), bf16[8,24,2304]{2,1,0:T(8,128)(2,1)S(1)}, u32[]{:S(2)}, u32[]{:S(2)}) async-start(bf16[8,24,2304]{2,1,0:T(8,128)(2,1)} %broadcast_in_dim.20), calls=%async_computation.2 | async-start | bytes 1769472 | tf_op jit(solution)/shard_map/all_to_all | solution.py:31
  92.3 39.2 %collective-permute-start.1 = (bf16[192,1536]{1,0:T(8,128)(2,1)S(1)}, bf16[192,1536]{1,0:T(8,128)(2,1)}, u32[]{:S(2)}, u32[]{:S(2)}) collective-permute-start(bf16[192,1536]{1,0:T(8,128)(2,1)S(1)} %get-tuple-element.8), channel_id=1, source_target_pairs={{0,8},{8,0},{1,9},{9,1},{2,10},{10,2},{3,11},{11,3},{4,12},{12,4},... | collective-permute-start | bytes 1769480 | tf_op jit(solution)/shard_map/ppermute | solution.py:27
  116.5 15.0 %collective-permute-start.2 = (bf16[192,1152]{1,0:T(8,128)(2,1)}, bf16[192,1152]{1,0:T(8,128)(2,1)}, u32[]{:S(2)}, u32[]{:S(2)}) collective-permute-start(bf16[192,1152]{1,0:T(8,128)(2,1)} %slice.78), channel_id=1, source_target_pairs={{0,8},{8,0},{1,9},{9,1},{2,10},{10,2},{3,11},{11,3},{4,12},{12,4},... | collective-permute-start | bytes 1327112 | tf_op jit(solution)/shard_map/ppermute | solution.py:27
  118.4 1.5 copy-start.1
  122.3 26.5 %all-to-all-start.3 = ((bf16[64,24,128]{2,1,0:T(8,128)(2,1)}), bf16[64,24,128]{2,1,0:T(8,128)(2,1)S(1)}, u32[]{:S(2)}, u32[]{:S(2)}) async-start(bf16[64,24,128]{2,1,0:T(8,128)(2,1)} %bitcast.5), calls=%async_computation.3 | async-start | bytes 786432 | tf_op jit(solution)/shard_map/all_to_all | solution.py:31
  131.5 1.5 copy-start.8
  134.2 1.7 %copy-start.7 = (bf16[1,768,768]{2,1,0:T(8,128)(2,1)S(1)}, bf16[1,768,768]{2,1,0:T(8,128)(2,1)}, u32[]{:S(2)}) copy-start(bf16[1,768,768]{2,1,0:T(8,128)(2,1)} %param.12) | copy-start | bytes 3538948

commit v3 on v2

--- a/solution.py
+++ b/solution.py
@@ -12,15 +12,6 @@
 VMEM_LIMIT = 24 * 1024 * 1024
 F32 = jnp.float32
 BF16 = jnp.bfloat16
-
-
-def clip_only(weights, scales):
-    bound = 448.0 * scales.astype(F32)
-    return jnp.clip(weights.astype(F32), -bound, bound).astype(BF16)
-
-
-def keep_mask(weights, scales):
-    return jnp.abs(weights.astype(F32)) <= 448.0 * scales.astype(F32)
 
 
 def swap(x):
@@ -83,15 +74,20 @@
             out_ref[e * n_y + y] = message
 
 
-def gather_kernel(parties, size, got_ref, own_ref, oth_ref, part_ref, rows_ref, gate_ref, got, wide, own, oth, sems):
+def gather_kernel(
+    parties, size, got_ref, own_ref, oth_in_ref, oth_out_ref, part_ref, rows_ref, gate_ref, got, wide, own, oth, rows, part, sems
+):
     width = own.shape[1]
     hidden = width
     units = own.shape[0] - width
     tiles = width // LANE
-    copies = [
-        pltpu.make_async_copy(src, dst, sems.at[n])
-        for n, (src, dst) in enumerate([(got_ref, got), (own_ref, own), (oth_ref, oth)])
+    pairs = [
+        (got_ref, got),
+        (own_ref, own),
+        (oth_in_ref, oth.at[0:width, :]),
+        (oth_out_ref, oth.at[width : width + units, :]),
     ]
+    copies = [pltpu.make_async_copy(src, dst, sems.at[n]) for n, (src, dst) in enumerate(pairs)]
     for c in copies:
         c.start()
     copies[0].wait()
@@ -102,17 +98,68 @@
         gate_ref[at, :] = jnp.broadcast_to(gates[:, j : j + 1], (parties, LANE))
         for k in range(2 * tiles):
             value = wide[pl.ds(j * 2 * tiles + k, parties, stride=size), :]
-            rows_ref[at, k * LANE : (k + 1) * LANE] = value.astype(BF16)
+            rows[at, k * LANE : (k + 1) * LANE] = value.astype(BF16)
+    outs = [pltpu.make_async_copy(rows, rows_ref, sems.at[4])]
+    outs[0].start()
     for n, weights in enumerate((own, oth)):
-        copies[n + 1].wait()
-        pre = dot(rows_ref[:, :width], weights[:width, :], ((1,), (0,)))
-        part_ref[:, n * hidden : (n + 1) * hidden] = pre.astype(BF16)
-        back = dot(rows_ref[:, width:], weights[width:, :], ((1,), (1,)))
-        start = 2 * hidden + n * units
-        part_ref[:, start : start + units] = back.astype(BF16)
-
-
-def scatter_kernel(parties, size, offset, full_ref, own_ref, oth_ref, out_ref, dh, own, oth, wide, sems):
+        for c in copies[n + 1 : 2 + 2 * n]:
+            c.wait()
+        pre = dot(rows[:, :width], weights[:width, :], ((1,), (0,)))
+        back = dot(rows[:, width:], weights[width:, :], ((1,), (1,)))
+        for q, (value, at) in enumerate(((pre, n * hidden), (back, CORES * hidden + n * units))):
+            cols = slice(at, at + value.shape[1])
+            part[:, cols] = value.astype(BF16)
+            c = pltpu.make_async_copy(part.at[:, cols], part_ref.at[:, cols], sems.at[5 + 2 * n + q])
+            c.start()
+            outs.append(c)
+    for c in outs:
+        c.wait()
+
+
+def clip_kernel(step, after_ref, w_in_ref, scale_in_ref, w_out_ref, scale_out_ref, out_ref, *piece_refs):
+    del after_ref
+    start = 0
+    for weights, scales, piece in zip((w_in_ref, w_out_ref), (scale_in_ref, scale_out_ref), piece_refs):
+        bound = 448.0 * scales[...].astype(F32)
+        for r in range(0, weights.shape[0], step):
+            block = weights[r : r + step, :].astype(F32)
+            block = jnp.clip(block, -bound, bound).astype(BF16)
+            out_ref[start + r : start + r + step, :] = block
+            piece[r : r + step, :] = block
+        start += weights.shape[0]
+
+
+def activate_kernel(share, units, z_ref, parts_ref, gate_ref, out_ref):
+    n_dp = parts_ref.shape[0]
+    hidden = 2 * units
+    gates = gate_ref[pl.ds(pl.multiple_of(z_ref[0] * share, 8), share), :]
+
+    def total(at):
+        value = parts_ref[0, :, at : at + LANE].astype(F32)
+        for p in range(1, n_dp):
+            value = value + parts_ref[p, :, at : at + LANE].astype(F32)
+        return value
+
+    for n in range(CORES):
+        for c in range(0, units, LANE):
+            gate_pre = total(n * hidden + c)
+            up_pre = total(n * hidden + units + c)
+            d_act = gates * total(CORES * hidden + n * units + c)
+            sigmoid_gate = jax.nn.sigmoid(gate_pre)
+            silu_gate = gate_pre * sigmoid_gate
+            slope = sigmoid_gate * (1.0 + gate_pre * (1.0 - sigmoid_gate))
+            values = (d_act * up_pre * slope, d_act * silu_gate, gates * silu_gate * up_pre)
+            for q, value in enumerate(values):
+                at = n * (hidden + units) + q * units + c
+                value = value.astype(BF16)
+                for p in range(n_dp):
+                    out_ref[p, :, at : at + LANE] = value
+
+
+def scatter_kernel(
+    parties, size, offset, after_ref, full_ref, own_ref, oth_ref, out_ref, dh_ref, act_ref, dh, own, oth, wide, out, sems
+):
+    del after_ref
     width = own.shape[0]
     hidden = own.shape[1]
     tiles = width // LANE
@@ -120,7 +167,9 @@
         (full_ref.at[:, 0:hidden], dh.at[0]),
         (own_ref.at[0:width, :], own),
         (full_ref.at[:, offset : offset + hidden], dh.at[1]),
-        (oth_ref.at[0:width, :], oth),
+        (oth_ref, oth),
+        (full_ref.at[:, offset : offset + hidden], dh_ref),
+        (full_ref.at[:, offset + hidden : 2 * offset], act_ref),
     ]
     copies = [pltpu.make_async_copy(src, dst, sems.at[n]) for n, (src, dst) in enumerate(pairs)]
     for c in copies:
@@ -136,7 +185,30 @@
         for k in range(tiles):
             value = dx[j * parties : (j + 1) * parties, k * LANE : (k + 1) * LANE]
             wide[pl.ds(j * tiles + k, parties, stride=size), :] = value
-    out_ref[...] = wide[...].astype(BF16)
+    out[...] = wide[...].astype(BF16)
+    copies.append(pltpu.make_async_copy(out, out_ref, sems.at[6]))
+    copies[6].start()
+    for c in copies[4:]:
+        c.wait()
+
+
+def grads_kernel(
+    step, mine_ref, theirs_ref, full_ref, dh_ref, act_ref, w_in_ref, scale_in_ref, w_out_ref, scale_out_ref, in_ref, out_ref
+):
+    width, hidden = w_in_ref.shape
+    for weights, scales, grad in ((w_in_ref, scale_in_ref, in_ref), (w_out_ref, scale_out_ref, out_ref)):
+        bound = 448.0 * scales[...].astype(F32)
+        for r in range(0, weights.shape[0], step):
+            at = slice(r, r + step)
+            if grad is in_ref:
+                total = dot(mine_ref[:, at], full_ref[:, :hidden], ((0,), (0,)))
+                total = total + dot(theirs_ref[:, at], dh_ref[...], ((0,), (0,)))
+            else:
+                own_act = full_ref[:, hidden + r : hidden + r + step]
+                total = dot(own_act, mine_ref[:, width:], ((0,), (0,)))
+                total = total + dot(act_ref[:, at], theirs_ref[:, width:], ((0,), (0,)))
+            keep = jnp.abs(weights[at, :].astype(F32)) <= bound
+            grad[at, :] = jnp.where(keep, total, 0.0).astype(BF16)
 
 
 def combine_kernel(n_expert, n_y, size, ids_ref, back_ref, out_ref, wide):
@@ -169,6 +241,7 @@
 
 VM = pl.BlockSpec(memory_space=pltpu.VMEM)
 ANY = pl.BlockSpec(memory_space=pl.ANY)
+HBM = pl.BlockSpec(memory_space=pltpu.HBM)
 
 
 def make_slots(ids, gates, tokens, cotangents, n_expert, n_y):
@@ -180,7 +253,24 @@
     return call(kernel, shape, [VM] * 4, VM, scratch, 1 << 20, 1 << 20)(ids, gates, tokens, cotangents)
 
 
-def gather(got, own, oth):
+def clip_weights(after, w_in, scale_in, w_out, scale_out):
+    width = w_in.shape[1]
+    heights = (w_in.shape[0] + w_out.shape[0], w_in.shape[0], w_out.shape[0])
+    shapes = tuple(jax.ShapeDtypeStruct((h, width), BF16) for h in heights)
+    size = w_in.size + w_out.size
+    kernel = functools.partial(clip_kernel, 64)
+    return call(kernel, shapes, [ANY] + [VM] * 4, (VM,) * 3, [], 4 * size, 4 * size)(after, w_in, scale_in, w_out, scale_out)
+
+
+def activate(z, parts, gate_rows, units):
+    share = parts.shape[1]
+    shape = jax.ShapeDtypeStruct(parts.shape, BF16)
+    kernel = functools.partial(activate_kernel, share, units)
+    specs = [pl.BlockSpec(memory_space=pltpu.SMEM), VM, VM]
+    return call(kernel, shape, specs, VM, [], 2 * parts.size, 4 * parts.size)(z, parts, gate_rows)
+
+
+def gather(got, own, oth_in, oth_out):
     parties, size, _ = got.shape
     width = own.shape[1]
     rows = parties * CAP
@@ -194,31 +284,46 @@
         pltpu.VMEM((parties * size, LANE), F32),
         pltpu.VMEM(own.shape, BF16),
         pltpu.VMEM(own.shape, BF16),
-        pltpu.SemaphoreType.DMA((3,)),
+        pltpu.VMEM((rows, 2 * width), BF16),
+        pltpu.VMEM((rows, 2 * own.shape[0]), BF16),
+        pltpu.SemaphoreType.DMA((5 + 2 * CORES,)),
     ]
     kernel = functools.partial(gather_kernel, parties, size)
     moved = 4 * own.size + 6 * got.size
-    return call(kernel, shapes, [ANY] * 3, (VM,) * 3, scratch, 4 * rows * own.size, moved)(
-        got.reshape(parties * size, LANE), own, oth
-    )
-
-
-def scatter(full, own, oth, parties):
+    return call(kernel, shapes, [ANY, HBM, HBM, HBM], (HBM, HBM, VM), scratch, 4 * rows * own.size, moved)(
+        got.reshape(parties * size, LANE), own, oth_in, oth_out
+    )
+
+
+def scatter(after, full, own, oth, parties):
     rows = full.shape[0]
     width = own.shape[1]
     hidden = width
     size = up(CAP * width // LANE, 8)
-    shape = jax.ShapeDtypeStruct((parties * size, LANE), BF16)
+    shapes = (
+        jax.ShapeDtypeStruct((parties * size, LANE), BF16),
+        jax.ShapeDtypeStruct((rows, hidden), BF16),
+        jax.ShapeDtypeStruct((rows, own.shape[0] - width), BF16),
+    )
     scratch = [
         pltpu.VMEM((2, rows, hidden), BF16),
         pltpu.VMEM((width, hidden), BF16),
         pltpu.VMEM((width, hidden), BF16),
         pltpu.VMEM((parties * size, LANE), F32),
-        pltpu.SemaphoreType.DMA((4,)),
+        pltpu.VMEM((parties * size, LANE), BF16),
+        pltpu.SemaphoreType.DMA((7,)),
     ]
     kernel = functools.partial(scatter_kernel, parties, size, own.shape[0])
-    out = call(kernel, shape, [ANY] * 3, VM, scratch, 4 * rows * width * hidden, 4 * own.size)(full, own, oth)
-    return out.reshape(parties, size, LANE)
+    flops, moved = 4 * rows * width * hidden, 4 * own.size
+    out, dh, act = call(kernel, shapes, [HBM, HBM, ANY, ANY], (HBM,) * 3, scratch, flops, moved)(after, full, own, oth)
+    return out.reshape(parties, size, LANE), dh, act
+
+
+def weight_grads(mine, theirs, full, dh, act, w_in, scale_in, w_out, scale_out):
+    shapes = (jax.ShapeDtypeStruct(w_in.shape, BF16), jax.ShapeDtypeStruct(w_out.shape, BF16))
+    kernel = functools.partial(grads_kernel, 128)
+    args = (mine, theirs, full, dh, act, w_in, scale_in, w_out, scale_out)
+    return call(kernel, shapes, [VM] * 9, (VM, VM), [], 1 << 20, 1 << 20)(*args)
 
 
 def combine(ids, back, tok_rows, width, n_expert, n_y):
@@ -244,45 +349,22 @@
     messages = make_slots(expert_ids, gate_weights, tokens, grad_output, n_expert, n_y)
     got = exchange(messages, ("expert", "y"))
 
-    own = jnp.concatenate([clip_only(w_in, scale_in), clip_only(w_out, scale_out)], axis=0)
-    oth = swap(own)
-
-    part, xdy, gate_rows = gather(got, own, oth)
+    own, own_in, own_out = clip_weights(messages, w_in, scale_in, w_out, scale_out)
+    oth_in, oth_out = swap(own_in), swap(own_out)
+
+    part, xdy, gate_rows = gather(got, own, oth_in, oth_out)
     parts = exchange(part.reshape(n_dp, share, 3 * hidden), "dp")
-    total = jnp.sum(parts.astype(F32), axis=0)
-
-    z = lax.axis_index("dp")
-    gate = lax.dynamic_slice_in_dim(gate_rows, z * share, share, 0)[:, :1]
-
-    def activate(pre, back):
-        gate_pre, up_pre = pre[:, :units], pre[:, units:]
-        d_act = gate * back
-        sigmoid_gate = jax.nn.sigmoid(gate_pre)
-        silu_gate = gate_pre * sigmoid_gate
-        slope = sigmoid_gate * (1.0 + gate_pre * (1.0 - sigmoid_gate))
-        act = gate * silu_gate * up_pre
-        return d_act * up_pre * slope, d_act * silu_gate, act
-
-    first = activate(total[:, :hidden], total[:, 2 * hidden : 2 * hidden + units])
-    second = activate(total[:, hidden : 2 * hidden], total[:, 2 * hidden + units :])
-    mine = jnp.concatenate([*first, *second], axis=1).astype(BF16)
-    copies = jnp.broadcast_to(mine[None], (n_dp, share, 3 * hidden))
+    z = lax.axis_index("dp").astype(jnp.int32).reshape(1)
+    copies = activate(z, parts, gate_rows, units)
     full = exchange(copies, "dp").reshape(rows, 3 * hidden)
-    half = hidden + units
-
-    back = exchange(scatter(full, own, oth, parties), ("expert", "y"))
+
+    xdy_r = swap(xdy)
+    returns, dh_oth, act_oth = scatter(xdy_r, full, own, oth_in, parties)
+    back = exchange(returns, ("expert", "y"))
     grad_tokens = combine(expert_ids, back, tok_rows, width, n_expert, n_y)
 
-    xdy_r = swap(xdy)
-    full_r = swap(full[:, half:])
-    x, dy = xdy[:, :width], xdy[:, width:]
-    x_r, dy_r = xdy_r[:, :width], xdy_r[:, width:]
-    dh, act = full[:, :hidden], full[:, hidden:half]
-    dh_r, act_r = full_r[:, :hidden], full_r[:, hidden:]
-    sum_in = dot(x, dh, ((0,), (0,))) + dot(x_r, dh_r, ((0,), (0,)))
-    sum_out = dot(act, dy, ((0,), (0,))) + dot(act_r, dy_r, ((0,), (0,)))
-    grad_in = jnp.where(keep_mask(w_in, scale_in), sum_in, 0.0).astype(BF16)
-    grad_out = jnp.where(keep_mask(w_out, scale_out), sum_out, 0.0).astype(BF16)
+    dh_r, act_r = swap(dh_oth), swap(act_oth)
+    grad_in, grad_out = weight_grads(xdy, xdy_r, full, dh_r, act_r, w_in, scale_in, w_out, scale_out)
     return grad_tokens, grad_in[None], grad_out[None]
 
 

time: 150 us -> 144 us (0.960)
  blocking collectives: 39.6 us -> 0 us
  starting transfers between devices: 31.7 us -> 59 us
  local copies, waits for them, and re-layouts: 3.39 us -> 12.2 us
  matrix products: 6.01 us -> 0 us
  other arithmetic: 4.9 us -> 0 us
  waiting for transfers between devices: 56.3 us -> 60.4 us
  Pallas kernels: 6.99 us -> 10.9 us
    all_to_all x1 -> x0, blocking collectives: 39.6 us -> none  [exchange(): return lax.all_to_all(x, axes, split_axis=0, concat_axis=0, tiled=True)]
    all_to_all x3 -> x4, starting transfers between devices: 25.9 us -> 48.5 us  [exchange(): return lax.all_to_all(x, axes, split_axis=0, concat_axis=0, tiled=True)]
    unnamed x18 -> x36, local copies, waits for them, and re-layouts: 1.51 us -> 12.2 us
    dot_general x4 -> x0, matrix products: 6.01 us -> none  [dot(): return lax.dot_general(a, b, (dims, ((), ())), preferred_element_type=F32)]
    ppermute x3 -> x5, waiting for transfers between devices: 0.01 us -> 4.99 us  [swap(): return lax.ppermute(x, 'core', [(0, 1), (1, 0)])]
    ppermute x3 -> x5, starting transfers between devices: 5.75 us -> 10.6 us  [swap(): return lax.ppermute(x, 'core', [(0, 1), (1, 0)])]
    pallas_call x2 -> x5, Pallas kernels: 5.91 us -> 9.01 us  [the longest x1 3.44 us: gather(): call(kernel, shapes, [ANY, HBM, HBM, HBM], (HBM, HBM, VM), scratch, 4 * r...]
    mul x2 -> x0, other arithmetic: 1.52 us -> none  [clip_only(): bound = 448.0 * scales.astype(F32)]
  transfers between devices with their start and end apart: 6 -> 9, of which waited for: 3 -> 7; matrix products, arithmetic and copies ran while one was open for 5% -> 0% of each run, Pallas kernels for 2% -> 2%
where the time goes in v3:
time: 144 us; the launch traced here: 143 us
  waiting for transfers between devices  60.4 us (42%)
  starting transfers between devices  59 us (41%)
  local copies, waits for them, and re-layouts  12.2 us (8%)
  Pallas kernels  10.9 us (8%)
    all_to_all x4, waiting for transfers between devices, exchange(): return lax.all_to_all(x, axes, split_axis=0, concat_axis=0, tiled=True)  55.4 us
    all_to_all x4, starting transfers between devices, exchange(): return lax.all_to_all(x, axes, split_axis=0, concat_axis=0, tiled=True)  48.5 us
    unnamed x36, local copies, waits for them, and re-layouts  12.2 us
    ppermute x5, starting transfers between devices, swap(): return lax.ppermute(x, 'core', [(0, 1), (1, 0)])  10.6 us
    ppermute x5, waiting for transfers between devices, swap(): return lax.ppermute(x, 'core', [(0, 1), (1, 0)])  4.99 us
    pallas_call x1, Pallas kernels, gather(): call(kernel, shapes, [ANY, HBM, HBM, HBM], (HBM, HBM, VM), scratch, 4 * r...  3.44 us
  transfers between devices with their start and end apart: 9, of which 7 were waited for; matrix products, arithmetic and copies ran while one was open for 0% of the time, Pallas kernels for 2%

profile of v3, /device:TPU:4, one launch (start us, length us, event | category | flops | bytes accessed | tf_op | source)
XLA Modules:
  0.0 143.4 jit_solution(4637872621147757014)
XLA Ops:
  0.6 0.0 copy-start.11
  0.6 0.0 copy-start.10
  0.7 0.0 copy-start.5
  0.7 0.0 copy-start.12
  0.7 0.7 copy-done.12
  1.4 0.7 copy-done.14
  2.1 0.7 copy-done.15
  2.8 0.7 copy-done.16
  3.5 1.0 shard_map.103.after_ref
  4.5 17.3 %all-to-all-start = ((bf16[64,40,128]{2,1,0:T(8,128)(2,1)}), bf16[64,40,128]{2,1,0:T(8,128)(2,1)S(1)}, u32[]{:S(2)}, u32[]{:S(2)}) async-start(bf16[64,40,128]{2,1,0:T(8,128)(2,1)} %shard_map.103.after_ref), calls=%async_computation | async-start | bytes 1310720 | tf_op jit(solution)/shard_map/all_to_all | solution.py:22
  21.8 0.0 copy-done.11
  21.8 0.0 copy-done.10
  21.9 0.0 copy-done.5
  21.9 0.0 copy-start
  21.9 1.3 copy-done
  23.1 0.4 shard_map.104
  23.6 1.9 %collective-permute-start = (bf16[768,768]{1,0:T(8,128)(2,1)S(1)}, bf16[768,768]{1,0:T(8,128)(2,1)S(1)}, u32[]{:S(2)}, u32[]{:S(2)}) collective-permute-start(bf16[768,768]{1,0:T(8,128)(2,1)S(1)} %get-tuple-element.15), channel_id=1, source_target_pairs={{0,8},{8,0},{1,9},{9,1},{2,10},{10,2},{3,11},{11,3},{4,12},{12,4},... | collective-permute-start | bytes 3538952 | tf_op jit(solution)/shard_map/ppermute | solution.py:18
  25.5 2.4 %collective-permute-start.1 = (bf16[384,768]{1,0:T(8,128)(2,1)S(1)}, bf16[384,768]{1,0:T(8,128)(2,1)S(1)}, u32[]{:S(2)}, u32[]{:S(2)}) collective-permute-start(bf16[384,768]{1,0:T(8,128)(2,1)S(1)} %get-tuple-element.16), channel_id=1, source_target_pairs={{0,8},{8,0},{1,9},{9,1},{2,10},{10,2},{3,11},{11,3},{4,12},{12,4},... | collective-permute-start | bytes 1769480 | tf_op jit(solution)/shard_map/ppermute | solution.py:18
  27.9 1.6 %collective-permute-done.1.oth_out_ref = bf16[384,768]{1,0:T(8,128)(2,1)S(1)} collective-permute-done((bf16[384,768]{1,0:T(8,128)(2,1)S(1)}, bf16[384,768]{1,0:T(8,128)(2,1)S(1)}, u32[]{:S(2)}, u32[]{:S(2)}) %collective-permute-start.1) | collective-permute-done | bytes 589856 | tf_op jit(solution)/shard_map/ppermute | solution.py:18
  29.5 0.0 collective-permute-done.oth_in_ref.oth_ref
  29.5 1.0 copy-done.2
  30.5 9.8 %all-to-all-done = bf16[64,40,128]{2,1,0:T(8,128)(2,1)S(1)} async-done(((bf16[64,40,128]{2,1,0:T(8,128)(2,1)}), bf16[64,40,128]{2,1,0:T(8,128)(2,1)S(1)}, u32[]{:S(2)}, u32[]{:S(2)}) %all-to-all-start) | async-done | bytes 655392 | tf_op jit(solution)/shard_map/all_to_all | solution.py:22
  40.3 1.3 copy-done.3
  41.6 3.4 %shard_map.105 = (bf16[192,2304]{1,0:T(8,128)(2,1)}, bf16[192,1536]{1,0:T(8,128)(2,1)S(1)}, f32[192,128]{1,0:T(8,128)S(1)}) custom-call(bf16[2560,128]{1,0:T(8,128)(2,1)S(1)} %bitcast.14, bf16[1152,768]{1,0:T(8,128)(2,1)S(1)} %get-tuple-element.14.own_ref, bf16[768,768]{1,0:T(8,128)(2,1)S(1)} %copy-done.3, ...), custom_call_target="tpu_custom_call" | custom-call | flops 679477248 | bytes 5505024 | tf_op jit(solution)/shard_map/pallas_call | solution.py:293
  45.0 0.0 copy-start.7
  45.0 0.8 copy-done.7
  45.8 16.7 %all-to-all-start.1 = ((bf16[8,24,2304]{2,1,0:T(8,128)(2,1)}), bf16[8,24,2304]{2,1,0:T(8,128)(2,1)S(1)}, u32[]{:S(2)}, u32[]{:S(2)}) async-start(bf16[8,24,2304]{2,1,0:T(8,128)(2,1)} %bitcast.4), calls=%async_computation.1 | async-start | bytes 1769472 | tf_op jit(solution)/shard_map/all_to_all | solution.py:22
  62.5 22.7 %all-to-all-done.1.parts_ref = bf16[8,24,2304]{2,1,0:T(8,128)(2,1)S(1)} async-done(((bf16[8,24,2304]{2,1,0:T(8,128)(2,1)}), bf16[8,24,2304]{2,1,0:T(8,128)(2,1)S(1)}, u32[]{:S(2)}, u32[]{:S(2)}) %all-to-all-start.1) | async-done | bytes 884768 | tf_op jit(solution)/shard_map/all_to_all | solution.py:22
  85.2 1.1 shard_map.106
  86.3 3.5 %all-to-all-start.2 = ((bf16[8,24,2304]{2,1,0:T(8,128)(2,1)}), bf16[8,24,2304]{2,1,0:T(8,128)(2,1)S(1)}, u32[]{:S(2)}, u32[]{:S(2)}) async-start(bf16[8,24,2304]{2,1,0:T(8,128)(2,1)} %shard_map.106), calls=%async_computation.2 | async-start | bytes 1769472 | tf_op jit(solution)/shard_map/all_to_all | solution.py:22
  89.9 1.9 %collective-permute-start.2 = (bf16[192,1536]{1,0:T(8,128)(2,1)}, bf16[192,1536]{1,0:T(8,128)(2,1)S(1)}, u32[]{:S(2)}, u32[]{:S(2)}) collective-permute-start(bf16[192,1536]{1,0:T(8,128)(2,1)} %copy-done.7), channel_id=1, source_target_pairs={{0,8},{8,0},{1,9},{9,1},{2,10},{10,2},{3,11},{11,3},{4,12},{12,4},... | collective-permute-start | bytes 1769480 | tf_op jit(solution)/shard_map/ppermute | solution.py:18
  91.8 2.2 %collective-permute-done.2.after_ref.theirs_ref = bf16[192,1536]{1,0:T(8,128)(2,1)S(1)} collective-permute-done((bf16[192,1536]{1,0:T(8,128)(2,1)}, bf16[192,1536]{1,0:T(8,128)(2,1)S(1)}, u32[]{:S(2)}, u32[]{:S(2)}) %collective-permute-start.2) | collective-permute-done | bytes 589856 | tf_op jit(solution)/shard_map/ppermute | solution.py:18
  94.0 18.3 %all-to-all-done.2 = bf16[8,24,2304]{2,1,0:T(8,128)(2,1)S(1)} async-done(((bf16[8,24,2304]{2,1,0:T(8,128)(2,1)}), bf16[8,24,2304]{2,1,0:T(8,128)(2,1)S(1)}, u32[]{:S(2)}, u32[]{:S(2)}) %all-to-all-start.2) | async-done | bytes 884768 | tf_op jit(solution)/shard_map/all_to_all | solution.py:22
  112.2 1.3 copy-done.4
  113.5 1.9 %shard_map.107 = (bf16[1536,128]{1,0:T(8,128)(2,1)S(1)}, bf16[192,768]{1,0:T(8,128)(2,1)S(1)}, bf16[192,384]{1,0:T(8,128)(2,1)S(1)}) custom-call(bf16[192,1536]{1,0:T(8,128)(2,1)S(1)} %collective-permute-done.2.after_ref.theirs_ref, bf16[192,2304]{1,0:T(8,128)(2,1)S(1)} %bitcast.10, bf16[1152,768]{1,0:T(8,128)(2,1)S(1)} %get-tuple-element.14.own_ref, ...), custom_call_target="tpu_custom_call" | custom-call | flops 452984832 | bytes 3538944 | tf_op jit(solution)/shard_map/pallas_call | solution.py:318
  115.4 0.7 copy-done.9
  116.2 0.7 copy-done.17
  116.8 10.9 %all-to-all-start.3 = ((bf16[64,24,128]{2,1,0:T(8,128)(2,1)}), bf16[64,24,128]{2,1,0:T(8,128)(2,1)S(1)}, u32[]{:S(2)}, u32[]{:S(2)}) async-start(bf16[64,24,128]{2,1,0:T(8,128)(2,1)} %bitcast.18), calls=%async_computation.3 | async-start | bytes 786432 | tf_op jit(solution)/shard_map/all_to_all | solution.py:22
  127.8 1.9 %collective-permute-start.3 = (bf16[192,768]{1,0:T(8,128)(2,1)S(1)}, bf16[192,768]{1,0:T(8,128)(2,1)S(1)}, u32[]{:S(2)}, u32[]{:S(2)}) collective-permute-start(bf16[192,768]{1,0:T(8,128)(2,1)S(1)} %get-tuple-element.21), channel_id=1, source_target_pairs={{0,8},{8,0},{1,9},{9,1},{2,10},{10,2},{3,11},{11,3},{4,12},{12,4},... | collective-permute-start | bytes 884744 | tf_op jit(solution)/shard_map/ppermute | solution.py:18
  129.7 2.4 %collective-permute-start.4 = (bf16[192,384]{1,0:T(8,128)(2,1)}, bf16[192,384]{1,0:T(8,128)(2,1)S(1)}, u32[]{:S(2)}, u32[]{:S(2)}) collective-permute-start(bf16[192,384]{1,0:T(8,128)(2,1)} %copy-done.17), channel_id=1, source_target_pairs={{0,8},{8,0},{1,9},{9,1},{2,10},{10,2},{3,11},{11,3},{4,12},{12,4},... | collective-permute-start | bytes 442376 | tf_op jit(solution)/shard_map/ppermute | solution.py:18
  132.1 1.2 collective-permute-done.4.act_ref
  133.3 0.0 collective-permute-done.3.dh_ref
  133.3 1.3 copy-done.1
  134.6 1.1 copy-done.8
  135.7 2.2 %shard_map.109 = (bf16[768,768]{1,0:T(8,128)(2,1)}, bf16[384,768]{1,0:T(8,128)(2,1)}) custom-call(bf16[192,1536]{1,0:T(8,128)(2,1)S(1)} %copy-done.8, bf16[192,1536]{1,0:T(8,128)(2,1)S(1)} %collective-permute-done.2.after_ref.theirs_ref, bf16[192,2304]{1,0:T(8,128)(2,1)S(1)} %bitcast.11, bf16[192,768]{1,0:T(8,128)(2,1)S(1)} %collective-permute-done.3.dh_ref, ...), custom_call_target="tpu_custom_call" | custom-call | flops 1048576 | bytes 1048576 | tf_op jit(solution)/shard_map/pallas_call | solution.py:326
  137.8 4.6 %all-to-all-done.3 = bf16[64,24,128]{2,1,0:T(8,128)(2,1)S(1)} async-done(((bf16[64,24,128]{2,1,0:T(8,128)(2,1)}), bf16[64,24,128]{2,1,0:T(8,128)(2,1)S(1)}, u32[]{:S(2)}, u32[]{:S(2)}) %all-to-all-start.3) | async-done | bytes 393248 | tf_op jit(solution)/shard_map/all_to_all | solution.py:22
  142.5 0.0 copy-done.13
  142.5 0.9 shard_map.108
  (13 shorter events, 0.0 us)
Async XLA Ops:
  0.6 21.2 %copy-start.11 = (bf16[1,768]{1,0:T(2,128)(2,1)S(1)}, bf16[1,768]{1,0:T(2,128)(2,1)}, u32[]{:S(2)}) copy-start(bf16[1,768]{1,0:T(2,128)(2,1)} %scale_out_ref.3) | copy-start | bytes 4612
  0.6 21.2 %copy-start.10 = (bf16[1,768]{1,0:T(2,128)(2,1)S(1)}, bf16[1,768]{1,0:T(2,128)(2,1)}, u32[]{:S(2)}) copy-start(bf16[1,768]{1,0:T(2,128)(2,1)} %scale_in_ref.3) | copy-start | bytes 4612
  0.7 21.2 %copy-start.5 = (bf16[1,384,768]{2,1,0:T(8,128)(2,1)S(1)}, bf16[1,384,768]{2,1,0:T(8,128)(2,1)}, u32[]{:S(2)}) copy-start(bf16[1,384,768]{2,1,0:T(8,128)(2,1)} %param.14) | copy-start | bytes 1769476
  0.7 0.7 copy-start.12
  1.4 0.7 copy-start.14
  2.1 0.7 copy-start.15
  2.8 0.7 copy-start.16
  4.5 35.8 %all-to-all-start = ((bf16[64,40,128]{2,1,0:T(8,128)(2,1)}), bf16[64,40,128]{2,1,0:T(8,128)(2,1)S(1)}, u32[]{:S(2)}, u32[]{:S(2)}) async-start(bf16[64,40,128]{2,1,0:T(8,128)(2,1)} %shard_map.103.after_ref), calls=%async_computation | async-start | bytes 1310720 | tf_op jit(solution)/shard_map/all_to_all | solution.py:22
  21.9 1.3 copy-start
  23.6 6.0 %collective-permute-start = (bf16[768,768]{1,0:T(8,128)(2,1)S(1)}, bf16[768,768]{1,0:T(8,128)(2,1)S(1)}, u32[]{:S(2)}, u32[]{:S(2)}) collective-permute-start(bf16[768,768]{1,0:T(8,128)(2,1)S(1)} %get-tuple-element.15), channel_id=1, source_target_pairs={{0,8},{8,0},{1,9},{9,1},{2,10},{10,2},{3,11},{11,3},{4,12},{12,4},... | collective-permute-start | bytes 3538952 | tf_op jit(solution)/shard_map/ppermute | solution.py:18
  25.5 4.0 %collective-permute-start.1 = (bf16[384,768]{1,0:T(8,128)(2,1)S(1)}, bf16[384,768]{1,0:T(8,128)(2,1)S(1)}, u32[]{:S(2)}, u32[]{:S(2)}) collective-permute-start(bf16[384,768]{1,0:T(8,128)(2,1)S(1)} %get-tuple-element.16), channel_id=1, source_target_pairs={{0,8},{8,0},{1,9},{9,1},{2,10},{10,2},{3,11},{11,3},{4,12},{12,4},... | collective-permute-start | bytes 1769480 | tf_op jit(solution)/shard_map/ppermute | solution.py:18
  29.5 1.0 copy-start.2
  40.3 1.3 copy-start.3
  45.0 0.8 copy-start.7
  45.8 39.4 %all-to-all-start.1 = ((bf16[8,24,2304]{2,1,0:T(8,128)(2,1)}), bf16[8,24,2304]{2,1,0:T(8,128)(2,1)S(1)}, u32[]{:S(2)}, u32[]{:S(2)}) async-start(bf16[8,24,2304]{2,1,0:T(8,128)(2,1)} %bitcast.4), calls=%async_computation.1 | async-start | bytes 1769472 | tf_op jit(solution)/shard_map/all_to_all | solution.py:22
  86.3 25.9 %all-to-all-start.2 = ((bf16[8,24,2304]{2,1,0:T(8,128)(2,1)}), bf16[8,24,2304]{2,1,0:T(8,128)(2,1)S(1)}, u32[]{:S(2)}, u32[]{:S(2)}) async-start(bf16[8,24,2304]{2,1,0:T(8,128)(2,1)} %shard_map.106), calls=%async_computation.2 | async-start | bytes 1769472 | tf_op jit(solution)/shard_map/all_to_all | solution.py:22
  89.9 4.1 %collective-permute-start.2 = (bf16[192,1536]{1,0:T(8,128)(2,1)}, bf16[192,1536]{1,0:T(8,128)(2,1)S(1)}, u32[]{:S(2)}, u32[]{:S(2)}) collective-permute-start(bf16[192,1536]{1,0:T(8,128)(2,1)} %copy-done.7), channel_id=1, source_target_pairs={{0,8},{8,0},{1,9},{9,1},{2,10},{10,2},{3,11},{11,3},{4,12},{12,4},... | collective-permute-start | bytes 1769480 | tf_op jit(solution)/shard_map/ppermute | solution.py:18
  112.2 1.3 copy-start.4
  115.4 0.7 copy-start.9
  116.2 0.7 copy-start.17
  116.8 16.5 %copy-start.6 = (bf16[1,384,768]{2,1,0:T(8,128)(2,1)S(1)}, bf16[1,384,768]{2,1,0:T(8,128)(2,1)}, u32[]{:S(2)}) copy-start(bf16[1,384,768]{2,1,0:T(8,128)(2,1)} %param.14) | copy-start | bytes 1769476
  116.8 25.6 %all-to-all-start.3 = ((bf16[64,24,128]{2,1,0:T(8,128)(2,1)}), bf16[64,24,128]{2,1,0:T(8,128)(2,1)S(1)}, u32[]{:S(2)}, u32[]{:S(2)}) async-start(bf16[64,24,128]{2,1,0:T(8,128)(2,1)} %bitcast.18), calls=%async_computation.3 | async-start | bytes 786432 | tf_op jit(solution)/shard_map/all_to_all | solution.py:22
  127.8 5.5 %collective-permute-start.3 = (bf16[192,768]{1,0:T(8,128)(2,1)S(1)}, bf16[192,768]{1,0:T(8,128)(2,1)S(1)}, u32[]{:S(2)}, u32[]{:S(2)}) collective-permute-start(bf16[192,768]{1,0:T(8,128)(2,1)S(1)} %get-tuple-element.21), channel_id=1, source_target_pairs={{0,8},{8,0},{1,9},{9,1},{2,10},{10,2},{3,11},{11,3},{4,12},{12,4},... | collective-permute-start | bytes 884744 | tf_op jit(solution)/shard_map/ppermute | solution.py:18
  129.7 3.6 %collective-permute-start.4 = (bf16[192,384]{1,0:T(8,128)(2,1)}, bf16[192,384]{1,0:T(8,128)(2,1)S(1)}, u32[]{:S(2)}, u32[]{:S(2)}) collective-permute-start(bf16[192,384]{1,0:T(8,128)(2,1)} %copy-done.17), channel_id=1, source_target_pairs={{0,8},{8,0},{1,9},{9,1},{2,10},{10,2},{3,11},{11,3},{4,12},{12,4},... | collective-permute-start | bytes 442376 | tf_op jit(solution)/shard_map/ppermute | solution.py:18
  133.3 1.3 copy-start.1
  134.6 1.1 copy-start.8
  135.7 6.8 %copy-start.13 = (s32[4,4]{1,0:T(4,128)S(1)}, s32[4,4]{1,0:T(4,128)}, u32[]{:S(2)}) copy-start(s32[4,4]{1,0:T(4,128)} %ids_ref.3) | copy-start | bytes 196

commit v4 on v3

v4 whole, which is shorter than its diff:
```python
import functools
import jax
import jax.numpy as jnp
from jax import lax
from jax.experimental import pallas as pl
from jax.experimental.pallas import tpu as pltpu
from jax.sharding import Mesh, PartitionSpec as P

CAP = 3
CORES = 2
LANE = 128
MIB = 1024 * 1024
ROOMY, FULL = 28 * MIB, 60 * MIB
F32 = jnp.float32
BF16 = jnp.bfloat16


def swap(x):
    return lax.ppermute(x, "core", [(0, 1), (1, 0)])


def exchange(x, axes):
    return lax.all_to_all(x, axes, split_axis=0, concat_axis=0, tiled=True)


def dot(a, b, dims):
    return lax.dot_general(a, b, (dims, ((), ())), preferred_element_type=F32)


def up(n, m):
    return -(-n // m) * m


def routing(ids, n_expert):
    tok_rows, top = ids.shape
    at = lax.broadcasted_iota(jnp.int32, (n_expert, LANE), 0)
    seen = jnp.zeros((n_expert, LANE), jnp.int32)
    masks, named = [], []
    for i in range(tok_rows):
        hits = [jnp.broadcast_to(ids[i : i + 1, k : k + 1], at.shape) == at for k in range(top)]
        any_hit = functools.reduce(jnp.logical_or, hits)
        masks.append([any_hit & (seen == j) for j in range(CAP)])
        named.append(hits)
        seen = seen + any_hit.astype(jnp.int32)
    return masks, named


def start_all(pairs, sems, first=0):
    copies = [pltpu.make_async_copy(src, dst, sems.at[first + n]) for n, (src, dst) in enumerate(pairs)]
    for c in copies:
        c.start()
    return copies


def wait_all(copies):
    for c in copies:
        c.wait()


def slots_kernel(
    n_expert, n_y, size, ids_ref, gates_ref, tok_ref, cot_ref, out_ref, ids, gates, tok, cot, wide, narrow, sems
):
    tok_rows, width = tok.shape
    tiles = width // LANE
    copies = start_all([(ids_ref, ids), (gates_ref, gates), (tok_ref, tok), (cot_ref, cot)], sems)
    wide[...] = jnp.zeros_like(wide)
    wait_all(copies)
    masks, named = routing(ids[...], n_expert)
    gate = gates[...].astype(F32)
    lane = lax.broadcasted_iota(jnp.int32, (n_expert, LANE), 1)
    gate_row = jnp.zeros((n_expert, LANE), F32)
    for i in range(tok_rows):
        weight = jnp.zeros((n_expert, LANE), F32)
        for k, hit in enumerate(named[i]):
            weight = jnp.where(hit, jnp.broadcast_to(gate[i : i + 1, k : k + 1], hit.shape), weight)
        for j in range(CAP):
            gate_row = jnp.where(masks[i][j] & (lane == j), weight, gate_row)
    wide[pl.ds(2 * tiles * CAP, n_expert, stride=size), :] = gate_row
    both = [tok[...].astype(F32), cot[...].astype(F32)]
    for k in range(2 * tiles):
        at = (k % tiles) * LANE
        cols = both[k // tiles][:, at : at + LANE]
        for j in range(CAP):
            value = jnp.zeros((n_expert, LANE), F32)
            for i in range(tok_rows):
                value = jnp.where(masks[i][j], jnp.broadcast_to(cols[i : i + 1], value.shape), value)
            wide[pl.ds(j * 2 * tiles + k, n_expert, stride=size), :] = value
    narrow[...] = wide[...].reshape(n_expert, size, LANE).astype(BF16)
    wait_all(start_all([(narrow, out_ref.at[:, y]) for y in range(n_y)], sems, 4))


def gather_kernel(
    parties, size, got_ref, own_ref, oth_in_ref, oth_out_ref, part_ref, rows_ref, gate_ref,
    got, wide, own, oth, rows, part, gate, sems,
):
    width = own.shape[1]
    units = own.shape[0] - width
    tiles = width // LANE
    half = width + units
    copies = start_all(
        [
            (got_ref, got),
            (own_ref, own),
            (oth_in_ref, oth.at[0:width, :]),
            (oth_out_ref, oth.at[width:half, :]),
        ],
        sems,
    )
    copies[0].wait()
    wide[...] = got[...].astype(F32)
    gates = wide[pl.ds(2 * tiles * CAP, parties, stride=size), :]
    for j in range(CAP):
        at = slice(j * parties, (j + 1) * parties)
        gate[at, :] = jnp.broadcast_to(gates[:, j : j + 1], (parties, LANE))
        for k in range(2 * tiles):
            value = wide[pl.ds(j * 2 * tiles + k, parties, stride=size), :]
            rows[at, k * LANE : (k + 1) * LANE] = value.astype(BF16)
    outs = start_all([(rows, rows_ref), (gate, gate_ref)], sems, 4)
    for n, weights in enumerate((own, oth)):
        wait_all(copies[n + 1 : 2 + 2 * n])
        pre = dot(rows[:, :width], weights[:width, :], ((1,), (0,)))
        part[:, n * half : n * half + width] = pre.astype(BF16)
        back = dot(rows[:, width:], weights[width:, :], ((1,), (1,)))
        part[:, n * half + width : (n + 1) * half] = back.astype(BF16)
        cols = slice(n * half, (n + 1) * half)
        outs += start_all([(part.at[:, cols], part_ref.at[:, cols])], sems, 6 + n)
    wait_all(outs)


def clip_kernel(
    step, after_ref, w_in_ref, scale_in_ref, w_out_ref, scale_out_ref, own_ref, in_ref, out_ref,
    w_in, scale_in, w_out, scale_out, own, sems,
):
    del after_ref
    wait_all(
        start_all([(w_in_ref, w_in), (scale_in_ref, scale_in), (w_out_ref, w_out), (scale_out_ref, scale_out)], sems)
    )
    start = 0
    for weights, scales in ((w_in, scale_in), (w_out, scale_out)):
        bound = 448.0 * scales[...].astype(F32)
        for r in range(0, weights.shape[0], step):
            block = weights[r : r + step, :].astype(F32)
            own[start + r : start + r + step, :] = jnp.clip(block, -bound, bound).astype(BF16)
        start += weights.shape[0]
    tall = w_in.shape[0]
    wait_all(start_all([(own, own_ref), (own.at[0:tall, :], in_ref), (own.at[tall:start, :], out_ref)], sems, 4))


def activate_kernel(share, units, z_ref, parts_ref, gate_ref, out_ref, parts, gate, out, sems):
    n_dp = parts.shape[0]
    half = 3 * units
    at = pl.multiple_of(z_ref[0] * share, 8)
    halves = [slice(n * half, (n + 1) * half) for n in range(CORES)]
    copies = start_all(
        [(gate_ref.at[pl.ds(at, share), :], gate)] + [(parts_ref.at[:, :, h], parts.at[:, :, h]) for h in halves], sems
    )
    copies[0].wait()
    gates = gate[...]

    def total(at):
        value = parts[0, :, at : at + LANE].astype(F32)
        for p in range(1, n_dp):
            value = value + parts[p, :, at : at + LANE].astype(F32)
        return value

    outs = []
    for n in range(CORES):
        copies[1 + n].wait()
        for c in range(n * half, n * half + units, LANE):
            gate_pre = total(c)
            up_pre = total(c + units)
            d_act = gates * total(c + 2 * units)
            sigmoid_gate = jax.nn.sigmoid(gate_pre)
            silu_gate = gate_pre * sigmoid_gate
            slope = sigmoid_gate * (1.0 + gate_pre * (1.0 - sigmoid_gate))
            out[:, c : c + LANE] = (d_act * up_pre * slope).astype(BF16)
            out[:, c + units : c + units + LANE] = (d_act * silu_gate).astype(BF16)
            out[:, c + 2 * units : c + 2 * units + LANE] = (gates * silu_gate * up_pre).astype(BF16)
        pairs = [(out.at[:, halves[n]], out_ref.at[p, :, halves[n]]) for p in range(n_dp)]
        outs += start_all(pairs, sems, 1 + CORES + n * n_dp)
    wait_all(outs)


def scatter_kernel(
    parties, size, offset, after_ref, full_ref, own_ref, oth_ref, out_ref, dh_ref, act_ref, dh, own, oth, wide, out, sems
):
    del after_ref
    width = own.shape[0]
    hidden = own.shape[1]
    tiles = width // LANE
    copies = start_all(
        [
            (full_ref.at[:, 0:hidden], dh.at[0]),
            (own_ref.at[0:width, :], own),
            (full_ref.at[:, offset : offset + hidden], dh.at[1]),
            (oth_ref, oth),
            (full_ref.at[:, offset : offset + hidden], dh_ref),
            (full_ref.at[:, offset + hidden : 2 * offset], act_ref),
        ],
        sems,
    )
    wide[...] = jnp.zeros_like(wide)
    wait_all(copies[0:2])
    dx = dot(dh[0], own[...], ((1,), (1,)))
    wait_all(copies[2:4])
    dx = dx + dot(dh[1], oth[...], ((1,), (1,)))
    for j in range(CAP):
        for k in range(tiles):
            value = dx[j * parties : (j + 1) * parties, k * LANE : (k + 1) * LANE]
            wide[pl.ds(j * tiles + k, parties, stride=size), :] = value
    out[...] = wide[...].astype(BF16)
    wait_all(copies[4:] + start_all([(out, out_ref)], sems, 6))


def grads_kernel(step, *refs):
    n_in = 9
    sources, (in_ref, out_ref) = refs[:n_in], refs[n_in : n_in + 2]
    held, (in_v, out_v, sems) = refs[n_in + 2 : 2 * n_in + 2], refs[2 * n_in + 2 :]
    mine, theirs, full, dh, act, w_in, scale_in, w_out, scale_out = held
    half = full.shape[1]
    pairs = [(src.at[:, 0:half] if dst is full else src, dst) for src, dst in zip(sources, held)]
    wait_all(start_all(pairs, sems))
    width, hidden = w_in.shape
    outs = []
    for n, (weights, scales, grad, dst) in enumerate(((w_in, scale_in, in_v, in_ref), (w_out, scale_out, out_v, out_ref))):
        bound = 448.0 * scales[...].astype(F32)
        for r in range(0, weights.shape[0], step):
            at = slice(r, r + step)
            if grad is in_v:
                total = dot(mine[:, at], full[:, :hidden], ((0,), (0,)))
                total = total + dot(theirs[:, at], dh[...], ((0,), (0,)))
            else:
                total = dot(full[:, hidden + r : hidden + r + step], mine[:, width:], ((0,), (0,)))
                total = total + dot(act[:, at], theirs[:, width:], ((0,), (0,)))
            keep = jnp.abs(weights[at, :].astype(F32)) <= bound
            grad[at, :] = jnp.where(keep, total, 0.0).astype(BF16)
        outs += start_all([(grad, dst)], sems, n_in + n)
    wait_all(outs)


def combine_kernel(n_expert, n_y, size, ids_ref, back_ref, out_ref, ids, back, wide, out, sems):
    tok_rows, width = out.shape
    tiles = width // LANE
    parties = n_expert * n_y
    copies = start_all([(ids_ref, ids), (back_ref, back)], sems)
    copies[0].wait()
    masks, _ = routing(ids[...], n_expert)
    copies[1].wait()
    wide[...] = back[...].astype(F32)
    for k in range(tiles):
        totals = [jnp.zeros((1, LANE), F32) for _ in range(tok_rows)]
        for j in range(CAP):
            value = wide[pl.ds(j * tiles + k, parties, stride=size), :]
            value = jnp.sum(value.reshape(n_expert, n_y, LANE), axis=1)
            for i in range(tok_rows):
                totals[i] = totals[i] + jnp.sum(jnp.where(masks[i][j], value, 0.0), axis=0, keepdims=True)
        out[:, k * LANE : (k + 1) * LANE] = jnp.concatenate(totals, axis=0).astype(BF16)
    wait_all(start_all([(out, out_ref)], sems, 2))


ANY = pl.BlockSpec(memory_space=pl.ANY)
SMEM = pl.BlockSpec(memory_space=pltpu.SMEM)


def array(shape, dtype=BF16):
    return jax.ShapeDtypeStruct(shape, dtype)


def call(kernel, outs, scratch, n_sems, flops, moved, *args, limit=FULL):
    return pl.pallas_call(
        kernel,
        out_shape=outs,
        in_specs=[SMEM if a.shape == (1,) else ANY for a in args],
        out_specs=jax.tree.map(lambda _: ANY, outs),
        scratch_shapes=[pltpu.VMEM(*s) for s in scratch] + [pltpu.SemaphoreType.DMA((n_sems,))],
        compiler_params=pltpu.CompilerParams(vmem_limit_bytes=limit),
        cost_estimate=pl.CostEstimate(flops=flops, bytes_accessed=moved, transcendentals=0),
    )(*args)


def like(*arrays):
    return [(a.shape, a.dtype) for a in arrays]


def make_slots(ids, gates, tokens, cotangents, n_expert, n_y):
    size = up(2 * CAP * tokens.shape[1] // LANE + 1, 8)
    args = (ids, gates, tokens, cotangents)
    scratch = like(*args) + [((n_expert * size, LANE), F32), ((n_expert, size, LANE), BF16)]
    kernel = functools.partial(slots_kernel, n_expert, n_y, size)
    out = call(kernel, array((n_expert, n_y, size, LANE)), scratch, 4 + n_y, 1 << 20, 1 << 20, *args)
    return out.reshape(n_expert * n_y, size, LANE)


def clip_weights(after, w_in, scale_in, w_out, scale_out):
    width = w_in.shape[1]
    args = (w_in, scale_in, w_out, scale_out)
    heights = (w_in.shape[0] + w_out.shape[0], w_in.shape[0], w_out.shape[0])
    scratch = like(*args) + [((heights[0], width), BF16)]
    size = heights[0] * width
    kernel = functools.partial(clip_kernel, 64)
    return call(kernel, tuple(array((h, width)) for h in heights), scratch, 7, 4 * size, 4 * size, after, *args)


def activate(z, parts, gate_rows, units):
    n_dp, share, cols = parts.shape
    scratch = like(parts) + [((share, LANE), F32), ((share, cols), BF16)]
    kernel = functools.partial(activate_kernel, share, units)
    n_sems = 1 + CORES + CORES * n_dp
    return call(kernel, array(parts.shape), scratch, n_sems, 2 * parts.size, 4 * parts.size, z, parts, gate_rows, limit=ROOMY)


def gather(got, own, oth_in, oth_out):
    parties, size, _ = got.shape
    height, width = own.shape
    rows = parties * CAP
    flat = got.reshape(parties * size, LANE)
    shapes = (array((rows, 2 * height)), array((rows, 2 * width)), array((rows, LANE), F32))
    scratch = like(flat) + [(flat.shape, F32)] + like(own, own, shapes[1], shapes[0], shapes[2])
    kernel = functools.partial(gather_kernel, parties, size)
    moved = 4 * own.size + 6 * got.size
    return call(kernel, shapes, scratch, 6 + CORES, 4 * rows * own.size, moved, flat, own, oth_in, oth_out)


def scatter(after, full, own, oth, parties):
    rows = full.shape[0]
    height, width = own.shape
    hidden = width
    size = up(CAP * width // LANE, 8)
    flat = array((parties * size, LANE))
    shapes = (flat, array((rows, hidden)), array((rows, height - width)))
    scratch = [((2, rows, hidden), BF16), (oth.shape, BF16), (oth.shape, BF16), (flat.shape, F32), (flat.shape, BF16)]
    kernel = functools.partial(scatter_kernel, parties, size, height)
    flops, moved = 4 * rows * width * hidden, 4 * own.size
    out, dh, act = call(kernel, shapes, scratch, 7, flops, moved, after, full, own, oth)
    return out.reshape(parties, size, LANE), dh, act


def weight_grads(mine, theirs, full, dh, act, w_in, scale_in, w_out, scale_out):
    shapes = (array(w_in.shape), array(w_out.shape))
    kernel = functools.partial(grads_kernel, 128)
    args = (mine, theirs, full, dh, act, w_in, scale_in, w_out, scale_out)
    held = like(*args)
    held[2] = ((full.shape[0], full.shape[1] // CORES), BF16)
    return call(kernel, shapes, held + like(*shapes), len(args) + 2, 1 << 20, 1 << 20, *args)


def combine(ids, back, tok_rows, width, n_expert, n_y):
    parties, size, _ = back.shape
    flat = back.reshape(parties * size, LANE)
    shape = array((tok_rows, width))
    scratch = like(ids, flat) + [(flat.shape, F32)] + like(shape)
    kernel = functools.partial(combine_kernel, n_expert, n_y, size)
    return call(kernel, shape, scratch, 3, 1 << 20, 1 << 20, ids, flat, limit=ROOMY)


def per_device(tokens, grad_output, expert_ids, gate_weights, w_in, scale_in, w_out, scale_out):
    n_expert = lax.axis_size("expert")
    n_y = lax.axis_size("y")
    n_dp = lax.axis_size("dp")
    tok_rows, width = tokens.shape
    units = w_out.shape[1]
    hidden = 2 * units
    w_in, w_out = w_in[0], w_out[0]
    parties = n_expert * n_y
    rows = parties * CAP
    share = rows // n_dp

    messages = make_slots(expert_ids, gate_weights, tokens, grad_output, n_expert, n_y)
    got = exchange(messages, ("expert", "y"))

    own, own_in, own_out = clip_weights(messages, w_in, scale_in, w_out, scale_out)
    oth_in, oth_out = swap(own_in), swap(own_out)

    part, xdy, gate_rows = gather(got, own, oth_in, oth_out)
    parts = exchange(part.reshape(n_dp, share, 3 * hidden), "dp")
    z = lax.axis_index("dp").astype(jnp.int32).reshape(1)
    copies = activate(z, parts, gate_rows, units)
    full = exchange(copies, "dp").reshape(rows, 3 * hidden)

    xdy_r = swap(xdy)
    returns, dh_oth, act_oth = scatter(xdy_r, full, own, oth_in, parties)
    back = exchange(returns, ("expert", "y"))
    grad_tokens = combine(expert_ids, back, tok_rows, width, n_expert, n_y)

    dh_r, act_r = swap(dh_oth), swap(act_oth)
    grad_in, grad_out = weight_grads(xdy, xdy_r, full, dh_r, act_r, w_in, scale_in, w_out, scale_out)
    return grad_tokens, grad_in[None], grad_out[None]


def solution(mesh):
    names = ("expert", "y", "core", "dp")
    n_expert, n_tensor, n_dp = (mesh.shape[a] for a in ("expert", "tensor", "dp"))
    fine = Mesh(mesh.devices.reshape(n_expert, n_tensor // CORES, CORES, n_dp), names)
    tensor = ("y", "core")
    block = ("expert", "y", "core")
    placed = (
        P(block, "dp"),
        P(block, "dp"),
        P(block, None),
        P(block, None),
        P("expert", "dp", tensor),
        P("expert", tensor),
        P("expert", tensor, "dp"),
        P("expert", "dp"),
    )
    return jax.shard_map(
        per_device,
        mesh=fine,
        in_specs=placed,
        out_specs=(P(block, "dp"), P("expert", "dp", tensor), P("expert", tensor, "dp")),
        check_vma=False,
    )
```

time: 144 us -> 153 us (1.062)
  Pallas kernels: 10.9 us -> 30.7 us
  local copies, waits for them, and re-layouts: 12.2 us -> 3.11 us
  waiting for transfers between devices: 60.4 us -> 58.3 us
    pallas_call x7, Pallas kernels: 10.9 us -> 30.7 us  [call(): pl.pallas_call(kernel, out_shape=outs, in_specs=[SMEM if a.shape == (1,)...]
    unnamed x36 -> x20, local copies, waits for them, and re-layouts: 12.2 us -> 3.11 us
    all_to_all x4, waiting for transfers between devices: 55.4 us -> 53.3 us  [exchange(): return lax.all_to_all(x, axes, split_axis=0, concat_axis=0, tiled=True)]
  transfers between devices with their start and end apart: 9 -> 9, of which waited for: 7 -> 7; matrix products, arithmetic and copies ran while one was open for 0% -> 0% of each run, Pallas kernels for 2% -> 5%
where the time goes in v4:
time: 153 us; the launch traced here: 152 us
  starting transfers between devices  59.2 us (39%)
  waiting for transfers between devices  58.3 us (38%)
  Pallas kernels  30.7 us (20%)
  local copies, waits for them, and re-layouts  3.11 us (2%)
    all_to_all x4, waiting for transfers between devices, exchange(): return lax.all_to_all(x, axes, split_axis=0, concat_axis=0, tiled=True)  53.3 us
    all_to_all x4, starting transfers between devices, exchange(): return lax.all_to_all(x, axes, split_axis=0, concat_axis=0, tiled=True)  48.7 us
    pallas_call x7, Pallas kernels, call(): pl.pallas_call(kernel, out_shape=outs, in_specs=[SMEM if a.shape == (1,)...  30.7 us
    ppermute x5, starting transfers between devices, swap(): return lax.ppermute(x, 'core', [(0, 1), (1, 0)])  10.6 us
    ppermute x5, waiting for transfers between devices, swap(): return lax.ppermute(x, 'core', [(0, 1), (1, 0)])  4.99 us
    unnamed x20, local copies, waits for them, and re-layouts  3.11 us
  transfers between devices with their start and end apart: 9, of which 7 were waited for; matrix products, arithmetic and copies ran while one was open for 0% of the time, Pallas kernels for 5%

profile of v4, /device:TPU:4, one launch (start us, length us, event | category | flops | bytes accessed | tf_op | source)
XLA Modules:
  0.0 152.1 jit_solution(11105396031200091088)
XLA Ops:
  0.6 1.9 %shard_map.103 = bf16[8,8,40,128]{3,2,1,0:T(8,128)(2,1)} custom-call(s32[4,4]{1,0:T(4,128)} %ids_ref.3, bf16[4,4]{1,0:T(4,128)(2,1)} %gates_ref.1, bf16[4,768]{1,0:T(4,128)(2,1)} %tok_ref.1, bf16[4,768]{1,0:T(4,128)(2,1)} %cot_ref.1), custom_call_target="tpu_custom_call" | custom-call | flops 1048576 | bytes 1048576 | tf_op jit(solution)/shard_map/pallas_call | solution.py:270
  2.5 17.3 %all-to-all-start = ((bf16[64,40,128]{2,1,0:T(8,128)(2,1)}), bf16[64,40,128]{2,1,0:T(8,128)(2,1)S(1)}, u32[]{:S(2)}, u32[]{:S(2)}) async-start(bf16[64,40,128]{2,1,0:T(8,128)(2,1)} %bitcast.14), calls=%async_computation | async-start | bytes 1310720 | tf_op jit(solution)/shard_map/all_to_all | solution.py:23
  19.9 3.7 %shard_map.104 = (bf16[1152,768]{1,0:T(8,128)(2,1)}, bf16[768,768]{1,0:T(8,128)(2,1)}, bf16[384,768]{1,0:T(8,128)(2,1)}) custom-call(bf16[64,40,128]{2,1,0:T(8,128)(2,1)} %bitcast.15, bf16[768,768]{1,0:T(8,128)(2,1)} %bitcast.16, bf16[1,768]{1,0:T(2,128)(2,1)} %refs_6_.1, bf16[384,768]{1,0:T(8,128)(2,1)} %bitcast.19, bf16[1,768]{1,0:T(2,128)(2,1)} %refs_8_.1), custom_call_target="tpu_custom_call" | custom-call | flops 3538944 | bytes 3538944 | tf_op jit(solution)/shard_map/pallas_call | solution.py:270
  23.6 1.9 %collective-permute-start = (bf16[768,768]{1,0:T(8,128)(2,1)}, bf16[768,768]{1,0:T(8,128)(2,1)S(1)}, u32[]{:S(2)}, u32[]{:S(2)}) collective-permute-start(bf16[768,768]{1,0:T(8,128)(2,1)} %get-tuple-element.15), channel_id=1, source_target_pairs={{0,8},{8,0},{1,9},{9,1},{2,10},{10,2},{3,11},{11,3},{4,12},{12,4},... | collective-permute-start | bytes 3538952 | tf_op jit(solution)/shard_map/ppermute | solution.py:19
  25.5 2.4 %collective-permute-start.1 = (bf16[384,768]{1,0:T(8,128)(2,1)}, bf16[384,768]{1,0:T(8,128)(2,1)S(1)}, u32[]{:S(2)}, u32[]{:S(2)}) collective-permute-start(bf16[384,768]{1,0:T(8,128)(2,1)} %get-tuple-element.16), channel_id=1, source_target_pairs={{0,8},{8,0},{1,9},{9,1},{2,10},{10,2},{3,11},{11,3},{4,12},{12,4},... | collective-permute-start | bytes 1769480 | tf_op jit(solution)/shard_map/ppermute | solution.py:19
  27.9 1.8 %collective-permute-done.1.oth_out_ref = bf16[384,768]{1,0:T(8,128)(2,1)S(1)} collective-permute-done((bf16[384,768]{1,0:T(8,128)(2,1)}, bf16[384,768]{1,0:T(8,128)(2,1)S(1)}, u32[]{:S(2)}, u32[]{:S(2)}) %collective-permute-start.1) | collective-permute-done | bytes 589856 | tf_op jit(solution)/shard_map/ppermute | solution.py:19
  29.7 0.0 copy-start.7
  29.7 0.0 collective-permute-done.oth_in_ref.oth_ref
  29.7 0.0 copy-start.3
  29.7 8.6 %all-to-all-done = bf16[64,40,128]{2,1,0:T(8,128)(2,1)S(1)} async-done(((bf16[64,40,128]{2,1,0:T(8,128)(2,1)}), bf16[64,40,128]{2,1,0:T(8,128)(2,1)S(1)}, u32[]{:S(2)}, u32[]{:S(2)}) %all-to-all-start) | async-done | bytes 655392 | tf_op jit(solution)/shard_map/all_to_all | solution.py:23
  38.3 0.0 copy-start.4
  38.3 0.0 copy-done.7
  38.3 0.0 copy-done.3
  38.3 0.8 copy-done.4
  39.2 3.9 %shard_map.105 = (bf16[192,2304]{1,0:T(8,128)(2,1)}, bf16[192,1536]{1,0:T(8,128)(2,1)}, f32[192,128]{1,0:T(8,128)}) custom-call(bf16[2560,128]{1,0:T(8,128)(2,1)} %bitcast.18, bf16[1152,768]{1,0:T(8,128)(2,1)} %get-tuple-element.14.own_ref, bf16[768,768]{1,0:T(8,128)(2,1)} %copy-done.3, bf16[384,768]{1,0:T(8,128)(2,1)} %copy-done.7), custom_call_target="tpu_custom_call" | custom-call | flops 679477248 | bytes 5505024 | tf_op jit(solution)/shard_map/pallas_call | solution.py:270
  43.0 0.0 copy-start
  43.0 16.8 %all-to-all-start.1 = ((bf16[8,24,2304]{2,1,0:T(8,128)(2,1)}), bf16[8,24,2304]{2,1,0:T(8,128)(2,1)S(1)}, u32[]{:S(2)}, u32[]{:S(2)}) async-start(bf16[8,24,2304]{2,1,0:T(8,128)(2,1)} %bitcast.21), calls=%async_computation.1 | async-start | bytes 1769472 | tf_op jit(solution)/shard_map/all_to_all | solution.py:23
  59.8 22.7 %all-to-all-done.1.parts_ref = bf16[8,24,2304]{2,1,0:T(8,128)(2,1)S(1)} async-done(((bf16[8,24,2304]{2,1,0:T(8,128)(2,1)}), bf16[8,24,2304]{2,1,0:T(8,128)(2,1)S(1)}, u32[]{:S(2)}, u32[]{:S(2)}) %all-to-all-start.1) | async-done | bytes 884768 | tf_op jit(solution)/shard_map/all_to_all | solution.py:23
  82.5 0.0 copy-done
  82.5 1.3 shard_map.106
  83.8 0.0 copy-start.6
  83.8 3.7 %all-to-all-start.2 = ((bf16[8,24,2304]{2,1,0:T(8,128)(2,1)}), bf16[8,24,2304]{2,1,0:T(8,128)(2,1)S(1)}, u32[]{:S(2)}, u32[]{:S(2)}) async-start(bf16[8,24,2304]{2,1,0:T(8,128)(2,1)} %shard_map.106), calls=%async_computation.2 | async-start | bytes 1769472 | tf_op jit(solution)/shard_map/all_to_all | solution.py:23
  87.5 0.0 copy-done.6
  87.5 1.9 %collective-permute-start.2 = (bf16[192,1536]{1,0:T(8,128)(2,1)S(1)}, bf16[192,1536]{1,0:T(8,128)(2,1)S(1)}, u32[]{:S(2)}, u32[]{:S(2)}) collective-permute-start(bf16[192,1536]{1,0:T(8,128)(2,1)S(1)} %copy-done.6), channel_id=1, source_target_pairs={{0,8},{8,0},{1,9},{9,1},{2,10},{10,2},{3,11},{11,3},{4,12},{12,4},... | collective-permute-start | bytes 1769480 | tf_op jit(solution)/shard_map/ppermute | solution.py:19
  89.5 2.0 %collective-permute-done.2.after_ref.refs_1_ = bf16[192,1536]{1,0:T(8,128)(2,1)S(1)} collective-permute-done((bf16[192,1536]{1,0:T(8,128)(2,1)S(1)}, bf16[192,1536]{1,0:T(8,128)(2,1)S(1)}, u32[]{:S(2)}, u32[]{:S(2)}) %collective-permute-start.2) | collective-permute-done | bytes 589856 | tf_op jit(solution)/shard_map/ppermute | solution.py:19
  91.4 0.0 copy-start.5
  91.4 18.5 %all-to-all-done.2 = bf16[8,24,2304]{2,1,0:T(8,128)(2,1)S(1)} async-done(((bf16[8,24,2304]{2,1,0:T(8,128)(2,1)}), bf16[8,24,2304]{2,1,0:T(8,128)(2,1)S(1)}, u32[]{:S(2)}, u32[]{:S(2)}) %all-to-all-start.2) | async-done | bytes 884768 | tf_op jit(solution)/shard_map/all_to_all | solution.py:23
  109.9 0.0 copy-start.2
  109.9 0.0 copy-done.5
  109.9 0.9 copy-done.2
  110.8 14.6 %shard_map.107 = (bf16[1536,128]{1,0:T(8,128)(2,1)}, bf16[192,768]{1,0:T(8,128)(2,1)}, bf16[192,384]{1,0:T(8,128)(2,1)}) custom-call(bf16[192,1536]{1,0:T(8,128)(2,1)} %copy-done.5, bf16[192,2304]{1,0:T(8,128)(2,1)} %bitcast.12, bf16[1152,768]{1,0:T(8,128)(2,1)} %get-tuple-element.14.own_ref, bf16[768,768]{1,0:T(8,128)(2,1)} %copy-done.3), custom_call_target="tpu_custom_call" | custom-call | flops 452984832 | bytes 3538944 | tf_op jit(solution)/shard_map/pallas_call | solution.py:270
  125.4 10.8 %all-to-all-start.3 = ((bf16[64,24,128]{2,1,0:T(8,128)(2,1)}), bf16[64,24,128]{2,1,0:T(8,128)(2,1)S(1)}, u32[]{:S(2)}, u32[]{:S(2)}) async-start(bf16[64,24,128]{2,1,0:T(8,128)(2,1)} %bitcast.22), calls=%async_computation.3 | async-start | bytes 786432 | tf_op jit(solution)/shard_map/all_to_all | solution.py:23
  136.2 1.9 %collective-permute-start.3 = (bf16[192,768]{1,0:T(8,128)(2,1)}, bf16[192,768]{1,0:T(8,128)(2,1)S(1)}, u32[]{:S(2)}, u32[]{:S(2)}) collective-permute-start(bf16[192,768]{1,0:T(8,128)(2,1)} %get-tuple-element.21), channel_id=1, source_target_pairs={{0,8},{8,0},{1,9},{9,1},{2,10},{10,2},{3,11},{11,3},{4,12},{12,4},... | collective-permute-start | bytes 884744 | tf_op jit(solution)/shard_map/ppermute | solution.py:19
  138.1 0.0 copy-start.1
  138.2 2.4 %collective-permute-start.4 = (bf16[192,384]{1,0:T(8,128)(2,1)}, bf16[192,384]{1,0:T(8,128)(2,1)S(1)}, u32[]{:S(2)}, u32[]{:S(2)}) collective-permute-start(bf16[192,384]{1,0:T(8,128)(2,1)} %get-tuple-element.22), channel_id=1, source_target_pairs={{0,8},{8,0},{1,9},{9,1},{2,10},{10,2},{3,11},{11,3},{4,12},{12,4},... | collective-permute-start | bytes 442376 | tf_op jit(solution)/shard_map/ppermute | solution.py:19
  140.6 1.2 collective-permute-done.4.refs_4_
  141.8 0.0 copy-start.9
  141.8 0.0 collective-permute-done.3.refs_3_
  141.8 0.6 copy-done.9
  142.4 0.0 copy-start.8
  142.4 0.7 copy-done.8
  143.1 4.2 %shard_map.109 = (bf16[768,768]{1,0:T(8,128)(2,1)}, bf16[384,768]{1,0:T(8,128)(2,1)}) custom-call(bf16[192,1536]{1,0:T(8,128)(2,1)} %get-tuple-element.17.refs_0_, bf16[192,1536]{1,0:T(8,128)(2,1)} %copy-done.5, bf16[192,2304]{1,0:T(8,128)(2,1)} %bitcast.13, bf16[192,768]{1,0:T(8,128)(2,1)} %copy-done.8, bf16[192,384]{1,0:T(8,128)(2,1)} %copy-done.9, ...), custom_call_target="tpu_custom_call" | custom-call | flops 1048576 | bytes 1048576 | tf_op jit(solution)/shard_map/pallas_call | solution.py:270
  147.3 3.6 %all-to-all-done.3 = bf16[64,24,128]{2,1,0:T(8,128)(2,1)S(1)} async-done(((bf16[64,24,128]{2,1,0:T(8,128)(2,1)}), bf16[64,24,128]{2,1,0:T(8,128)(2,1)S(1)}, u32[]{:S(2)}, u32[]{:S(2)}) %all-to-all-start.3) | async-done | bytes 393248 | tf_op jit(solution)/shard_map/all_to_all | solution.py:23
  150.9 0.0 copy-done.1
  150.9 1.2 shard_map.108
Async XLA Ops:
  2.5 35.8 %all-to-all-start = ((bf16[64,40,128]{2,1,0:T(8,128)(2,1)}), bf16[64,40,128]{2,1,0:T(8,128)(2,1)S(1)}, u32[]{:S(2)}, u32[]{:S(2)}) async-start(bf16[64,40,128]{2,1,0:T(8,128)(2,1)} %bitcast.14), calls=%async_computation | async-start | bytes 1310720 | tf_op jit(solution)/shard_map/all_to_all | solution.py:23
  23.6 6.2 %collective-permute-start = (bf16[768,768]{1,0:T(8,128)(2,1)}, bf16[768,768]{1,0:T(8,128)(2,1)S(1)}, u32[]{:S(2)}, u32[]{:S(2)}) collective-permute-start(bf16[768,768]{1,0:T(8,128)(2,1)} %get-tuple-element.15), channel_id=1, source_target_pairs={{0,8},{8,0},{1,9},{9,1},{2,10},{10,2},{3,11},{11,3},{4,12},{12,4},... | collective-permute-start | bytes 3538952 | tf_op jit(solution)/shard_map/ppermute | solution.py:19
  25.5 4.2 %collective-permute-start.1 = (bf16[384,768]{1,0:T(8,128)(2,1)}, bf16[384,768]{1,0:T(8,128)(2,1)S(1)}, u32[]{:S(2)}, u32[]{:S(2)}) collective-permute-start(bf16[384,768]{1,0:T(8,128)(2,1)} %get-tuple-element.16), channel_id=1, source_target_pairs={{0,8},{8,0},{1,9},{9,1},{2,10},{10,2},{3,11},{11,3},{4,12},{12,4},... | collective-permute-start | bytes 1769480 | tf_op jit(solution)/shard_map/ppermute | solution.py:19
  29.7 8.6 %copy-start.7 = (bf16[384,768]{1,0:T(8,128)(2,1)}, bf16[384,768]{1,0:T(8,128)(2,1)S(1)}, u32[]{:S(2)}) copy-start(bf16[384,768]{1,0:T(8,128)(2,1)S(1)} %collective-permute-done.1.oth_out_ref) | copy-start | bytes 1769476
  29.7 8.6 %copy-start.3 = (bf16[768,768]{1,0:T(8,128)(2,1)}, bf16[768,768]{1,0:T(8,128)(2,1)S(1)}, u32[]{:S(2)}) copy-start(bf16[768,768]{1,0:T(8,128)(2,1)S(1)} %collective-permute-done.oth_in_ref.oth_ref) | copy-start | bytes 3538948
  38.3 0.8 copy-start.4
  43.0 39.5 %copy-start = (f32[192,128]{1,0:T(8,128)S(1)}, f32[192,128]{1,0:T(8,128)}, u32[]{:S(2)}) copy-start(f32[192,128]{1,0:T(8,128)} %get-tuple-element.19.gate_ref) | copy-start | bytes 294916
  43.0 39.5 %all-to-all-start.1 = ((bf16[8,24,2304]{2,1,0:T(8,128)(2,1)}), bf16[8,24,2304]{2,1,0:T(8,128)(2,1)S(1)}, u32[]{:S(2)}, u32[]{:S(2)}) async-start(bf16[8,24,2304]{2,1,0:T(8,128)(2,1)} %bitcast.21), calls=%async_computation.1 | async-start | bytes 1769472 | tf_op jit(solution)/shard_map/all_to_all | solution.py:23
  83.8 3.7 %copy-start.6 = (bf16[192,1536]{1,0:T(8,128)(2,1)S(1)}, bf16[192,1536]{1,0:T(8,128)(2,1)}, u32[]{:S(2)}) copy-start(bf16[192,1536]{1,0:T(8,128)(2,1)} %get-tuple-element.17.refs_0_) | copy-start | bytes 1769476
  83.8 26.1 %all-to-all-start.2 = ((bf16[8,24,2304]{2,1,0:T(8,128)(2,1)}), bf16[8,24,2304]{2,1,0:T(8,128)(2,1)S(1)}, u32[]{:S(2)}, u32[]{:S(2)}) async-start(bf16[8,24,2304]{2,1,0:T(8,128)(2,1)} %shard_map.106), calls=%async_computation.2 | async-start | bytes 1769472 | tf_op jit(solution)/shard_map/all_to_all | solution.py:23
  87.5 3.9 %collective-permute-start.2 = (bf16[192,1536]{1,0:T(8,128)(2,1)S(1)}, bf16[192,1536]{1,0:T(8,128)(2,1)S(1)}, u32[]{:S(2)}, u32[]{:S(2)}) collective-permute-start(bf16[192,1536]{1,0:T(8,128)(2,1)S(1)} %copy-done.6), channel_id=1, source_target_pairs={{0,8},{8,0},{1,9},{9,1},{2,10},{10,2},{3,11},{11,3},{4,12},{12,4},... | collective-permute-start | bytes 1769480 | tf_op jit(solution)/shard_map/ppermute | solution.py:19
  91.4 18.5 %copy-start.5 = (bf16[192,1536]{1,0:T(8,128)(2,1)}, bf16[192,1536]{1,0:T(8,128)(2,1)S(1)}, u32[]{:S(2)}) copy-start(bf16[192,1536]{1,0:T(8,128)(2,1)S(1)} %collective-permute-done.2.after_ref.refs_1_) | copy-start | bytes 1769476
  109.9 0.9 copy-start.2
  125.4 25.5 %all-to-all-start.3 = ((bf16[64,24,128]{2,1,0:T(8,128)(2,1)}), bf16[64,24,128]{2,1,0:T(8,128)(2,1)S(1)}, u32[]{:S(2)}, u32[]{:S(2)}) async-start(bf16[64,24,128]{2,1,0:T(8,128)(2,1)} %bitcast.22), calls=%async_computation.3 | async-start | bytes 786432 | tf_op jit(solution)/shard_map/all_to_all | solution.py:23
  136.2 5.6 %collective-permute-start.3 = (bf16[192,768]{1,0:T(8,128)(2,1)}, bf16[192,768]{1,0:T(8,128)(2,1)S(1)}, u32[]{:S(2)}, u32[]{:S(2)}) collective-permute-start(bf16[192,768]{1,0:T(8,128)(2,1)} %get-tuple-element.21), channel_id=1, source_target_pairs={{0,8},{8,0},{1,9},{9,1},{2,10},{10,2},{3,11},{11,3},{4,12},{12,4},... | collective-permute-start | bytes 884744 | tf_op jit(solution)/shard_map/ppermute | solution.py:19
  138.1 12.8 %copy-start.1 = (s32[4,4]{1,0:T(4,128)S(1)}, s32[4,4]{1,0:T(4,128)}, u32[]{:S(2)}) copy-start(s32[4,4]{1,0:T(4,128)} %ids_ref.3) | copy-start | bytes 196
  138.2 3.6 %collective-permute-start.4 = (bf16[192,384]{1,0:T(8,128)(2,1)}, bf16[192,384]{1,0:T(8,128)(2,1)S(1)}, u32[]{:S(2)}, u32[]{:S(2)}) collective-permute-start(bf16[192,384]{1,0:T(8,128)(2,1)} %get-tuple-element.22), channel_id=1, source_target_pairs={{0,8},{8,0},{1,9},{9,1},{2,10},{10,2},{3,11},{11,3},{4,12},{12,4},... | collective-permute-start | bytes 442376 | tf_op jit(solution)/shard_map/ppermute | solution.py:19
  141.8 0.7 copy-start.9
  142.4 0.7 copy-start.8

commit v5 on v4

--- a/solution.py
+++ b/solution.py
@@ -182,7 +182,7 @@
 
 
 def scatter_kernel(
-    parties, size, offset, after_ref, full_ref, own_ref, oth_ref, out_ref, dh_ref, act_ref, dh, own, oth, wide, out, sems
+    parties, size, offset, after_ref, full_ref, own_ref, oth_ref, out_ref, dh_ref, act_ref, dh, act, own, oth, wide, out, sems
 ):
     del after_ref
     width = own.shape[0]
@@ -194,8 +194,7 @@
             (own_ref.at[0:width, :], own),
             (full_ref.at[:, offset : offset + hidden], dh.at[1]),
             (oth_ref, oth),
-            (full_ref.at[:, offset : offset + hidden], dh_ref),
-            (full_ref.at[:, offset + hidden : 2 * offset], act_ref),
+            (full_ref.at[:, offset + hidden : 2 * offset], act),
         ],
         sems,
     )
@@ -203,13 +202,15 @@
     wait_all(copies[0:2])
     dx = dot(dh[0], own[...], ((1,), (1,)))
     wait_all(copies[2:4])
+    copies[4].wait()
+    outs = start_all([(dh.at[1], dh_ref), (act, act_ref)], sems, 5)
     dx = dx + dot(dh[1], oth[...], ((1,), (1,)))
     for j in range(CAP):
         for k in range(tiles):
             value = dx[j * parties : (j + 1) * parties, k * LANE : (k + 1) * LANE]
             wide[pl.ds(j * tiles + k, parties, stride=size), :] = value
     out[...] = wide[...].astype(BF16)
-    wait_all(copies[4:] + start_all([(out, out_ref)], sems, 6))
+    wait_all(outs + start_all([(out, out_ref)], sems, 7))
 
 
 def grads_kernel(step, *refs):
@@ -328,10 +329,10 @@
     size = up(CAP * width // LANE, 8)
     flat = array((parties * size, LANE))
     shapes = (flat, array((rows, hidden)), array((rows, height - width)))
-    scratch = [((2, rows, hidden), BF16), (oth.shape, BF16), (oth.shape, BF16), (flat.shape, F32), (flat.shape, BF16)]
+    scratch = [((2, rows, hidden), BF16)] + like(shapes[2], oth, oth) + [(flat.shape, F32), (flat.shape, BF16)]
     kernel = functools.partial(scatter_kernel, parties, size, height)
     flops, moved = 4 * rows * width * hidden, 4 * own.size
-    out, dh, act = call(kernel, shapes, scratch, 7, flops, moved, after, full, own, oth)
+    out, dh, act = call(kernel, shapes, scratch, 8, flops, moved, after, full, own, oth)
     return out.reshape(parties, size, LANE), dh, act
 
 

time: 153 us -> 142 us (0.928)
  Pallas kernels: 30.7 us -> 19.7 us
    pallas_call x7, Pallas kernels: 30.7 us -> 19.7 us  [call(): pl.pallas_call(kernel, out_shape=outs, in_specs=[SMEM if a.shape == (1,)...]
  transfers between devices with their start and end apart: 9 -> 9, of which waited for: 7 -> 7; matrix products, arithmetic and copies ran while one was open for 0% -> 0% of each run, Pallas kernels for 5% -> 6%
where the time goes in v5:
time: 142 us; the launch traced here: 141 us
  starting transfers between devices  59.2 us (42%)
  waiting for transfers between devices  58.3 us (41%)
  Pallas kernels  19.7 us (14%)
  local copies, waits for them, and re-layouts  3.11 us (2%)
    all_to_all x4, waiting for transfers between devices, exchange(): return lax.all_to_all(x, axes, split_axis=0, concat_axis=0, tiled=True)  53.3 us
    all_to_all x4, starting transfers between devices, exchange(): return lax.all_to_all(x, axes, split_axis=0, concat_axis=0, tiled=True)  48.7 us
    pallas_call x7, Pallas kernels, call(): pl.pallas_call(kernel, out_shape=outs, in_specs=[SMEM if a.shape == (1,)...  19.7 us
    ppermute x5, starting transfers between devices, swap(): return lax.ppermute(x, 'core', [(0, 1), (1, 0)])  10.6 us
    ppermute x5, waiting for transfers between devices, swap(): return lax.ppermute(x, 'core', [(0, 1), (1, 0)])  4.99 us
    unnamed x20, local copies, waits for them, and re-layouts  3.11 us
  transfers between devices with their start and end apart: 9, of which 7 were waited for; matrix products, arithmetic and copies ran while one was open for 0% of the time, Pallas kernels for 6%

profile of v5, /device:TPU:4, one launch (start us, length us, event | category | flops | bytes accessed | tf_op | source)
XLA Modules:
  0.0 141.1 jit_solution(9669241941617793992)
XLA Ops:
  0.6 1.9 %shard_map.103 = bf16[8,8,40,128]{3,2,1,0:T(8,128)(2,1)} custom-call(s32[4,4]{1,0:T(4,128)} %ids_ref.3, bf16[4,4]{1,0:T(4,128)(2,1)} %gates_ref.1, bf16[4,768]{1,0:T(4,128)(2,1)} %tok_ref.1, bf16[4,768]{1,0:T(4,128)(2,1)} %cot_ref.1), custom_call_target="tpu_custom_call" | custom-call | flops 1048576 | bytes 1048576 | tf_op jit(solution)/shard_map/pallas_call | solution.py:271
  2.5 17.3 %all-to-all-start = ((bf16[64,40,128]{2,1,0:T(8,128)(2,1)}), bf16[64,40,128]{2,1,0:T(8,128)(2,1)S(1)}, u32[]{:S(2)}, u32[]{:S(2)}) async-start(bf16[64,40,128]{2,1,0:T(8,128)(2,1)} %bitcast.14), calls=%async_computation | async-start | bytes 1310720 | tf_op jit(solution)/shard_map/all_to_all | solution.py:23
  19.9 3.7 %shard_map.104 = (bf16[1152,768]{1,0:T(8,128)(2,1)}, bf16[768,768]{1,0:T(8,128)(2,1)}, bf16[384,768]{1,0:T(8,128)(2,1)}) custom-call(bf16[64,40,128]{2,1,0:T(8,128)(2,1)} %bitcast.15, bf16[768,768]{1,0:T(8,128)(2,1)} %bitcast.16, bf16[1,768]{1,0:T(2,128)(2,1)} %refs_6_.1, bf16[384,768]{1,0:T(8,128)(2,1)} %bitcast.19, bf16[1,768]{1,0:T(2,128)(2,1)} %refs_8_.1), custom_call_target="tpu_custom_call" | custom-call | flops 3538944 | bytes 3538944 | tf_op jit(solution)/shard_map/pallas_call | solution.py:271
  23.6 1.9 %collective-permute-start = (bf16[768,768]{1,0:T(8,128)(2,1)}, bf16[768,768]{1,0:T(8,128)(2,1)S(1)}, u32[]{:S(2)}, u32[]{:S(2)}) collective-permute-start(bf16[768,768]{1,0:T(8,128)(2,1)} %get-tuple-element.15), channel_id=1, source_target_pairs={{0,8},{8,0},{1,9},{9,1},{2,10},{10,2},{3,11},{11,3},{4,12},{12,4},... | collective-permute-start | bytes 3538952 | tf_op jit(solution)/shard_map/ppermute | solution.py:19
  25.5 2.4 %collective-permute-start.1 = (bf16[384,768]{1,0:T(8,128)(2,1)}, bf16[384,768]{1,0:T(8,128)(2,1)S(1)}, u32[]{:S(2)}, u32[]{:S(2)}) collective-permute-start(bf16[384,768]{1,0:T(8,128)(2,1)} %get-tuple-element.16), channel_id=1, source_target_pairs={{0,8},{8,0},{1,9},{9,1},{2,10},{10,2},{3,11},{11,3},{4,12},{12,4},... | collective-permute-start | bytes 1769480 | tf_op jit(solution)/shard_map/ppermute | solution.py:19
  27.9 1.8 %collective-permute-done.1.oth_out_ref = bf16[384,768]{1,0:T(8,128)(2,1)S(1)} collective-permute-done((bf16[384,768]{1,0:T(8,128)(2,1)}, bf16[384,768]{1,0:T(8,128)(2,1)S(1)}, u32[]{:S(2)}, u32[]{:S(2)}) %collective-permute-start.1) | collective-permute-done | bytes 589856 | tf_op jit(solution)/shard_map/ppermute | solution.py:19
  29.7 0.0 copy-start.7
  29.7 0.0 collective-permute-done.oth_in_ref.oth_ref
  29.7 0.0 copy-start.3
  29.7 8.6 %all-to-all-done = bf16[64,40,128]{2,1,0:T(8,128)(2,1)S(1)} async-done(((bf16[64,40,128]{2,1,0:T(8,128)(2,1)}), bf16[64,40,128]{2,1,0:T(8,128)(2,1)S(1)}, u32[]{:S(2)}, u32[]{:S(2)}) %all-to-all-start) | async-done | bytes 655392 | tf_op jit(solution)/shard_map/all_to_all | solution.py:23
  38.3 0.0 copy-start.4
  38.3 0.0 copy-done.7
  38.3 0.0 copy-done.3
  38.3 0.8 copy-done.4
  39.2 3.9 %shard_map.105 = (bf16[192,2304]{1,0:T(8,128)(2,1)}, bf16[192,1536]{1,0:T(8,128)(2,1)}, f32[192,128]{1,0:T(8,128)}) custom-call(bf16[2560,128]{1,0:T(8,128)(2,1)} %bitcast.18, bf16[1152,768]{1,0:T(8,128)(2,1)} %get-tuple-element.14.own_ref, bf16[768,768]{1,0:T(8,128)(2,1)} %copy-done.3, bf16[384,768]{1,0:T(8,128)(2,1)} %copy-done.7), custom_call_target="tpu_custom_call" | custom-call | flops 679477248 | bytes 5505024 | tf_op jit(solution)/shard_map/pallas_call | solution.py:271
  43.0 0.0 copy-start
  43.0 16.8 %all-to-all-start.1 = ((bf16[8,24,2304]{2,1,0:T(8,128)(2,1)}), bf16[8,24,2304]{2,1,0:T(8,128)(2,1)S(1)}, u32[]{:S(2)}, u32[]{:S(2)}) async-start(bf16[8,24,2304]{2,1,0:T(8,128)(2,1)} %bitcast.21), calls=%async_computation.1 | async-start | bytes 1769472 | tf_op jit(solution)/shard_map/all_to_all | solution.py:23
  59.8 22.7 %all-to-all-done.1.parts_ref = bf16[8,24,2304]{2,1,0:T(8,128)(2,1)S(1)} async-done(((bf16[8,24,2304]{2,1,0:T(8,128)(2,1)}), bf16[8,24,2304]{2,1,0:T(8,128)(2,1)S(1)}, u32[]{:S(2)}, u32[]{:S(2)}) %all-to-all-start.1) | async-done | bytes 884768 | tf_op jit(solution)/shard_map/all_to_all | solution.py:23
  82.5 0.0 copy-done
  82.5 1.3 shard_map.106
  83.8 0.0 copy-start.6
  83.8 3.7 %all-to-all-start.2 = ((bf16[8,24,2304]{2,1,0:T(8,128)(2,1)}), bf16[8,24,2304]{2,1,0:T(8,128)(2,1)S(1)}, u32[]{:S(2)}, u32[]{:S(2)}) async-start(bf16[8,24,2304]{2,1,0:T(8,128)(2,1)} %shard_map.106), calls=%async_computation.2 | async-start | bytes 1769472 | tf_op jit(solution)/shard_map/all_to_all | solution.py:23
  87.5 0.0 copy-done.6
  87.5 1.9 %collective-permute-start.2 = (bf16[192,1536]{1,0:T(8,128)(2,1)S(1)}, bf16[192,1536]{1,0:T(8,128)(2,1)S(1)}, u32[]{:S(2)}, u32[]{:S(2)}) collective-permute-start(bf16[192,1536]{1,0:T(8,128)(2,1)S(1)} %copy-done.6), channel_id=1, source_target_pairs={{0,8},{8,0},{1,9},{9,1},{2,10},{10,2},{3,11},{11,3},{4,12},{12,4},... | collective-permute-start | bytes 1769480 | tf_op jit(solution)/shard_map/ppermute | solution.py:19
  89.5 2.0 %collective-permute-done.2.after_ref.refs_1_ = bf16[192,1536]{1,0:T(8,128)(2,1)S(1)} collective-permute-done((bf16[192,1536]{1,0:T(8,128)(2,1)S(1)}, bf16[192,1536]{1,0:T(8,128)(2,1)S(1)}, u32[]{:S(2)}, u32[]{:S(2)}) %collective-permute-start.2) | collective-permute-done | bytes 589856 | tf_op jit(solution)/shard_map/ppermute | solution.py:19
  91.4 0.0 copy-start.5
  91.4 18.5 %all-to-all-done.2 = bf16[8,24,2304]{2,1,0:T(8,128)(2,1)S(1)} async-done(((bf16[8,24,2304]{2,1,0:T(8,128)(2,1)}), bf16[8,24,2304]{2,1,0:T(8,128)(2,1)S(1)}, u32[]{:S(2)}, u32[]{:S(2)}) %all-to-all-start.2) | async-done | bytes 884768 | tf_op jit(solution)/shard_map/all_to_all | solution.py:23
  109.9 0.0 copy-start.2
  109.9 0.0 copy-done.5
  109.9 0.9 copy-done.2
  110.8 3.6 %shard_map.107 = (bf16[1536,128]{1,0:T(8,128)(2,1)}, bf16[192,768]{1,0:T(8,128)(2,1)}, bf16[192,384]{1,0:T(8,128)(2,1)}) custom-call(bf16[192,1536]{1,0:T(8,128)(2,1)} %copy-done.5, bf16[192,2304]{1,0:T(8,128)(2,1)} %bitcast.12, bf16[1152,768]{1,0:T(8,128)(2,1)} %get-tuple-element.14.own_ref, bf16[768,768]{1,0:T(8,128)(2,1)} %copy-done.3), custom_call_target="tpu_custom_call" | custom-call | flops 452984832 | bytes 3538944 | tf_op jit(solution)/shard_map/pallas_call | solution.py:271
  114.4 10.8 %all-to-all-start.3 = ((bf16[64,24,128]{2,1,0:T(8,128)(2,1)}), bf16[64,24,128]{2,1,0:T(8,128)(2,1)S(1)}, u32[]{:S(2)}, u32[]{:S(2)}) async-start(bf16[64,24,128]{2,1,0:T(8,128)(2,1)} %bitcast.22), calls=%async_computation.3 | async-start | bytes 786432 | tf_op jit(solution)/shard_map/all_to_all | solution.py:23
  125.2 1.9 %collective-permute-start.3 = (bf16[192,768]{1,0:T(8,128)(2,1)}, bf16[192,768]{1,0:T(8,128)(2,1)S(1)}, u32[]{:S(2)}, u32[]{:S(2)}) collective-permute-start(bf16[192,768]{1,0:T(8,128)(2,1)} %get-tuple-element.21), channel_id=1, source_target_pairs={{0,8},{8,0},{1,9},{9,1},{2,10},{10,2},{3,11},{11,3},{4,12},{12,4},... | collective-permute-start | bytes 884744 | tf_op jit(solution)/shard_map/ppermute | solution.py:19
  127.2 0.0 copy-start.1
  127.2 2.4 %collective-permute-start.4 = (bf16[192,384]{1,0:T(8,128)(2,1)}, bf16[192,384]{1,0:T(8,128)(2,1)S(1)}, u32[]{:S(2)}, u32[]{:S(2)}) collective-permute-start(bf16[192,384]{1,0:T(8,128)(2,1)} %get-tuple-element.22), channel_id=1, source_target_pairs={{0,8},{8,0},{1,9},{9,1},{2,10},{10,2},{3,11},{11,3},{4,12},{12,4},... | collective-permute-start | bytes 442376 | tf_op jit(solution)/shard_map/ppermute | solution.py:19
  129.6 1.2 collective-permute-done.4.refs_4_
  130.8 0.0 copy-start.9
  130.8 0.0 collective-permute-done.3.refs_3_
  130.8 0.6 copy-done.9
  131.4 0.0 copy-start.8
  131.4 0.7 copy-done.8
  132.2 4.2 %shard_map.109 = (bf16[768,768]{1,0:T(8,128)(2,1)}, bf16[384,768]{1,0:T(8,128)(2,1)}) custom-call(bf16[192,1536]{1,0:T(8,128)(2,1)} %get-tuple-element.17.refs_0_, bf16[192,1536]{1,0:T(8,128)(2,1)} %copy-done.5, bf16[192,2304]{1,0:T(8,128)(2,1)} %bitcast.13, bf16[192,768]{1,0:T(8,128)(2,1)} %copy-done.8, bf16[192,384]{1,0:T(8,128)(2,1)} %copy-done.9, ...), custom_call_target="tpu_custom_call" | custom-call | flops 1048576 | bytes 1048576 | tf_op jit(solution)/shard_map/pallas_call | solution.py:271
  136.4 3.6 %all-to-all-done.3 = bf16[64,24,128]{2,1,0:T(8,128)(2,1)S(1)} async-done(((bf16[64,24,128]{2,1,0:T(8,128)(2,1)}), bf16[64,24,128]{2,1,0:T(8,128)(2,1)S(1)}, u32[]{:S(2)}, u32[]{:S(2)}) %all-to-all-start.3) | async-done | bytes 393248 | tf_op jit(solution)/shard_map/all_to_all | solution.py:23
  139.9 0.0 copy-done.1
  139.9 1.2 shard_map.108
Async XLA Ops:
  2.5 35.8 %all-to-all-start = ((bf16[64,40,128]{2,1,0:T(8,128)(2,1)}), bf16[64,40,128]{2,1,0:T(8,128)(2,1)S(1)}, u32[]{:S(2)}, u32[]{:S(2)}) async-start(bf16[64,40,128]{2,1,0:T(8,128)(2,1)} %bitcast.14), calls=%async_computation | async-start | bytes 1310720 | tf_op jit(solution)/shard_map/all_to_all | solution.py:23
  23.6 6.2 %collective-permute-start = (bf16[768,768]{1,0:T(8,128)(2,1)}, bf16[768,768]{1,0:T(8,128)(2,1)S(1)}, u32[]{:S(2)}, u32[]{:S(2)}) collective-permute-start(bf16[768,768]{1,0:T(8,128)(2,1)} %get-tuple-element.15), channel_id=1, source_target_pairs={{0,8},{8,0},{1,9},{9,1},{2,10},{10,2},{3,11},{11,3},{4,12},{12,4},... | collective-permute-start | bytes 3538952 | tf_op jit(solution)/shard_map/ppermute | solution.py:19
  25.5 4.2 %collective-permute-start.1 = (bf16[384,768]{1,0:T(8,128)(2,1)}, bf16[384,768]{1,0:T(8,128)(2,1)S(1)}, u32[]{:S(2)}, u32[]{:S(2)}) collective-permute-start(bf16[384,768]{1,0:T(8,128)(2,1)} %get-tuple-element.16), channel_id=1, source_target_pairs={{0,8},{8,0},{1,9},{9,1},{2,10},{10,2},{3,11},{11,3},{4,12},{12,4},... | collective-permute-start | bytes 1769480 | tf_op jit(solution)/shard_map/ppermute | solution.py:19
  29.7 8.6 %copy-start.7 = (bf16[384,768]{1,0:T(8,128)(2,1)}, bf16[384,768]{1,0:T(8,128)(2,1)S(1)}, u32[]{:S(2)}) copy-start(bf16[384,768]{1,0:T(8,128)(2,1)S(1)} %collective-permute-done.1.oth_out_ref) | copy-start | bytes 1769476
  29.7 8.6 %copy-start.3 = (bf16[768,768]{1,0:T(8,128)(2,1)}, bf16[768,768]{1,0:T(8,128)(2,1)S(1)}, u32[]{:S(2)}) copy-start(bf16[768,768]{1,0:T(8,128)(2,1)S(1)} %collective-permute-done.oth_in_ref.oth_ref) | copy-start | bytes 3538948
  38.3 0.8 copy-start.4
  43.0 39.5 %copy-start = (f32[192,128]{1,0:T(8,128)S(1)}, f32[192,128]{1,0:T(8,128)}, u32[]{:S(2)}) copy-start(f32[192,128]{1,0:T(8,128)} %get-tuple-element.19.gate_ref) | copy-start | bytes 294916
  43.0 39.5 %all-to-all-start.1 = ((bf16[8,24,2304]{2,1,0:T(8,128)(2,1)}), bf16[8,24,2304]{2,1,0:T(8,128)(2,1)S(1)}, u32[]{:S(2)}, u32[]{:S(2)}) async-start(bf16[8,24,2304]{2,1,0:T(8,128)(2,1)} %bitcast.21), calls=%async_computation.1 | async-start | bytes 1769472 | tf_op jit(solution)/shard_map/all_to_all | solution.py:23
  83.8 3.7 %copy-start.6 = (bf16[192,1536]{1,0:T(8,128)(2,1)S(1)}, bf16[192,1536]{1,0:T(8,128)(2,1)}, u32[]{:S(2)}) copy-start(bf16[192,1536]{1,0:T(8,128)(2,1)} %get-tuple-element.17.refs_0_) | copy-start | bytes 1769476
  83.8 26.1 %all-to-all-start.2 = ((bf16[8,24,2304]{2,1,0:T(8,128)(2,1)}), bf16[8,24,2304]{2,1,0:T(8,128)(2,1)S(1)}, u32[]{:S(2)}, u32[]{:S(2)}) async-start(bf16[8,24,2304]{2,1,0:T(8,128)(2,1)} %shard_map.106), calls=%async_computation.2 | async-start | bytes 1769472 | tf_op jit(solution)/shard_map/all_to_all | solution.py:23
  87.5 3.9 %collective-permute-start.2 = (bf16[192,1536]{1,0:T(8,128)(2,1)S(1)}, bf16[192,1536]{1,0:T(8,128)(2,1)S(1)}, u32[]{:S(2)}, u32[]{:S(2)}) collective-permute-start(bf16[192,1536]{1,0:T(8,128)(2,1)S(1)} %copy-done.6), channel_id=1, source_target_pairs={{0,8},{8,0},{1,9},{9,1},{2,10},{10,2},{3,11},{11,3},{4,12},{12,4},... | collective-permute-start | bytes 1769480 | tf_op jit(solution)/shard_map/ppermute | solution.py:19
  91.4 18.5 %copy-start.5 = (bf16[192,1536]{1,0:T(8,128)(2,1)}, bf16[192,1536]{1,0:T(8,128)(2,1)S(1)}, u32[]{:S(2)}) copy-start(bf16[192,1536]{1,0:T(8,128)(2,1)S(1)} %collective-permute-done.2.after_ref.refs_1_) | copy-start | bytes 1769476
  109.9 0.9 copy-start.2
  114.4 25.5 %all-to-all-start.3 = ((bf16[64,24,128]{2,1,0:T(8,128)(2,1)}), bf16[64,24,128]{2,1,0:T(8,128)(2,1)S(1)}, u32[]{:S(2)}, u32[]{:S(2)}) async-start(bf16[64,24,128]{2,1,0:T(8,128)(2,1)} %bitcast.22), calls=%async_computation.3 | async-start | bytes 786432 | tf_op jit(solution)/shard_map/all_to_all | solution.py:23
  125.2 5.6 %collective-permute-start.3 = (bf16[192,768]{1,0:T(8,128)(2,1)}, bf16[192,768]{1,0:T(8,128)(2,1)S(1)}, u32[]{:S(2)}, u32[]{:S(2)}) collective-permute-start(bf16[192,768]{1,0:T(8,128)(2,1)} %get-tuple-element.21), channel_id=1, source_target_pairs={{0,8},{8,0},{1,9},{9,1},{2,10},{10,2},{3,11},{11,3},{4,12},{12,4},... | collective-permute-start | bytes 884744 | tf_op jit(solution)/shard_map/ppermute | solution.py:19
  127.2 12.8 %copy-start.1 = (s32[4,4]{1,0:T(4,128)S(1)}, s32[4,4]{1,0:T(4,128)}, u32[]{:S(2)}) copy-start(s32[4,4]{1,0:T(4,128)} %ids_ref.3) | copy-start | bytes 196
  127.2 3.6 %collective-permute-start.4 = (bf16[192,384]{1,0:T(8,128)(2,1)}, bf16[192,384]{1,0:T(8,128)(2,1)S(1)}, u32[]{:S(2)}, u32[]{:S(2)}) collective-permute-start(bf16[192,384]{1,0:T(8,128)(2,1)} %get-tuple-element.22), channel_id=1, source_target_pairs={{0,8},{8,0},{1,9},{9,1},{2,10},{10,2},{3,11},{11,3},{4,12},{12,4},... | collective-permute-start | bytes 442376 | tf_op jit(solution)/shard_map/ppermute | solution.py:19
  130.8 0.7 copy-start.9
  131.4 0.7 copy-start.8

commit v6 on v5

--- a/solution.py
+++ b/solution.py
@@ -90,23 +90,13 @@
 
 
 def gather_kernel(
-    parties, size, got_ref, own_ref, oth_in_ref, oth_out_ref, part_ref, rows_ref, gate_ref,
-    got, wide, own, oth, rows, part, gate, sems,
+    parties, size, got, own, oth_in, oth_out, part_ref, rows_ref, gate_ref, keep_ref, wide, rows, part, gate, sems
 ):
     width = own.shape[1]
     units = own.shape[0] - width
     tiles = width // LANE
     half = width + units
-    copies = start_all(
-        [
-            (got_ref, got),
-            (own_ref, own),
-            (oth_in_ref, oth.at[0:width, :]),
-            (oth_out_ref, oth.at[width:half, :]),
-        ],
-        sems,
-    )
-    copies[0].wait()
+    outs = start_all([(oth_in, keep_ref)], sems)
     wide[...] = got[...].astype(F32)
     gates = wide[pl.ds(2 * tiles * CAP, parties, stride=size), :]
     for j in range(CAP):
@@ -115,15 +105,14 @@
         for k in range(2 * tiles):
             value = wide[pl.ds(j * 2 * tiles + k, parties, stride=size), :]
             rows[at, k * LANE : (k + 1) * LANE] = value.astype(BF16)
-    outs = start_all([(rows, rows_ref), (gate, gate_ref)], sems, 4)
-    for n, weights in enumerate((own, oth)):
-        wait_all(copies[n + 1 : 2 + 2 * n])
-        pre = dot(rows[:, :width], weights[:width, :], ((1,), (0,)))
+    outs += start_all([(rows, rows_ref), (gate, gate_ref)], sems, 1)
+    for n, (w_in, w_out) in enumerate(((own.at[:width, :], own.at[width:, :]), (oth_in, oth_out))):
+        pre = dot(rows[:, :width], w_in[...], ((1,), (0,)))
         part[:, n * half : n * half + width] = pre.astype(BF16)
-        back = dot(rows[:, width:], weights[width:, :], ((1,), (1,)))
+        back = dot(rows[:, width:], w_out[...], ((1,), (1,)))
         part[:, n * half + width : (n + 1) * half] = back.astype(BF16)
         cols = slice(n * half, (n + 1) * half)
-        outs += start_all([(part.at[:, cols], part_ref.at[:, cols])], sems, 6 + n)
+        outs += start_all([(part.at[:, cols], part_ref.at[:, cols])], sems, 3 + n)
     wait_all(outs)
 
 
@@ -191,7 +180,7 @@
     copies = start_all(
         [
             (full_ref.at[:, 0:hidden], dh.at[0]),
-            (own_ref.at[0:width, :], own),
+            (own_ref, own),
             (full_ref.at[:, offset : offset + hidden], dh.at[1]),
             (oth_ref, oth),
             (full_ref.at[:, offset + hidden : 2 * offset], act),
@@ -260,6 +249,7 @@
 
 
 ANY = pl.BlockSpec(memory_space=pl.ANY)
+VM = pl.BlockSpec(memory_space=pltpu.VMEM)
 SMEM = pl.BlockSpec(memory_space=pltpu.SMEM)
 
 
@@ -267,11 +257,11 @@
     return jax.ShapeDtypeStruct(shape, dtype)
 
 
-def call(kernel, outs, scratch, n_sems, flops, moved, *args, limit=FULL):
+def call(kernel, outs, scratch, n_sems, flops, moved, *args, limit=FULL, spec=ANY):
     return pl.pallas_call(
         kernel,
         out_shape=outs,
-        in_specs=[SMEM if a.shape == (1,) else ANY for a in args],
+        in_specs=[SMEM if a.shape == (1,) else spec for a in args],
         out_specs=jax.tree.map(lambda _: ANY, outs),
         scratch_shapes=[pltpu.VMEM(*s) for s in scratch] + [pltpu.SemaphoreType.DMA((n_sems,))],
         compiler_params=pltpu.CompilerParams(vmem_limit_bytes=limit),
@@ -299,7 +289,7 @@
     scratch = like(*args) + [((heights[0], width), BF16)]
     size = heights[0] * width
     kernel = functools.partial(clip_kernel, 64)
-    return call(kernel, tuple(array((h, width)) for h in heights), scratch, 7, 4 * size, 4 * size, after, *args)
+    return call(kernel, tuple(array((h, width)) for h in heights), scratch, 7, 4 * size, 4 * size, after, *args, limit=ROOMY)
 
 
 def activate(z, parts, gate_rows, units):
@@ -315,24 +305,24 @@
     height, width = own.shape
     rows = parties * CAP
     flat = got.reshape(parties * size, LANE)
-    shapes = (array((rows, 2 * height)), array((rows, 2 * width)), array((rows, LANE), F32))
-    scratch = like(flat) + [(flat.shape, F32)] + like(own, own, shapes[1], shapes[0], shapes[2])
+    shapes = (array((rows, 2 * height)), array((rows, 2 * width)), array((rows, LANE), F32), array(oth_in.shape))
+    scratch = [(flat.shape, F32)] + like(shapes[1], shapes[0], shapes[2])
     kernel = functools.partial(gather_kernel, parties, size)
-    moved = 4 * own.size + 6 * got.size
-    return call(kernel, shapes, scratch, 6 + CORES, 4 * rows * own.size, moved, flat, own, oth_in, oth_out)
+    flops, moved = 4 * rows * own.size, 4 * own.size + 6 * got.size
+    return call(kernel, shapes, scratch, 3 + CORES, flops, moved, flat, own, oth_in, oth_out, limit=ROOMY, spec=VM)
 
 
 def scatter(after, full, own, oth, parties):
     rows = full.shape[0]
-    height, width = own.shape
-    hidden = width
+    width, hidden = own.shape
+    height = full.shape[1] // CORES
     size = up(CAP * width // LANE, 8)
     flat = array((parties * size, LANE))
-    shapes = (flat, array((rows, hidden)), array((rows, height - width)))
+    shapes = (flat, array((rows, hidden)), array((rows, height - hidden)))
     scratch = [((2, rows, hidden), BF16)] + like(shapes[2], oth, oth) + [(flat.shape, F32), (flat.shape, BF16)]
     kernel = functools.partial(scatter_kernel, parties, size, height)
     flops, moved = 4 * rows * width * hidden, 4 * own.size
-    out, dh, act = call(kernel, shapes, scratch, 8, flops, moved, after, full, own, oth)
+    out, dh, act = call(kernel, shapes, scratch, 8, flops, moved, after, full, own, oth, limit=ROOMY)
     return out.reshape(parties, size, LANE), dh, act
 
 
@@ -372,14 +362,14 @@
     own, own_in, own_out = clip_weights(messages, w_in, scale_in, w_out, scale_out)
     oth_in, oth_out = swap(own_in), swap(own_out)
 
-    part, xdy, gate_rows = gather(got, own, oth_in, oth_out)
+    part, xdy, gate_rows, keep_in = gather(got, own, oth_in, oth_out)
     parts = exchange(part.reshape(n_dp, share, 3 * hidden), "dp")
     z = lax.axis_index("dp").astype(jnp.int32).reshape(1)
     copies = activate(z, parts, gate_rows, units)
     full = exchange(copies, "dp").reshape(rows, 3 * hidden)
 
     xdy_r = swap(xdy)
-    returns, dh_oth, act_oth = scatter(xdy_r, full, own, oth_in, parties)
+    returns, dh_oth, act_oth = scatter(xdy_r, full, own_in, keep_in, parties)
     back = exchange(returns, ("expert", "y"))
     grad_tokens = combine(expert_ids, back, tok_rows, width, n_expert, n_y)
 

time: 142 us -> 142 us (level)
  local copies, waits for them, and re-layouts: 3.11 us -> 8.78 us
  Pallas kernels: 19.7 us -> 15.6 us
    unnamed x20 -> x34, local copies, waits for them, and re-layouts: 3.11 us -> 8.78 us
    pallas_call x7, Pallas kernels: 19.7 us -> 15.6 us  [call(): pl.pallas_call(kernel, out_shape=outs, in_specs=[SMEM if a.shape == (1,)...]
  transfers between devices with their start and end apart: 9 -> 9, of which waited for: 7 -> 7; matrix products, arithmetic and copies ran while one was open for 0% -> 0% of each run, Pallas kernels for 6% -> 4%
where the time goes in v6:
time: 142 us
  starting transfers between devices  59.2 us (42%)
  waiting for transfers between devices  57.1 us (40%)
  Pallas kernels  15.6 us (11%)
  local copies, waits for them, and re-layouts  8.78 us (6%)
    all_to_all x4, waiting for transfers between devices, exchange(): return lax.all_to_all(x, axes, split_axis=0, concat_axis=0, tiled=True)  52.6 us
    all_to_all x4, starting transfers between devices, exchange(): return lax.all_to_all(x, axes, split_axis=0, concat_axis=0, tiled=True)  48.6 us
    pallas_call x7, Pallas kernels, call(): pl.pallas_call(kernel, out_shape=outs, in_specs=[SMEM if a.shape == (1,)...  15.6 us
    ppermute x5, starting transfers between devices, swap(): return lax.ppermute(x, 'core', [(0, 1), (1, 0)])  10.5 us
    unnamed x34, local copies, waits for them, and re-layouts  8.78 us
    ppermute x5, waiting for transfers between devices, swap(): return lax.ppermute(x, 'core', [(0, 1), (1, 0)])  4.57 us
  transfers between devices with their start and end apart: 9, of which 7 were waited for; matrix products, arithmetic and copies ran while one was open for 0% of the time, Pallas kernels for 4%

profile of v6, /device:TPU:4, one launch (start us, length us, event | category | flops | bytes accessed | tf_op | source)
XLA Modules:
  0.0 141.6 jit_solution(18264172412980560334)
XLA Ops:
  0.6 0.0 copy-start.2
  0.6 0.0 copy-start.12
  0.7 0.0 copy-start.13
  0.7 2.0 %shard_map.103 = bf16[8,8,40,128]{3,2,1,0:T(8,128)(2,1)} custom-call(s32[4,4]{1,0:T(4,128)} %ids_ref.3, bf16[4,4]{1,0:T(4,128)(2,1)} %gates_ref.1, bf16[4,768]{1,0:T(4,128)(2,1)} %tok_ref.1, bf16[4,768]{1,0:T(4,128)(2,1)} %cot_ref.1), custom_call_target="tpu_custom_call" | custom-call | flops 1048576 | bytes 1048576 | tf_op jit(solution)/shard_map/pallas_call | solution.py:261
  2.6 0.0 copy-start.1
  2.6 17.5 %all-to-all-start = ((bf16[64,40,128]{2,1,0:T(8,128)(2,1)}), bf16[64,40,128]{2,1,0:T(8,128)(2,1)S(1)}, u32[]{:S(2)}, u32[]{:S(2)}) async-start(bf16[64,40,128]{2,1,0:T(8,128)(2,1)} %bitcast.13), calls=%async_computation | async-start | bytes 1310720 | tf_op jit(solution)/shard_map/all_to_all | solution.py:23
  20.1 0.0 copy-done.2
  20.1 0.0 copy-done.12
  20.1 0.0 copy-done.13
  20.1 0.0 copy-done.1
  20.2 0.0 copy-start.3
  20.2 1.1 copy-done.3
  21.2 1.6 %shard_map.104 = (bf16[1152,768]{1,0:T(8,128)(2,1)S(1)}, bf16[768,768]{1,0:T(8,128)(2,1)S(1)}, bf16[384,768]{1,0:T(8,128)(2,1)S(1)}) custom-call(bf16[64,40,128]{2,1,0:T(8,128)(2,1)S(1)} %bitcast.14, bf16[768,768]{1,0:T(8,128)(2,1)S(1)} %bitcast.16, bf16[1,768]{1,0:T(2,128)(2,1)S(1)} %copy-done.12, bf16[384,768]{1,0:T(8,128)(2,1)S(1)} %bitcast.19, ...), custom_call_target="tpu_custom_call" | custom-call | flops 3538944 | bytes 3538944 | tf_op jit(solution)/shard_map/pallas_call | solution.py:261
  22.8 0.0 copy-start.5
  22.8 1.2 copy-done.5
  24.0 1.9 %collective-permute-start = (bf16[768,768]{1,0:T(8,128)(2,1)S(1)}, bf16[768,768]{1,0:T(8,128)(2,1)S(1)}, u32[]{:S(2)}, u32[]{:S(2)}) collective-permute-start(bf16[768,768]{1,0:T(8,128)(2,1)S(1)} %get-tuple-element.16.own_ref), channel_id=1, source_target_pairs={{0,8},{8,0},{1,9},{9,1},{2,10},{10,2},{3,11},{11,3},{4,12},{12,4},... | collective-permute-start | bytes 3538952 | tf_op jit(solution)/shard_map/ppermute | solution.py:19
  26.0 0.0 copy-start.7
  26.0 1.0 copy-done.7
  27.0 2.4 %collective-permute-start.1 = (bf16[384,768]{1,0:T(8,128)(2,1)S(1)}, bf16[384,768]{1,0:T(8,128)(2,1)S(1)}, u32[]{:S(2)}, u32[]{:S(2)}) collective-permute-start(bf16[384,768]{1,0:T(8,128)(2,1)S(1)} %get-tuple-element.17), channel_id=1, source_target_pairs={{0,8},{8,0},{1,9},{9,1},{2,10},{10,2},{3,11},{11,3},{4,12},{12,4},... | collective-permute-start | bytes 1769480 | tf_op jit(solution)/shard_map/ppermute | solution.py:19
  29.4 1.6 %collective-permute-done.1.oth_out = bf16[384,768]{1,0:T(8,128)(2,1)S(1)} collective-permute-done((bf16[384,768]{1,0:T(8,128)(2,1)S(1)}, bf16[384,768]{1,0:T(8,128)(2,1)S(1)}, u32[]{:S(2)}, u32[]{:S(2)}) %collective-permute-start.1) | collective-permute-done | bytes 589856 | tf_op jit(solution)/shard_map/ppermute | solution.py:19
  31.0 0.0 collective-permute-done.oth_in
  31.0 7.6 %all-to-all-done = bf16[64,40,128]{2,1,0:T(8,128)(2,1)S(1)} async-done(((bf16[64,40,128]{2,1,0:T(8,128)(2,1)}), bf16[64,40,128]{2,1,0:T(8,128)(2,1)S(1)}, u32[]{:S(2)}, u32[]{:S(2)}) %all-to-all-start) | async-done | bytes 655392 | tf_op jit(solution)/shard_map/all_to_all | solution.py:23
  38.6 1.5 %copy-done.6 = bf16[1152,768]{1,0:T(8,128)(2,1)S(1)} copy-done((bf16[1152,768]{1,0:T(8,128)(2,1)S(1)}, bf16[1152,768]{1,0:T(8,128)(2,1)}, u32[]{:S(2)}) %copy-start.6) | copy-done | bytes 1769496
  40.1 2.7 %shard_map.105 = (bf16[192,2304]{1,0:T(8,128)(2,1)}, bf16[192,1536]{1,0:T(8,128)(2,1)S(1)}, f32[192,128]{1,0:T(8,128)S(1)}, bf16[768,768]{1,0:T(8,128)(2,1)S(1)}) custom-call(bf16[2560,128]{1,0:T(8,128)(2,1)S(1)} %bitcast.17, bf16[1152,768]{1,0:T(8,128)(2,1)S(1)} %copy-done.6, bf16[768,768]{1,0:T(8,128)(2,1)S(1)} %collective-permute-done.oth_in, ...), custom_call_target="tpu_custom_call" | custom-call | flops 679477248 | bytes 5505024 | tf_op jit(solution)/shard_map/pallas_call | solution.py:261
  42.8 0.0 copy-start.9
  42.8 1.0 copy-done.9
  43.8 16.7 %all-to-all-start.1 = ((bf16[8,24,2304]{2,1,0:T(8,128)(2,1)}), bf16[8,24,2304]{2,1,0:T(8,128)(2,1)S(1)}, u32[]{:S(2)}, u32[]{:S(2)}) async-start(bf16[8,24,2304]{2,1,0:T(8,128)(2,1)} %bitcast.5), calls=%async_computation.1 | async-start | bytes 1769472 | tf_op jit(solution)/shard_map/all_to_all | solution.py:23
  60.5 22.7 %all-to-all-done.1.parts_ref = bf16[8,24,2304]{2,1,0:T(8,128)(2,1)S(1)} async-done(((bf16[8,24,2304]{2,1,0:T(8,128)(2,1)}), bf16[8,24,2304]{2,1,0:T(8,128)(2,1)S(1)}, u32[]{:S(2)}, u32[]{:S(2)}) %all-to-all-start.1) | async-done | bytes 884768 | tf_op jit(solution)/shard_map/all_to_all | solution.py:23
  83.2 1.3 shard_map.106
  84.5 0.0 copy-start.8
  84.5 3.7 %all-to-all-start.2 = ((bf16[8,24,2304]{2,1,0:T(8,128)(2,1)}), bf16[8,24,2304]{2,1,0:T(8,128)(2,1)S(1)}, u32[]{:S(2)}, u32[]{:S(2)}) async-start(bf16[8,24,2304]{2,1,0:T(8,128)(2,1)} %shard_map.106), calls=%async_computation.2 | async-start | bytes 1769472 | tf_op jit(solution)/shard_map/all_to_all | solution.py:23
  88.2 0.0 copy-done.11
  88.2 1.9 %collective-permute-start.2 = (bf16[192,1536]{1,0:T(8,128)(2,1)S(1)}, bf16[192,1536]{1,0:T(8,128)(2,1)S(1)}, u32[]{:S(2)}, u32[]{:S(2)}) collective-permute-start(bf16[192,1536]{1,0:T(8,128)(2,1)S(1)} %get-tuple-element.18.refs_0_), channel_id=1, source_target_pairs={{0,8},{8,0},{1,9},{9,1},{2,10},{10,2},{3,11},{11,3},{4,12},{12,4},... | collective-permute-start | bytes 1769480 | tf_op jit(solution)/shard_map/ppermute | solution.py:19
  90.1 2.0 %collective-permute-done.2.after_ref.refs_1_ = bf16[192,1536]{1,0:T(8,128)(2,1)S(1)} collective-permute-done((bf16[192,1536]{1,0:T(8,128)(2,1)S(1)}, bf16[192,1536]{1,0:T(8,128)(2,1)S(1)}, u32[]{:S(2)}, u32[]{:S(2)}) %collective-permute-start.2) | collective-permute-done | bytes 589856 | tf_op jit(solution)/shard_map/ppermute | solution.py:19
  92.1 18.5 %all-to-all-done.2 = bf16[8,24,2304]{2,1,0:T(8,128)(2,1)S(1)} async-done(((bf16[8,24,2304]{2,1,0:T(8,128)(2,1)}), bf16[8,24,2304]{2,1,0:T(8,128)(2,1)S(1)}, u32[]{:S(2)}, u32[]{:S(2)}) %all-to-all-start.2) | async-done | bytes 884768 | tf_op jit(solution)/shard_map/all_to_all | solution.py:23
  110.6 1.6 %copy-done.10 = bf16[768,768]{1,0:T(8,128)(2,1)S(1)} copy-done((bf16[768,768]{1,0:T(8,128)(2,1)S(1)}, bf16[768,768]{1,0:T(8,128)(2,1)}, u32[]{:S(2)}) %copy-start.10) | copy-done | bytes 1179672
  112.2 2.7 %shard_map.107 = (bf16[1536,128]{1,0:T(8,128)(2,1)}, bf16[192,768]{1,0:T(8,128)(2,1)S(1)}, bf16[192,384]{1,0:T(8,128)(2,1)S(1)}) custom-call(bf16[192,1536]{1,0:T(8,128)(2,1)S(1)} %collective-permute-done.2.after_ref.refs_1_, bf16[192,2304]{1,0:T(8,128)(2,1)S(1)} %bitcast.11, bf16[768,768]{1,0:T(8,128)(2,1)S(1)} %copy-done.8, bf16[768,768]{1,0:T(8,128)(2,1)S(1)} %copy-done.10), custom_call_target="tpu_custom_call" | custom-call | flops 452984832 | bytes 2359296 | tf_op jit(solution)/shard_map/pallas_call | solution.py:261
  114.9 10.8 %all-to-all-start.3 = ((bf16[64,24,128]{2,1,0:T(8,128)(2,1)}), bf16[64,24,128]{2,1,0:T(8,128)(2,1)S(1)}, u32[]{:S(2)}, u32[]{:S(2)}) async-start(bf16[64,24,128]{2,1,0:T(8,128)(2,1)} %bitcast.7), calls=%async_computation.3 | async-start | bytes 786432 | tf_op jit(solution)/shard_map/all_to_all | solution.py:23
  125.7 1.9 %collective-permute-start.3 = (bf16[192,768]{1,0:T(8,128)(2,1)S(1)}, bf16[192,768]{1,0:T(8,128)(2,1)S(1)}, u32[]{:S(2)}, u32[]{:S(2)}) collective-permute-start(bf16[192,768]{1,0:T(8,128)(2,1)S(1)} %get-tuple-element.23), channel_id=1, source_target_pairs={{0,8},{8,0},{1,9},{9,1},{2,10},{10,2},{3,11},{11,3},{4,12},{12,4},... | collective-permute-start | bytes 884744 | tf_op jit(solution)/shard_map/ppermute | solution.py:19
  127.7 0.0 copy-start.14
  127.7 2.4 %collective-permute-start.4 = (bf16[192,384]{1,0:T(8,128)(2,1)S(1)}, bf16[192,384]{1,0:T(8,128)(2,1)S(1)}, u32[]{:S(2)}, u32[]{:S(2)}) collective-permute-start(bf16[192,384]{1,0:T(8,128)(2,1)S(1)} %get-tuple-element.24), channel_id=1, source_target_pairs={{0,8},{8,0},{1,9},{9,1},{2,10},{10,2},{3,11},{11,3},{4,12},{12,4},... | collective-permute-start | bytes 442376 | tf_op jit(solution)/shard_map/ppermute | solution.py:19
  130.1 1.0 collective-permute-done.4.refs_4_
  131.1 0.0 collective-permute-done.3.refs_3_
  131.1 0.6 copy-done.16
  131.7 0.7 copy-done.15
  132.4 4.2 %shard_map.109 = (bf16[768,768]{1,0:T(8,128)(2,1)}, bf16[384,768]{1,0:T(8,128)(2,1)}) custom-call(bf16[192,1536]{1,0:T(8,128)(2,1)} %copy-done.11, bf16[192,1536]{1,0:T(8,128)(2,1)} %copy-done.4, bf16[192,2304]{1,0:T(8,128)(2,1)} %bitcast.12, bf16[192,768]{1,0:T(8,128)(2,1)} %copy-done.15, bf16[192,384]{1,0:T(8,128)(2,1)} %copy-done.16, ...), custom_call_target="tpu_custom_call" | custom-call | flops 1048576 | bytes 1048576 | tf_op jit(solution)/shard_map/pallas_call | solution.py:261
  136.7 3.8 %all-to-all-done.3 = bf16[64,24,128]{2,1,0:T(8,128)(2,1)S(1)} async-done(((bf16[64,24,128]{2,1,0:T(8,128)(2,1)}), bf16[64,24,128]{2,1,0:T(8,128)(2,1)S(1)}, u32[]{:S(2)}, u32[]{:S(2)}) %all-to-all-start.3) | async-done | bytes 393248 | tf_op jit(solution)/shard_map/all_to_all | solution.py:23
  140.4 1.2 shard_map.108
  (11 shorter events, 0.0 us)
Async XLA Ops:
  0.6 19.5 %copy-start.2 = (bf16[1,768,768]{2,1,0:T(8,128)(2,1)S(1)}, bf16[1,768,768]{2,1,0:T(8,128)(2,1)}, u32[]{:S(2)}) copy-start(bf16[1,768,768]{2,1,0:T(8,128)(2,1)} %param.12) | copy-start | bytes 3538948
  0.6 19.5 %copy-start.12 = (bf16[1,768]{1,0:T(2,128)(2,1)S(1)}, bf16[1,768]{1,0:T(2,128)(2,1)}, u32[]{:S(2)}) copy-start(bf16[1,768]{1,0:T(2,128)(2,1)} %refs_6_.1) | copy-start | bytes 4612
  0.7 19.5 %copy-start.13 = (bf16[1,768]{1,0:T(2,128)(2,1)S(1)}, bf16[1,768]{1,0:T(2,128)(2,1)}, u32[]{:S(2)}) copy-start(bf16[1,768]{1,0:T(2,128)(2,1)} %refs_8_.1) | copy-start | bytes 4612
  2.6 17.5 %copy-start.1 = (bf16[8,8,40,128]{3,2,1,0:T(8,128)(2,1)S(1)}, bf16[8,8,40,128]{3,2,1,0:T(8,128)(2,1)}, u32[]{:S(2)}) copy-start(bf16[8,8,40,128]{3,2,1,0:T(8,128)(2,1)} %shard_map.103) | copy-start | bytes 1966084
  2.6 35.9 %all-to-all-start = ((bf16[64,40,128]{2,1,0:T(8,128)(2,1)}), bf16[64,40,128]{2,1,0:T(8,128)(2,1)S(1)}, u32[]{:S(2)}, u32[]{:S(2)}) async-start(bf16[64,40,128]{2,1,0:T(8,128)(2,1)} %bitcast.13), calls=%async_computation | async-start | bytes 1310720 | tf_op jit(solution)/shard_map/all_to_all | solution.py:23
  20.2 1.1 copy-start.3
  22.8 1.2 copy-start.5
  24.0 6.9 %collective-permute-start = (bf16[768,768]{1,0:T(8,128)(2,1)S(1)}, bf16[768,768]{1,0:T(8,128)(2,1)S(1)}, u32[]{:S(2)}, u32[]{:S(2)}) collective-permute-start(bf16[768,768]{1,0:T(8,128)(2,1)S(1)} %get-tuple-element.16.own_ref), channel_id=1, source_target_pairs={{0,8},{8,0},{1,9},{9,1},{2,10},{10,2},{3,11},{11,3},{4,12},{12,4},... | collective-permute-start | bytes 3538952 | tf_op jit(solution)/shard_map/ppermute | solution.py:19
  26.0 1.0 copy-start.7
  27.0 4.0 %collective-permute-start.1 = (bf16[384,768]{1,0:T(8,128)(2,1)S(1)}, bf16[384,768]{1,0:T(8,128)(2,1)S(1)}, u32[]{:S(2)}, u32[]{:S(2)}) collective-permute-start(bf16[384,768]{1,0:T(8,128)(2,1)S(1)} %get-tuple-element.17), channel_id=1, source_target_pairs={{0,8},{8,0},{1,9},{9,1},{2,10},{10,2},{3,11},{11,3},{4,12},{12,4},... | collective-permute-start | bytes 1769480 | tf_op jit(solution)/shard_map/ppermute | solution.py:19
  38.6 1.5 %copy-start.6 = (bf16[1152,768]{1,0:T(8,128)(2,1)S(1)}, bf16[1152,768]{1,0:T(8,128)(2,1)}, u32[]{:S(2)}) copy-start(bf16[1152,768]{1,0:T(8,128)(2,1)} %copy-done.5) | copy-start | bytes 5308420
  42.8 1.0 copy-start.9
  43.8 44.4 %copy-start.11 = (bf16[192,1536]{1,0:T(8,128)(2,1)}, bf16[192,1536]{1,0:T(8,128)(2,1)S(1)}, u32[]{:S(2)}) copy-start(bf16[192,1536]{1,0:T(8,128)(2,1)S(1)} %get-tuple-element.18.refs_0_) | copy-start | bytes 1769476
  43.8 39.4 %all-to-all-start.1 = ((bf16[8,24,2304]{2,1,0:T(8,128)(2,1)}), bf16[8,24,2304]{2,1,0:T(8,128)(2,1)S(1)}, u32[]{:S(2)}, u32[]{:S(2)}) async-start(bf16[8,24,2304]{2,1,0:T(8,128)(2,1)} %bitcast.5), calls=%async_computation.1 | async-start | bytes 1769472 | tf_op jit(solution)/shard_map/all_to_all | solution.py:23
  84.5 26.1 %copy-start.8 = (bf16[768,768]{1,0:T(8,128)(2,1)S(1)}, bf16[768,768]{1,0:T(8,128)(2,1)}, u32[]{:S(2)}) copy-start(bf16[768,768]{1,0:T(8,128)(2,1)} %copy-done.7) | copy-start | bytes 3538948
  84.5 26.1 %all-to-all-start.2 = ((bf16[8,24,2304]{2,1,0:T(8,128)(2,1)}), bf16[8,24,2304]{2,1,0:T(8,128)(2,1)S(1)}, u32[]{:S(2)}, u32[]{:S(2)}) async-start(bf16[8,24,2304]{2,1,0:T(8,128)(2,1)} %shard_map.106), calls=%async_computation.2 | async-start | bytes 1769472 | tf_op jit(solution)/shard_map/all_to_all | solution.py:23
  88.2 3.9 %collective-permute-start.2 = (bf16[192,1536]{1,0:T(8,128)(2,1)S(1)}, bf16[192,1536]{1,0:T(8,128)(2,1)S(1)}, u32[]{:S(2)}, u32[]{:S(2)}) collective-permute-start(bf16[192,1536]{1,0:T(8,128)(2,1)S(1)} %get-tuple-element.18.refs_0_), channel_id=1, source_target_pairs={{0,8},{8,0},{1,9},{9,1},{2,10},{10,2},{3,11},{11,3},{4,12},{12,4},... | collective-permute-start | bytes 1769480 | tf_op jit(solution)/shard_map/ppermute | solution.py:19
  92.1 22.8 %copy-start.4 = (bf16[192,1536]{1,0:T(8,128)(2,1)}, bf16[192,1536]{1,0:T(8,128)(2,1)S(1)}, u32[]{:S(2)}) copy-start(bf16[192,1536]{1,0:T(8,128)(2,1)S(1)} %collective-permute-done.2.after_ref.refs_1_) | copy-start | bytes 1769476
  110.6 4.3 %copy-start = (bf16[8,24,2304]{2,1,0:T(8,128)(2,1)}, bf16[8,24,2304]{2,1,0:T(8,128)(2,1)S(1)}, u32[]{:S(2)}) copy-start(bf16[8,24,2304]{2,1,0:T(8,128)(2,1)S(1)} %all-to-all-done.2) | copy-start | bytes 2654212
  110.6 1.6 %copy-start.10 = (bf16[768,768]{1,0:T(8,128)(2,1)S(1)}, bf16[768,768]{1,0:T(8,128)(2,1)}, u32[]{:S(2)}) copy-start(bf16[768,768]{1,0:T(8,128)(2,1)} %copy-done.9) | copy-start | bytes 3538948
  114.9 25.5 %all-to-all-start.3 = ((bf16[64,24,128]{2,1,0:T(8,128)(2,1)}), bf16[64,24,128]{2,1,0:T(8,128)(2,1)S(1)}, u32[]{:S(2)}, u32[]{:S(2)}) async-start(bf16[64,24,128]{2,1,0:T(8,128)(2,1)} %bitcast.7), calls=%async_computation.3 | async-start | bytes 786432 | tf_op jit(solution)/shard_map/all_to_all | solution.py:23
  125.7 5.3 %collective-permute-start.3 = (bf16[192,768]{1,0:T(8,128)(2,1)S(1)}, bf16[192,768]{1,0:T(8,128)(2,1)S(1)}, u32[]{:S(2)}, u32[]{:S(2)}) collective-permute-start(bf16[192,768]{1,0:T(8,128)(2,1)S(1)} %get-tuple-element.23), channel_id=1, source_target_pairs={{0,8},{8,0},{1,9},{9,1},{2,10},{10,2},{3,11},{11,3},{4,12},{12,4},... | collective-permute-start | bytes 884744 | tf_op jit(solution)/shard_map/ppermute | solution.py:19
  127.7 12.8 %copy-start.14 = (s32[4,4]{1,0:T(4,128)S(1)}, s32[4,4]{1,0:T(4,128)}, u32[]{:S(2)}) copy-start(s32[4,4]{1,0:T(4,128)} %ids_ref.3) | copy-start | bytes 196
  127.7 3.4 %collective-permute-start.4 = (bf16[192,384]{1,0:T(8,128)(2,1)S(1)}, bf16[192,384]{1,0:T(8,128)(2,1)S(1)}, u32[]{:S(2)}, u32[]{:S(2)}) collective-permute-start(bf16[192,384]{1,0:T(8,128)(2,1)S(1)} %get-tuple-element.24), channel_id=1, source_target_pairs={{0,8},{8,0},{1,9},{9,1},{2,10},{10,2},{3,11},{11,3},{4,12},{12,4},... | collective-permute-start | bytes 442376 | tf_op jit(solution)/shard_map/ppermute | solution.py:19
  131.1 0.7 copy-start.16
  131.7 0.7 copy-start.15

commit v7 on v5

--- a/solution.py
+++ b/solution.py
@@ -10,7 +10,7 @@
 CORES = 2
 LANE = 128
 MIB = 1024 * 1024
-ROOMY, FULL = 28 * MIB, 60 * MIB
+ROOMY, SNUG, FULL = 28 * MIB, 51 * MIB, 60 * MIB
 F32 = jnp.float32
 BF16 = jnp.bfloat16
 
@@ -181,8 +181,14 @@
     wait_all(outs)
 
 
+def place(n, ref):
+    tiles = ref.shape[2] // LANE
+    at = n % tiles * LANE
+    return n // tiles, slice(at, at + LANE)
+
+
 def scatter_kernel(
-    parties, size, offset, after_ref, full_ref, own_ref, oth_ref, out_ref, dh_ref, act_ref, dh, act, own, oth, wide, out, sems
+    parties, offset, after_ref, full_ref, own_ref, oth_ref, out_ref, dh_ref, act_ref, dh, act, own, oth, wide, out, sems
 ):
     del after_ref
     width = own.shape[0]
@@ -198,7 +204,6 @@
         ],
         sems,
     )
-    wide[...] = jnp.zeros_like(wide)
     wait_all(copies[0:2])
     dx = dot(dh[0], own[...], ((1,), (1,)))
     wait_all(copies[2:4])
@@ -207,8 +212,8 @@
     dx = dx + dot(dh[1], oth[...], ((1,), (1,)))
     for j in range(CAP):
         for k in range(tiles):
-            value = dx[j * parties : (j + 1) * parties, k * LANE : (k + 1) * LANE]
-            wide[pl.ds(j * tiles + k, parties, stride=size), :] = value
+            row, cols = place(j * tiles + k, wide)
+            wide[:, row, cols] = dx[j * parties : (j + 1) * parties, k * LANE : (k + 1) * LANE]
     out[...] = wide[...].astype(BF16)
     wait_all(outs + start_all([(out, out_ref)], sems, 7))
 
@@ -239,10 +244,9 @@
     wait_all(outs)
 
 
-def combine_kernel(n_expert, n_y, size, ids_ref, back_ref, out_ref, ids, back, wide, out, sems):
+def combine_kernel(n_expert, n_y, ids_ref, back_ref, out_ref, ids, back, wide, out, sems):
     tok_rows, width = out.shape
     tiles = width // LANE
-    parties = n_expert * n_y
     copies = start_all([(ids_ref, ids), (back_ref, back)], sems)
     copies[0].wait()
     masks, _ = routing(ids[...], n_expert)
@@ -251,7 +255,8 @@
     for k in range(tiles):
         totals = [jnp.zeros((1, LANE), F32) for _ in range(tok_rows)]
         for j in range(CAP):
-            value = wide[pl.ds(j * tiles + k, parties, stride=size), :]
+            row, cols = place(j * tiles + k, wide)
+            value = wide[:, row, cols]
             value = jnp.sum(value.reshape(n_expert, n_y, LANE), axis=1)
             for i in range(tok_rows):
                 totals[i] = totals[i] + jnp.sum(jnp.where(masks[i][j], value, 0.0), axis=0, keepdims=True)
@@ -319,21 +324,19 @@
     scratch = like(flat) + [(flat.shape, F32)] + like(own, own, shapes[1], shapes[0], shapes[2])
     kernel = functools.partial(gather_kernel, parties, size)
     moved = 4 * own.size + 6 * got.size
-    return call(kernel, shapes, scratch, 6 + CORES, 4 * rows * own.size, moved, flat, own, oth_in, oth_out)
+    return call(kernel, shapes, scratch, 6 + CORES, 4 * rows * own.size, moved, flat, own, oth_in, oth_out, limit=SNUG)
 
 
 def scatter(after, full, own, oth, parties):
     rows = full.shape[0]
     height, width = own.shape
     hidden = width
-    size = up(CAP * width // LANE, 8)
-    flat = array((parties * size, LANE))
+    flat = array((parties, 2, CAP * width // 2))
     shapes = (flat, array((rows, hidden)), array((rows, height - width)))
     scratch = [((2, rows, hidden), BF16)] + like(shapes[2], oth, oth) + [(flat.shape, F32), (flat.shape, BF16)]
-    kernel = functools.partial(scatter_kernel, parties, size, height)
+    kernel = functools.partial(scatter_kernel, parties, height)
     flops, moved = 4 * rows * width * hidden, 4 * own.size
-    out, dh, act = call(kernel, shapes, scratch, 8, flops, moved, after, full, own, oth)
-    return out.reshape(parties, size, LANE), dh, act
+    return call(kernel, shapes, scratch, 8, flops, moved, after, full, own, oth, limit=SNUG)
 
 
 def weight_grads(mine, theirs, full, dh, act, w_in, scale_in, w_out, scale_out):
@@ -346,12 +349,10 @@
 
 
 def combine(ids, back, tok_rows, width, n_expert, n_y):
-    parties, size, _ = back.shape
-    flat = back.reshape(parties * size, LANE)
     shape = array((tok_rows, width))
-    scratch = like(ids, flat) + [(flat.shape, F32)] + like(shape)
-    kernel = functools.partial(combine_kernel, n_expert, n_y, size)
-    return call(kernel, shape, scratch, 3, 1 << 20, 1 << 20, ids, flat, limit=ROOMY)
+    scratch = like(ids, back) + [(back.shape, F32)] + like(shape)
+    kernel = functools.partial(combine_kernel, n_expert, n_y)
+    return call(kernel, shape, scratch, 3, 1 << 20, 1 << 20, ids, back, limit=ROOMY)
 
 
 def per_device(tokens, grad_output, expert_ids, gate_weights, w_in, scale_in, w_out, scale_out):

time: 142 us -> 139 us (0.979)
  the two profiles are of different devices: /device:TPU:4 before, /device:TPU:16 now
where the time goes in v7:
time: 139 us; the launch traced here: 138 us
  starting transfers between devices  60.9 us (44%)
  waiting for transfers between devices  54.6 us (39%)
  Pallas kernels  20.9 us (15%)
    all_to_all x4, starting transfers between devices, exchange(): return lax.all_to_all(x, axes, split_axis=0, concat_axis=0, tiled=True)  50.3 us
    all_to_all x4, waiting for transfers between devices, exchange(): return lax.all_to_all(x, axes, split_axis=0, concat_axis=0, tiled=True)  49.8 us
    pallas_call x7, Pallas kernels, call(): pl.pallas_call(kernel, out_shape=outs, in_specs=[SMEM if a.shape == (1,)...  20.9 us
    ppermute x5, starting transfers between devices, swap(): return lax.ppermute(x, 'core', [(0, 1), (1, 0)])  10.6 us
    ppermute x5, waiting for transfers between devices, swap(): return lax.ppermute(x, 'core', [(0, 1), (1, 0)])  4.78 us
  transfers between devices with their start and end apart: 9, of which 7 were waited for; matrix products, arithmetic and copies ran while one was open for 0% of the time, Pallas kernels for 6%

profile of v7, /device:TPU:16, one launch (start us, length us, event | category | flops | bytes accessed | tf_op | source)
XLA Modules:
  0.0 138.5 jit_solution(7210501693577884351)
XLA Ops:
  0.6 1.9 %shard_map.103 = bf16[8,8,40,128]{3,2,1,0:T(8,128)(2,1)} custom-call(s32[4,4]{1,0:T(4,128)} %ids_ref.3, bf16[4,4]{1,0:T(4,128)(2,1)} %gates_ref.1, bf16[4,768]{1,0:T(4,128)(2,1)} %tok_ref.1, bf16[4,768]{1,0:T(4,128)(2,1)} %cot_ref.1), custom_call_target="tpu_custom_call" | custom-call | flops 1048576 | bytes 1048576 | tf_op jit(solution)/shard_map/pallas_call | solution.py:276
  2.5 17.1 %all-to-all-start = ((bf16[64,40,128]{2,1,0:T(8,128)(2,1)}), bf16[64,40,128]{2,1,0:T(8,128)(2,1)S(1)}, u32[]{:S(2)}, u32[]{:S(2)}) async-start(bf16[64,40,128]{2,1,0:T(8,128)(2,1)} %bitcast.12), calls=%async_computation | async-start | bytes 1310720 | tf_op jit(solution)/shard_map/all_to_all | solution.py:23
  19.6 3.7 %shard_map.104 = (bf16[1152,768]{1,0:T(8,128)(2,1)}, bf16[768,768]{1,0:T(8,128)(2,1)}, bf16[384,768]{1,0:T(8,128)(2,1)}) custom-call(bf16[64,40,128]{2,1,0:T(8,128)(2,1)} %bitcast.13, bf16[768,768]{1,0:T(8,128)(2,1)} %bitcast.14, bf16[1,768]{1,0:T(2,128)(2,1)} %refs_6_.1, bf16[384,768]{1,0:T(8,128)(2,1)} %bitcast.16, bf16[1,768]{1,0:T(2,128)(2,1)} %refs_8_.1), custom_call_target="tpu_custom_call" | custom-call | flops 3538944 | bytes 3538944 | tf_op jit(solution)/shard_map/pallas_call | solution.py:276
  23.3 1.9 %collective-permute-start = (bf16[768,768]{1,0:T(8,128)(2,1)}, bf16[768,768]{1,0:T(8,128)(2,1)S(1)}, u32[]{:S(2)}, u32[]{:S(2)}) collective-permute-start(bf16[768,768]{1,0:T(8,128)(2,1)} %get-tuple-element.15), channel_id=1, source_target_pairs={{0,8},{8,0},{1,9},{9,1},{2,10},{10,2},{3,11},{11,3},{4,12},{12,4},... | collective-permute-start | bytes 3538952 | tf_op jit(solution)/shard_map/ppermute | solution.py:19
  25.2 2.4 %collective-permute-start.1 = (bf16[384,768]{1,0:T(8,128)(2,1)}, bf16[384,768]{1,0:T(8,128)(2,1)S(1)}, u32[]{:S(2)}, u32[]{:S(2)}) collective-permute-start(bf16[384,768]{1,0:T(8,128)(2,1)} %get-tuple-element.16), channel_id=1, source_target_pairs={{0,8},{8,0},{1,9},{9,1},{2,10},{10,2},{3,11},{11,3},{4,12},{12,4},... | collective-permute-start | bytes 1769480 | tf_op jit(solution)/shard_map/ppermute | solution.py:19
  27.6 1.8 %collective-permute-done.1.oth_out_ref = bf16[384,768]{1,0:T(8,128)(2,1)S(1)} collective-permute-done((bf16[384,768]{1,0:T(8,128)(2,1)}, bf16[384,768]{1,0:T(8,128)(2,1)S(1)}, u32[]{:S(2)}, u32[]{:S(2)}) %collective-permute-start.1) | collective-permute-done | bytes 589856 | tf_op jit(solution)/shard_map/ppermute | solution.py:19
  29.5 0.0 collective-permute-done.oth_in_ref.oth_ref
  29.5 0.0 copy-start.4
  29.5 7.8 %all-to-all-done = bf16[64,40,128]{2,1,0:T(8,128)(2,1)S(1)} async-done(((bf16[64,40,128]{2,1,0:T(8,128)(2,1)}), bf16[64,40,128]{2,1,0:T(8,128)(2,1)S(1)}, u32[]{:S(2)}, u32[]{:S(2)}) %all-to-all-start) | async-done | bytes 655392 | tf_op jit(solution)/shard_map/all_to_all | solution.py:23
  37.2 0.0 copy-done.4
  37.3 3.8 %shard_map.105 = (bf16[192,2304]{1,0:T(8,128)(2,1)}, bf16[192,1536]{1,0:T(8,128)(2,1)S(1)}, f32[192,128]{1,0:T(8,128)S(1)}) custom-call(bf16[2560,128]{1,0:T(8,128)(2,1)S(1)} %bitcast.11, bf16[1152,768]{1,0:T(8,128)(2,1)} %get-tuple-element.14.own_ref, bf16[768,768]{1,0:T(8,128)(2,1)} %copy-done.4, bf16[384,768]{1,0:T(8,128)(2,1)S(1)} %collective-permute-done.1.oth_out_ref), custom_call_target="tpu_custom_call" | custom-call | flops 679477248 | bytes 5505024 | tf_op jit(solution)/shard_map/pallas_call | solution.py:276
  41.1 0.0 copy-start.2
  41.1 16.5 %all-to-all-start.1 = ((bf16[8,24,2304]{2,1,0:T(8,128)(2,1)}), bf16[8,24,2304]{2,1,0:T(8,128)(2,1)S(1)}, u32[]{:S(2)}, u32[]{:S(2)}) async-start(bf16[8,24,2304]{2,1,0:T(8,128)(2,1)} %bitcast.5), calls=%async_computation.1 | async-start | bytes 1769472 | tf_op jit(solution)/shard_map/all_to_all | solution.py:23
  57.6 21.9 %all-to-all-done.1.parts_ref = bf16[8,24,2304]{2,1,0:T(8,128)(2,1)S(1)} async-done(((bf16[8,24,2304]{2,1,0:T(8,128)(2,1)}), bf16[8,24,2304]{2,1,0:T(8,128)(2,1)S(1)}, u32[]{:S(2)}, u32[]{:S(2)}) %all-to-all-start.1) | async-done | bytes 884768 | tf_op jit(solution)/shard_map/all_to_all | solution.py:23
  79.5 1.3 shard_map.106
  80.8 3.6 %all-to-all-start.2 = ((bf16[8,24,2304]{2,1,0:T(8,128)(2,1)}), bf16[8,24,2304]{2,1,0:T(8,128)(2,1)S(1)}, u32[]{:S(2)}, u32[]{:S(2)}) async-start(bf16[8,24,2304]{2,1,0:T(8,128)(2,1)} %shard_map.106), calls=%async_computation.2 | async-start | bytes 1769472 | tf_op jit(solution)/shard_map/all_to_all | solution.py:23
  84.3 0.0 copy-done.2
  84.4 1.9 %collective-permute-start.2 = (bf16[192,1536]{1,0:T(8,128)(2,1)S(1)}, bf16[192,1536]{1,0:T(8,128)(2,1)S(1)}, u32[]{:S(2)}, u32[]{:S(2)}) collective-permute-start(bf16[192,1536]{1,0:T(8,128)(2,1)S(1)} %get-tuple-element.17.refs_0_), channel_id=1, source_target_pairs={{0,8},{8,0},{1,9},{9,1},{2,10},{10,2},{3,11},{11,3},{4,12},{12,4},... | collective-permute-start | bytes 1769480 | tf_op jit(solution)/shard_map/ppermute | solution.py:19
  86.3 2.0 %collective-permute-done.2.after_ref.refs_1_ = bf16[192,1536]{1,0:T(8,128)(2,1)S(1)} collective-permute-done((bf16[192,1536]{1,0:T(8,128)(2,1)S(1)}, bf16[192,1536]{1,0:T(8,128)(2,1)S(1)}, u32[]{:S(2)}, u32[]{:S(2)}) %collective-permute-start.2) | collective-permute-done | bytes 589856 | tf_op jit(solution)/shard_map/ppermute | solution.py:19
  88.3 0.0 copy-start.1
  88.3 18.0 %all-to-all-done.2 = bf16[8,24,2304]{2,1,0:T(8,128)(2,1)S(1)} async-done(((bf16[8,24,2304]{2,1,0:T(8,128)(2,1)}), bf16[8,24,2304]{2,1,0:T(8,128)(2,1)S(1)}, u32[]{:S(2)}, u32[]{:S(2)}) %all-to-all-start.2) | async-done | bytes 884768 | tf_op jit(solution)/shard_map/all_to_all | solution.py:23
  106.3 0.0 copy-start
  106.3 4.4 %shard_map.107 = (bf16[64,2,1152]{2,1,0:T(2,128)(2,1)}, bf16[192,768]{1,0:T(8,128)(2,1)S(1)}, bf16[192,384]{1,0:T(8,128)(2,1)S(1)}) custom-call(bf16[192,1536]{1,0:T(8,128)(2,1)S(1)} %collective-permute-done.2.after_ref.refs_1_, bf16[192,2304]{1,0:T(8,128)(2,1)S(1)} %bitcast.9, bf16[1152,768]{1,0:T(8,128)(2,1)} %get-tuple-element.14.own_ref, ...), custom_call_target="tpu_custom_call" | custom-call | flops 452984832 | bytes 3538944 | tf_op jit(solution)/shard_map/pallas_call | solution.py:276
  110.7 0.0 copy-done.1
  110.7 0.0 copy-done
  110.7 13.1 %all-to-all-start.3 = ((bf16[64,2,1152]{2,1,0:T(2,128)(2,1)}), bf16[64,2,1152]{2,1,0:T(2,128)(2,1)S(1)}, u32[]{:S(2)}, u32[]{:S(2)}) async-start(bf16[64,2,1152]{2,1,0:T(2,128)(2,1)} %get-tuple-element.20), calls=%async_computation.3 | async-start | bytes 589824 | tf_op jit(solution)/shard_map/all_to_all | solution.py:23
  123.8 1.9 %collective-permute-start.3 = (bf16[192,768]{1,0:T(8,128)(2,1)S(1)}, bf16[192,768]{1,0:T(8,128)(2,1)S(1)}, u32[]{:S(2)}, u32[]{:S(2)}) collective-permute-start(bf16[192,768]{1,0:T(8,128)(2,1)S(1)} %get-tuple-element.21), channel_id=1, source_target_pairs={{0,8},{8,0},{1,9},{9,1},{2,10},{10,2},{3,11},{11,3},{4,12},{12,4},... | collective-permute-start | bytes 884744 | tf_op jit(solution)/shard_map/ppermute | solution.py:19
  125.8 0.0 copy-start.3
  125.8 2.4 %collective-permute-start.4 = (bf16[192,384]{1,0:T(8,128)(2,1)S(1)}, bf16[192,384]{1,0:T(8,128)(2,1)S(1)}, u32[]{:S(2)}, u32[]{:S(2)}) collective-permute-start(bf16[192,384]{1,0:T(8,128)(2,1)S(1)} %get-tuple-element.22), channel_id=1, source_target_pairs={{0,8},{8,0},{1,9},{9,1},{2,10},{10,2},{3,11},{11,3},{4,12},{12,4},... | collective-permute-start | bytes 442376 | tf_op jit(solution)/shard_map/ppermute | solution.py:19
  128.2 1.0 collective-permute-done.4.refs_4_
  129.2 0.0 copy-start.6
  129.2 0.0 collective-permute-done.3.refs_3_
  129.2 0.6 copy-done.6
  129.8 0.0 copy-start.5
  129.8 0.7 copy-done.5
  130.5 4.2 %shard_map.109 = (bf16[768,768]{1,0:T(8,128)(2,1)}, bf16[384,768]{1,0:T(8,128)(2,1)}) custom-call(bf16[192,1536]{1,0:T(8,128)(2,1)} %copy-done.2, bf16[192,1536]{1,0:T(8,128)(2,1)} %copy-done.1, bf16[192,2304]{1,0:T(8,128)(2,1)} %bitcast.10, bf16[192,768]{1,0:T(8,128)(2,1)} %copy-done.5, bf16[192,384]{1,0:T(8,128)(2,1)} %copy-done.6, ...), custom_call_target="tpu_custom_call" | custom-call | flops 1048576 | bytes 1048576 | tf_op jit(solution)/shard_map/pallas_call | solution.py:276
  134.8 2.1 %all-to-all-done.3.back_ref = bf16[64,2,1152]{2,1,0:T(2,128)(2,1)S(1)} async-done(((bf16[64,2,1152]{2,1,0:T(2,128)(2,1)}), bf16[64,2,1152]{2,1,0:T(2,128)(2,1)S(1)}, u32[]{:S(2)}, u32[]{:S(2)}) %all-to-all-start.3) | async-done | bytes 294944 | tf_op jit(solution)/shard_map/all_to_all | solution.py:23
  136.9 0.0 copy-done.3
  136.9 1.6 %shard_map.108 = bf16[4,768]{1,0:T(4,128)(2,1)} custom-call(s32[4,4]{1,0:T(4,128)S(1)} %copy-done.3, bf16[64,2,1152]{2,1,0:T(2,128)(2,1)S(1)} %all-to-all-done.3.back_ref), custom_call_target="tpu_custom_call" | custom-call | flops 1048576 | bytes 1048576 | tf_op jit(solution)/shard_map/pallas_call | solution.py:276
Async XLA Ops:
  2.5 34.7 %all-to-all-start = ((bf16[64,40,128]{2,1,0:T(8,128)(2,1)}), bf16[64,40,128]{2,1,0:T(8,128)(2,1)S(1)}, u32[]{:S(2)}, u32[]{:S(2)}) async-start(bf16[64,40,128]{2,1,0:T(8,128)(2,1)} %bitcast.12), calls=%async_computation | async-start | bytes 1310720 | tf_op jit(solution)/shard_map/all_to_all | solution.py:23
  23.3 6.2 %collective-permute-start = (bf16[768,768]{1,0:T(8,128)(2,1)}, bf16[768,768]{1,0:T(8,128)(2,1)S(1)}, u32[]{:S(2)}, u32[]{:S(2)}) collective-permute-start(bf16[768,768]{1,0:T(8,128)(2,1)} %get-tuple-element.15), channel_id=1, source_target_pairs={{0,8},{8,0},{1,9},{9,1},{2,10},{10,2},{3,11},{11,3},{4,12},{12,4},... | collective-permute-start | bytes 3538952 | tf_op jit(solution)/shard_map/ppermute | solution.py:19
  25.2 4.2 %collective-permute-start.1 = (bf16[384,768]{1,0:T(8,128)(2,1)}, bf16[384,768]{1,0:T(8,128)(2,1)S(1)}, u32[]{:S(2)}, u32[]{:S(2)}) collective-permute-start(bf16[384,768]{1,0:T(8,128)(2,1)} %get-tuple-element.16), channel_id=1, source_target_pairs={{0,8},{8,0},{1,9},{9,1},{2,10},{10,2},{3,11},{11,3},{4,12},{12,4},... | collective-permute-start | bytes 1769480 | tf_op jit(solution)/shard_map/ppermute | solution.py:19
  29.5 7.8 %copy-start.4 = (bf16[768,768]{1,0:T(8,128)(2,1)}, bf16[768,768]{1,0:T(8,128)(2,1)S(1)}, u32[]{:S(2)}) copy-start(bf16[768,768]{1,0:T(8,128)(2,1)S(1)} %collective-permute-done.oth_in_ref.oth_ref) | copy-start | bytes 3538948
  41.1 43.3 %copy-start.2 = (bf16[192,1536]{1,0:T(8,128)(2,1)}, bf16[192,1536]{1,0:T(8,128)(2,1)S(1)}, u32[]{:S(2)}) copy-start(bf16[192,1536]{1,0:T(8,128)(2,1)S(1)} %get-tuple-element.17.refs_0_) | copy-start | bytes 1769476
  41.1 38.4 %all-to-all-start.1 = ((bf16[8,24,2304]{2,1,0:T(8,128)(2,1)}), bf16[8,24,2304]{2,1,0:T(8,128)(2,1)S(1)}, u32[]{:S(2)}, u32[]{:S(2)}) async-start(bf16[8,24,2304]{2,1,0:T(8,128)(2,1)} %bitcast.5), calls=%async_computation.1 | async-start | bytes 1769472 | tf_op jit(solution)/shard_map/all_to_all | solution.py:23
  80.8 25.5 %all-to-all-start.2 = ((bf16[8,24,2304]{2,1,0:T(8,128)(2,1)}), bf16[8,24,2304]{2,1,0:T(8,128)(2,1)S(1)}, u32[]{:S(2)}, u32[]{:S(2)}) async-start(bf16[8,24,2304]{2,1,0:T(8,128)(2,1)} %shard_map.106), calls=%async_computation.2 | async-start | bytes 1769472 | tf_op jit(solution)/shard_map/all_to_all | solution.py:23
  84.4 3.9 %collective-permute-start.2 = (bf16[192,1536]{1,0:T(8,128)(2,1)S(1)}, bf16[192,1536]{1,0:T(8,128)(2,1)S(1)}, u32[]{:S(2)}, u32[]{:S(2)}) collective-permute-start(bf16[192,1536]{1,0:T(8,128)(2,1)S(1)} %get-tuple-element.17.refs_0_), channel_id=1, source_target_pairs={{0,8},{8,0},{1,9},{9,1},{2,10},{10,2},{3,11},{11,3},{4,12},{12,4},... | collective-permute-start | bytes 1769480 | tf_op jit(solution)/shard_map/ppermute | solution.py:19
  88.3 22.4 %copy-start.1 = (bf16[192,1536]{1,0:T(8,128)(2,1)}, bf16[192,1536]{1,0:T(8,128)(2,1)S(1)}, u32[]{:S(2)}) copy-start(bf16[192,1536]{1,0:T(8,128)(2,1)S(1)} %collective-permute-done.2.after_ref.refs_1_) | copy-start | bytes 1769476
  106.3 4.4 %copy-start = (bf16[8,24,2304]{2,1,0:T(8,128)(2,1)}, bf16[8,24,2304]{2,1,0:T(8,128)(2,1)S(1)}, u32[]{:S(2)}) copy-start(bf16[8,24,2304]{2,1,0:T(8,128)(2,1)S(1)} %all-to-all-done.2) | copy-start | bytes 2654212
  110.7 26.1 %all-to-all-start.3 = ((bf16[64,2,1152]{2,1,0:T(2,128)(2,1)}), bf16[64,2,1152]{2,1,0:T(2,128)(2,1)S(1)}, u32[]{:S(2)}, u32[]{:S(2)}) async-start(bf16[64,2,1152]{2,1,0:T(2,128)(2,1)} %get-tuple-element.20), calls=%async_computation.3 | async-start | bytes 589824 | tf_op jit(solution)/shard_map/all_to_all | solution.py:23
  123.8 5.3 %collective-permute-start.3 = (bf16[192,768]{1,0:T(8,128)(2,1)S(1)}, bf16[192,768]{1,0:T(8,128)(2,1)S(1)}, u32[]{:S(2)}, u32[]{:S(2)}) collective-permute-start(bf16[192,768]{1,0:T(8,128)(2,1)S(1)} %get-tuple-element.21), channel_id=1, source_target_pairs={{0,8},{8,0},{1,9},{9,1},{2,10},{10,2},{3,11},{11,3},{4,12},{12,4},... | collective-permute-start | bytes 884744 | tf_op jit(solution)/shard_map/ppermute | solution.py:19
  125.8 11.1 %copy-start.3 = (s32[4,4]{1,0:T(4,128)S(1)}, s32[4,4]{1,0:T(4,128)}, u32[]{:S(2)}) copy-start(s32[4,4]{1,0:T(4,128)} %ids_ref.3) | copy-start | bytes 196
  125.8 3.4 %collective-permute-start.4 = (bf16[192,384]{1,0:T(8,128)(2,1)S(1)}, bf16[192,384]{1,0:T(8,128)(2,1)S(1)}, u32[]{:S(2)}, u32[]{:S(2)}) collective-permute-start(bf16[192,384]{1,0:T(8,128)(2,1)S(1)} %get-tuple-element.22), channel_id=1, source_target_pairs={{0,8},{8,0},{1,9},{9,1},{2,10},{10,2},{3,11},{11,3},{4,12},{12,4},... | collective-permute-start | bytes 442376 | tf_op jit(solution)/shard_map/ppermute | solution.py:19
  129.2 0.7 copy-start.6
  129.8 0.7 copy-start.5

commit v8 on v7

--- a/solution.py
+++ b/solution.py
@@ -8,6 +8,7 @@
 
 CAP = 3
 CORES = 2
+PIECES = 3
 LANE = 128
 MIB = 1024 * 1024
 ROOMY, SNUG, FULL = 28 * MIB, 51 * MIB, 60 * MIB
@@ -97,17 +98,10 @@
     units = own.shape[0] - width
     tiles = width // LANE
     half = width + units
-    copies = start_all(
-        [
-            (got_ref, got),
-            (own_ref, own),
-            (oth_in_ref, oth.at[0:width, :]),
-            (oth_out_ref, oth.at[width:half, :]),
-        ],
-        sems,
-    )
+    copies = start_all([(got_ref, got), (own_ref, own)], sems)
     copies[0].wait()
     wide[...] = got[...].astype(F32)
+    copies += start_all([(oth_in_ref, oth.at[0:width, :]), (oth_out_ref, oth.at[width:half, :])], sems, 2)
     gates = wide[pl.ds(2 * tiles * CAP, parties, stride=size), :]
     for j in range(CAP):
         at = slice(j * parties, (j + 1) * parties)
@@ -194,28 +188,31 @@
     width = own.shape[0]
     hidden = own.shape[1]
     tiles = width // LANE
+    step = width // PIECES
     copies = start_all(
         [
             (full_ref.at[:, 0:hidden], dh.at[0]),
-            (own_ref.at[0:width, :], own),
             (full_ref.at[:, offset : offset + hidden], dh.at[1]),
-            (oth_ref, oth),
             (full_ref.at[:, offset + hidden : 2 * offset], act),
         ],
         sems,
     )
-    wait_all(copies[0:2])
-    dx = dot(dh[0], own[...], ((1,), (1,)))
-    wait_all(copies[2:4])
-    copies[4].wait()
-    outs = start_all([(dh.at[1], dh_ref), (act, act_ref)], sems, 5)
-    dx = dx + dot(dh[1], oth[...], ((1,), (1,)))
-    for j in range(CAP):
-        for k in range(tiles):
-            row, cols = place(j * tiles + k, wide)
-            wide[:, row, cols] = dx[j * parties : (j + 1) * parties, k * LANE : (k + 1) * LANE]
+    spans = [slice(p * step, (p + 1) * step) for p in range(PIECES)]
+    pieces = [
+        start_all([(own_ref.at[at, :], own.at[at, :]), (oth_ref.at[at, :], oth.at[at, :])], sems, 3 + 2 * p)
+        for p, at in enumerate(spans)
+    ]
+    wait_all(copies)
+    outs = start_all([(dh.at[1], dh_ref), (act, act_ref)], sems, 3 + 2 * PIECES)
+    for p, at in enumerate(spans):
+        wait_all(pieces[p])
+        dx = dot(dh[0], own[at, :], ((1,), (1,))) + dot(dh[1], oth[at, :], ((1,), (1,)))
+        for j in range(CAP):
+            for k in range(step // LANE):
+                row, cols = place(j * tiles + p * (step // LANE) + k, wide)
+                wide[:, row, cols] = dx[j * parties : (j + 1) * parties, k * LANE : (k + 1) * LANE]
     out[...] = wide[...].astype(BF16)
-    wait_all(outs + start_all([(out, out_ref)], sems, 7))
+    wait_all(outs + start_all([(out, out_ref)], sems, 5 + 2 * PIECES))
 
 
 def grads_kernel(step, *refs):
@@ -336,7 +333,7 @@
     scratch = [((2, rows, hidden), BF16)] + like(shapes[2], oth, oth) + [(flat.shape, F32), (flat.shape, BF16)]
     kernel = functools.partial(scatter_kernel, parties, height)
     flops, moved = 4 * rows * width * hidden, 4 * own.size
-    return call(kernel, shapes, scratch, 8, flops, moved, after, full, own, oth, limit=SNUG)
+    return call(kernel, shapes, scratch, 6 + 2 * PIECES, flops, moved, after, full, own, oth, limit=SNUG)
 
 
 def weight_grads(mine, theirs, full, dh, act, w_in, scale_in, w_out, scale_out):
@@ -345,7 +342,7 @@
     args = (mine, theirs, full, dh, act, w_in, scale_in, w_out, scale_out)
     held = like(*args)
     held[2] = ((full.shape[0], full.shape[1] // CORES), BF16)
-    return call(kernel, shapes, held + like(*shapes), len(args) + 2, 1 << 20, 1 << 20, *args)
+    return call(kernel, shapes, held + like(*shapes), len(args) + 2, 1 << 20, 1 << 20, *args, limit=SNUG)
 
 
 def combine(ids, back, tok_rows, width, n_expert, n_y):

time: 139 us -> 139 us (level)
  waiting for transfers between devices: 54.6 us -> 56.2 us
    all_to_all x4, waiting for transfers between devices: 49.8 us -> 51.4 us  [exchange(): return lax.all_to_all(x, axes, split_axis=0, concat_axis=0, tiled=True)]
where the time goes in v8:
time: 139 us; the launch traced here: 138 us
  starting transfers between devices  60.9 us (44%)
  waiting for transfers between devices  56.2 us (40%)
  Pallas kernels  20.6 us (15%)
    all_to_all x4, waiting for transfers between devices, exchange(): return lax.all_to_all(x, axes, split_axis=0, concat_axis=0, tiled=True)  51.4 us
    all_to_all x4, starting transfers between devices, exchange(): return lax.all_to_all(x, axes, split_axis=0, concat_axis=0, tiled=True)  50.3 us
    pallas_call x7, Pallas kernels, call(): pl.pallas_call(kernel, out_shape=outs, in_specs=[SMEM if a.shape == (1,)...  20.6 us
    ppermute x5, starting transfers between devices, swap(): return lax.ppermute(x, 'core', [(0, 1), (1, 0)])  10.6 us
    ppermute x5, waiting for transfers between devices, swap(): return lax.ppermute(x, 'core', [(0, 1), (1, 0)])  4.78 us
  transfers between devices with their start and end apart: 9, of which 7 were waited for; matrix products, arithmetic and copies ran while one was open for 0% of the time, Pallas kernels for 6%

profile of v8, /device:TPU:16, one launch (start us, length us, event | category | flops | bytes accessed | tf_op | source)
XLA Modules:
  0.0 138.4 jit_solution(15291387099172042070)
XLA Ops:
  0.6 1.9 %shard_map.103 = bf16[8,8,40,128]{3,2,1,0:T(8,128)(2,1)} custom-call(s32[4,4]{1,0:T(4,128)} %ids_ref.3, bf16[4,4]{1,0:T(4,128)(2,1)} %gates_ref.1, bf16[4,768]{1,0:T(4,128)(2,1)} %tok_ref.1, bf16[4,768]{1,0:T(4,128)(2,1)} %cot_ref.1), custom_call_target="tpu_custom_call" | custom-call | flops 1048576 | bytes 1048576 | tf_op jit(solution)/shard_map/pallas_call | solution.py:273
  2.5 17.1 %all-to-all-start = ((bf16[64,40,128]{2,1,0:T(8,128)(2,1)}), bf16[64,40,128]{2,1,0:T(8,128)(2,1)S(1)}, u32[]{:S(2)}, u32[]{:S(2)}) async-start(bf16[64,40,128]{2,1,0:T(8,128)(2,1)} %bitcast.14), calls=%async_computation | async-start | bytes 1310720 | tf_op jit(solution)/shard_map/all_to_all | solution.py:24
  19.6 3.7 %shard_map.104 = (bf16[1152,768]{1,0:T(8,128)(2,1)}, bf16[768,768]{1,0:T(8,128)(2,1)}, bf16[384,768]{1,0:T(8,128)(2,1)}) custom-call(bf16[64,40,128]{2,1,0:T(8,128)(2,1)} %bitcast.15, bf16[768,768]{1,0:T(8,128)(2,1)} %bitcast.16, bf16[1,768]{1,0:T(2,128)(2,1)} %refs_6_.1, bf16[384,768]{1,0:T(8,128)(2,1)} %bitcast.12, bf16[1,768]{1,0:T(2,128)(2,1)} %refs_8_.1), custom_call_target="tpu_custom_call" | custom-call | flops 3538944 | bytes 3538944 | tf_op jit(solution)/shard_map/pallas_call | solution.py:273
  23.3 1.9 %collective-permute-start = (bf16[768,768]{1,0:T(8,128)(2,1)}, bf16[768,768]{1,0:T(8,128)(2,1)S(1)}, u32[]{:S(2)}, u32[]{:S(2)}) collective-permute-start(bf16[768,768]{1,0:T(8,128)(2,1)} %get-tuple-element.15), channel_id=1, source_target_pairs={{0,8},{8,0},{1,9},{9,1},{2,10},{10,2},{3,11},{11,3},{4,12},{12,4},... | collective-permute-start | bytes 3538952 | tf_op jit(solution)/shard_map/ppermute | solution.py:20
  25.2 2.4 %collective-permute-start.1 = (bf16[384,768]{1,0:T(8,128)(2,1)}, bf16[384,768]{1,0:T(8,128)(2,1)S(1)}, u32[]{:S(2)}, u32[]{:S(2)}) collective-permute-start(bf16[384,768]{1,0:T(8,128)(2,1)} %get-tuple-element.16), channel_id=1, source_target_pairs={{0,8},{8,0},{1,9},{9,1},{2,10},{10,2},{3,11},{11,3},{4,12},{12,4},... | collective-permute-start | bytes 1769480 | tf_op jit(solution)/shard_map/ppermute | solution.py:20
  27.6 1.8 %collective-permute-done.1.oth_out_ref = bf16[384,768]{1,0:T(8,128)(2,1)S(1)} collective-permute-done((bf16[384,768]{1,0:T(8,128)(2,1)}, bf16[384,768]{1,0:T(8,128)(2,1)S(1)}, u32[]{:S(2)}, u32[]{:S(2)}) %collective-permute-start.1) | collective-permute-done | bytes 589856 | tf_op jit(solution)/shard_map/ppermute | solution.py:20
  29.5 0.0 collective-permute-done.oth_in_ref.oth_ref
  29.5 0.0 copy-start.5
  29.5 7.8 %all-to-all-done = bf16[64,40,128]{2,1,0:T(8,128)(2,1)S(1)} async-done(((bf16[64,40,128]{2,1,0:T(8,128)(2,1)}), bf16[64,40,128]{2,1,0:T(8,128)(2,1)S(1)}, u32[]{:S(2)}, u32[]{:S(2)}) %all-to-all-start) | async-done | bytes 655392 | tf_op jit(solution)/shard_map/all_to_all | solution.py:24
  37.3 0.0 copy-done.5
  37.3 3.8 %shard_map.105 = (bf16[192,2304]{1,0:T(8,128)(2,1)}, bf16[192,1536]{1,0:T(8,128)(2,1)S(1)}, f32[192,128]{1,0:T(8,128)S(1)}) custom-call(bf16[2560,128]{1,0:T(8,128)(2,1)S(1)} %bitcast.11, bf16[1152,768]{1,0:T(8,128)(2,1)} %get-tuple-element.14.own_ref, bf16[768,768]{1,0:T(8,128)(2,1)} %copy-done.5, bf16[384,768]{1,0:T(8,128)(2,1)S(1)} %collective-permute-done.1.oth_out_ref), custom_call_target="tpu_custom_call" | custom-call | flops 679477248 | bytes 5505024 | tf_op jit(solution)/shard_map/pallas_call | solution.py:273
  41.1 16.5 %all-to-all-start.1 = ((bf16[8,24,2304]{2,1,0:T(8,128)(2,1)}), bf16[8,24,2304]{2,1,0:T(8,128)(2,1)S(1)}, u32[]{:S(2)}, u32[]{:S(2)}) async-start(bf16[8,24,2304]{2,1,0:T(8,128)(2,1)} %bitcast.5), calls=%async_computation.1 | async-start | bytes 1769472 | tf_op jit(solution)/shard_map/all_to_all | solution.py:24
  57.6 21.9 %all-to-all-done.1.parts_ref = bf16[8,24,2304]{2,1,0:T(8,128)(2,1)S(1)} async-done(((bf16[8,24,2304]{2,1,0:T(8,128)(2,1)}), bf16[8,24,2304]{2,1,0:T(8,128)(2,1)S(1)}, u32[]{:S(2)}, u32[]{:S(2)}) %all-to-all-start.1) | async-done | bytes 884768 | tf_op jit(solution)/shard_map/all_to_all | solution.py:24
  79.5 1.3 shard_map.106
  80.8 3.6 %all-to-all-start.2 = ((bf16[8,24,2304]{2,1,0:T(8,128)(2,1)}), bf16[8,24,2304]{2,1,0:T(8,128)(2,1)S(1)}, u32[]{:S(2)}, u32[]{:S(2)}) async-start(bf16[8,24,2304]{2,1,0:T(8,128)(2,1)} %shard_map.106), calls=%async_computation.2 | async-start | bytes 1769472 | tf_op jit(solution)/shard_map/all_to_all | solution.py:24
  84.3 1.9 %collective-permute-start.2 = (bf16[192,1536]{1,0:T(8,128)(2,1)S(1)}, bf16[192,1536]{1,0:T(8,128)(2,1)S(1)}, u32[]{:S(2)}, u32[]{:S(2)}) collective-permute-start(bf16[192,1536]{1,0:T(8,128)(2,1)S(1)} %get-tuple-element.17.refs_0_), channel_id=1, source_target_pairs={{0,8},{8,0},{1,9},{9,1},{2,10},{10,2},{3,11},{11,3},{4,12},{12,4},... | collective-permute-start | bytes 1769480 | tf_op jit(solution)/shard_map/ppermute | solution.py:20
  86.3 2.0 %collective-permute-done.2.after_ref.refs_1_ = bf16[192,1536]{1,0:T(8,128)(2,1)S(1)} collective-permute-done((bf16[192,1536]{1,0:T(8,128)(2,1)S(1)}, bf16[192,1536]{1,0:T(8,128)(2,1)S(1)}, u32[]{:S(2)}, u32[]{:S(2)}) %collective-permute-start.2) | collective-permute-done | bytes 589856 | tf_op jit(solution)/shard_map/ppermute | solution.py:20
  88.2 18.1 %all-to-all-done.2 = bf16[8,24,2304]{2,1,0:T(8,128)(2,1)S(1)} async-done(((bf16[8,24,2304]{2,1,0:T(8,128)(2,1)}), bf16[8,24,2304]{2,1,0:T(8,128)(2,1)S(1)}, u32[]{:S(2)}, u32[]{:S(2)}) %all-to-all-start.2) | async-done | bytes 884768 | tf_op jit(solution)/shard_map/all_to_all | solution.py:24
  106.3 0.0 copy-start
  106.3 0.0 copy-start.1
  106.3 0.0 copy-start.2
  106.3 0.0 copy-start.3
  106.3 4.4 %shard_map.107 = (bf16[64,2,1152]{2,1,0:T(2,128)(2,1)}, bf16[192,768]{1,0:T(8,128)(2,1)S(1)}, bf16[192,384]{1,0:T(8,128)(2,1)S(1)}) custom-call(bf16[192,1536]{1,0:T(8,128)(2,1)S(1)} %collective-permute-done.2.after_ref.refs_1_, bf16[192,2304]{1,0:T(8,128)(2,1)S(1)} %bitcast.9, bf16[1152,768]{1,0:T(8,128)(2,1)} %get-tuple-element.14.own_ref, ...), custom_call_target="tpu_custom_call" | custom-call | flops 452984832 | bytes 3538944 | tf_op jit(solution)/shard_map/pallas_call | solution.py:273
  110.7 0.0 copy-done
  110.7 13.1 %all-to-all-start.3 = ((bf16[64,2,1152]{2,1,0:T(2,128)(2,1)}), bf16[64,2,1152]{2,1,0:T(2,128)(2,1)S(1)}, u32[]{:S(2)}, u32[]{:S(2)}) async-start(bf16[64,2,1152]{2,1,0:T(2,128)(2,1)} %get-tuple-element.20), calls=%async_computation.3 | async-start | bytes 589824 | tf_op jit(solution)/shard_map/all_to_all | solution.py:24
  123.8 1.9 %collective-permute-start.3 = (bf16[192,768]{1,0:T(8,128)(2,1)S(1)}, bf16[192,768]{1,0:T(8,128)(2,1)S(1)}, u32[]{:S(2)}, u32[]{:S(2)}) collective-permute-start(bf16[192,768]{1,0:T(8,128)(2,1)S(1)} %get-tuple-element.21), channel_id=1, source_target_pairs={{0,8},{8,0},{1,9},{9,1},{2,10},{10,2},{3,11},{11,3},{4,12},{12,4},... | collective-permute-start | bytes 884744 | tf_op jit(solution)/shard_map/ppermute | solution.py:20
  125.7 0.0 copy-start.4
  125.7 2.4 %collective-permute-start.4 = (bf16[192,384]{1,0:T(8,128)(2,1)S(1)}, bf16[192,384]{1,0:T(8,128)(2,1)S(1)}, u32[]{:S(2)}, u32[]{:S(2)}) collective-permute-start(bf16[192,384]{1,0:T(8,128)(2,1)S(1)} %get-tuple-element.22), channel_id=1, source_target_pairs={{0,8},{8,0},{1,9},{9,1},{2,10},{10,2},{3,11},{11,3},{4,12},{12,4},... | collective-permute-start | bytes 442376 | tf_op jit(solution)/shard_map/ppermute | solution.py:20
  128.2 1.0 collective-permute-done.4.refs_4_
  129.1 0.0 collective-permute-done.3.refs_3_
  129.1 0.0 copy-done.1
  129.1 0.0 copy-done.2
  129.1 0.0 copy-done.3
  129.2 4.0 %shard_map.109 = (bf16[768,768]{1,0:T(8,128)(2,1)}, bf16[384,768]{1,0:T(8,128)(2,1)}) custom-call(bf16[192,1536]{1,0:T(8,128)(2,1)S(1)} %get-tuple-element.17.refs_0_, bf16[192,1536]{1,0:T(8,128)(2,1)S(1)} %collective-permute-done.2.after_ref.refs_1_, bf16[192,2304]{1,0:T(8,128)(2,1)} %bitcast.10, bf16[192,768]{1,0:T(8,128)(2,1)S(1)} %collective-permute-done.3.refs_3_, ...), custom_call_target="tpu_custom_call" | custom-call | flops 1048576 | bytes 1048576 | tf_op jit(solution)/shard_map/pallas_call | solution.py:273
  133.1 3.7 %all-to-all-done.3.back_ref = bf16[64,2,1152]{2,1,0:T(2,128)(2,1)S(1)} async-done(((bf16[64,2,1152]{2,1,0:T(2,128)(2,1)}), bf16[64,2,1152]{2,1,0:T(2,128)(2,1)S(1)}, u32[]{:S(2)}, u32[]{:S(2)}) %all-to-all-start.3) | async-done | bytes 294944 | tf_op jit(solution)/shard_map/all_to_all | solution.py:24
  136.8 0.0 copy-done.4
  136.8 1.6 %shard_map.108 = bf16[4,768]{1,0:T(4,128)(2,1)} custom-call(s32[4,4]{1,0:T(4,128)S(1)} %copy-done.4, bf16[64,2,1152]{2,1,0:T(2,128)(2,1)S(1)} %all-to-all-done.3.back_ref), custom_call_target="tpu_custom_call" | custom-call | flops 1048576 | bytes 1048576 | tf_op jit(solution)/shard_map/pallas_call | solution.py:273
Async XLA Ops:
  2.5 34.7 %all-to-all-start = ((bf16[64,40,128]{2,1,0:T(8,128)(2,1)}), bf16[64,40,128]{2,1,0:T(8,128)(2,1)S(1)}, u32[]{:S(2)}, u32[]{:S(2)}) async-start(bf16[64,40,128]{2,1,0:T(8,128)(2,1)} %bitcast.14), calls=%async_computation | async-start | bytes 1310720 | tf_op jit(solution)/shard_map/all_to_all | solution.py:24
  23.3 6.2 %collective-permute-start = (bf16[768,768]{1,0:T(8,128)(2,1)}, bf16[768,768]{1,0:T(8,128)(2,1)S(1)}, u32[]{:S(2)}, u32[]{:S(2)}) collective-permute-start(bf16[768,768]{1,0:T(8,128)(2,1)} %get-tuple-element.15), channel_id=1, source_target_pairs={{0,8},{8,0},{1,9},{9,1},{2,10},{10,2},{3,11},{11,3},{4,12},{12,4},... | collective-permute-start | bytes 3538952 | tf_op jit(solution)/shard_map/ppermute | solution.py:20
  25.2 4.2 %collective-permute-start.1 = (bf16[384,768]{1,0:T(8,128)(2,1)}, bf16[384,768]{1,0:T(8,128)(2,1)S(1)}, u32[]{:S(2)}, u32[]{:S(2)}) collective-permute-start(bf16[384,768]{1,0:T(8,128)(2,1)} %get-tuple-element.16), channel_id=1, source_target_pairs={{0,8},{8,0},{1,9},{9,1},{2,10},{10,2},{3,11},{11,3},{4,12},{12,4},... | collective-permute-start | bytes 1769480 | tf_op jit(solution)/shard_map/ppermute | solution.py:20
  29.5 7.8 %copy-start.5 = (bf16[768,768]{1,0:T(8,128)(2,1)}, bf16[768,768]{1,0:T(8,128)(2,1)S(1)}, u32[]{:S(2)}) copy-start(bf16[768,768]{1,0:T(8,128)(2,1)S(1)} %collective-permute-done.oth_in_ref.oth_ref) | copy-start | bytes 3538948
  41.1 38.4 %all-to-all-start.1 = ((bf16[8,24,2304]{2,1,0:T(8,128)(2,1)}), bf16[8,24,2304]{2,1,0:T(8,128)(2,1)S(1)}, u32[]{:S(2)}, u32[]{:S(2)}) async-start(bf16[8,24,2304]{2,1,0:T(8,128)(2,1)} %bitcast.5), calls=%async_computation.1 | async-start | bytes 1769472 | tf_op jit(solution)/shard_map/all_to_all | solution.py:24
  80.8 25.5 %all-to-all-start.2 = ((bf16[8,24,2304]{2,1,0:T(8,128)(2,1)}), bf16[8,24,2304]{2,1,0:T(8,128)(2,1)S(1)}, u32[]{:S(2)}, u32[]{:S(2)}) async-start(bf16[8,24,2304]{2,1,0:T(8,128)(2,1)} %shard_map.106), calls=%async_computation.2 | async-start | bytes 1769472 | tf_op jit(solution)/shard_map/all_to_all | solution.py:24
  84.3 3.9 %collective-permute-start.2 = (bf16[192,1536]{1,0:T(8,128)(2,1)S(1)}, bf16[192,1536]{1,0:T(8,128)(2,1)S(1)}, u32[]{:S(2)}, u32[]{:S(2)}) collective-permute-start(bf16[192,1536]{1,0:T(8,128)(2,1)S(1)} %get-tuple-element.17.refs_0_), channel_id=1, source_target_pairs={{0,8},{8,0},{1,9},{9,1},{2,10},{10,2},{3,11},{11,3},{4,12},{12,4},... | collective-permute-start | bytes 1769480 | tf_op jit(solution)/shard_map/ppermute | solution.py:20
  106.3 4.4 %copy-start = (bf16[8,24,2304]{2,1,0:T(8,128)(2,1)}, bf16[8,24,2304]{2,1,0:T(8,128)(2,1)S(1)}, u32[]{:S(2)}) copy-start(bf16[8,24,2304]{2,1,0:T(8,128)(2,1)S(1)} %all-to-all-done.2) | copy-start | bytes 2654212
  106.3 22.9 %copy-start.1 = (bf16[1,384,768]{2,1,0:T(8,128)(2,1)S(1)}, bf16[1,384,768]{2,1,0:T(8,128)(2,1)}, u32[]{:S(2)}) copy-start(bf16[1,384,768]{2,1,0:T(8,128)(2,1)} %param.14) | copy-start | bytes 1769476
  106.3 22.9 %copy-start.2 = (bf16[1,768]{1,0:T(2,128)(2,1)S(1)}, bf16[1,768]{1,0:T(2,128)(2,1)}, u32[]{:S(2)}) copy-start(bf16[1,768]{1,0:T(2,128)(2,1)} %refs_6_.1) | copy-start | bytes 4612
  106.3 22.9 %copy-start.3 = (bf16[1,768]{1,0:T(2,128)(2,1)S(1)}, bf16[1,768]{1,0:T(2,128)(2,1)}, u32[]{:S(2)}) copy-start(bf16[1,768]{1,0:T(2,128)(2,1)} %refs_8_.1) | copy-start | bytes 4612
  110.7 26.1 %all-to-all-start.3 = ((bf16[64,2,1152]{2,1,0:T(2,128)(2,1)}), bf16[64,2,1152]{2,1,0:T(2,128)(2,1)S(1)}, u32[]{:S(2)}, u32[]{:S(2)}) async-start(bf16[64,2,1152]{2,1,0:T(2,128)(2,1)} %get-tuple-element.20), calls=%async_computation.3 | async-start | bytes 589824 | tf_op jit(solution)/shard_map/all_to_all | solution.py:24
  123.8 5.3 %collective-permute-start.3 = (bf16[192,768]{1,0:T(8,128)(2,1)S(1)}, bf16[192,768]{1,0:T(8,128)(2,1)S(1)}, u32[]{:S(2)}, u32[]{:S(2)}) collective-permute-start(bf16[192,768]{1,0:T(8,128)(2,1)S(1)} %get-tuple-element.21), channel_id=1, source_target_pairs={{0,8},{8,0},{1,9},{9,1},{2,10},{10,2},{3,11},{11,3},{4,12},{12,4},... | collective-permute-start | bytes 884744 | tf_op jit(solution)/shard_map/ppermute | solution.py:20
  125.7 11.1 %copy-start.4 = (s32[4,4]{1,0:T(4,128)S(1)}, s32[4,4]{1,0:T(4,128)}, u32[]{:S(2)}) copy-start(s32[4,4]{1,0:T(4,128)} %ids_ref.3) | copy-start | bytes 196
  125.7 3.4 %collective-permute-start.4 = (bf16[192,384]{1,0:T(8,128)(2,1)S(1)}, bf16[192,384]{1,0:T(8,128)(2,1)S(1)}, u32[]{:S(2)}, u32[]{:S(2)}) collective-permute-start(bf16[192,384]{1,0:T(8,128)(2,1)S(1)} %get-tuple-element.22), channel_id=1, source_target_pairs={{0,8},{8,0},{1,9},{9,1},{2,10},{10,2},{3,11},{11,3},{4,12},{12,4},... | collective-permute-start | bytes 442376 | tf_op jit(solution)/shard_map/ppermute | solution.py:20

commit v9 on v8

--- a/solution.py
+++ b/solution.py
@@ -92,7 +92,7 @@
 
 def gather_kernel(
     parties, size, got_ref, own_ref, oth_in_ref, oth_out_ref, part_ref, rows_ref, gate_ref,
-    got, wide, own, oth, rows, part, gate, sems,
+    got, wide, own, oth, x, dy, part, gate, sems,
 ):
     width = own.shape[1]
     units = own.shape[0] - width
@@ -102,22 +102,25 @@
     copies[0].wait()
     wide[...] = got[...].astype(F32)
     copies += start_all([(oth_in_ref, oth.at[0:width, :]), (oth_out_ref, oth.at[width:half, :])], sems, 2)
+    for q, rows in enumerate((x, dy)):
+        for j in range(CAP):
+            for k in range(tiles):
+                value = wide[pl.ds((2 * j + q) * tiles + k, parties, stride=size), :]
+                rows[j * parties : (j + 1) * parties, k * LANE : (k + 1) * LANE] = value.astype(BF16)
     gates = wide[pl.ds(2 * tiles * CAP, parties, stride=size), :]
     for j in range(CAP):
-        at = slice(j * parties, (j + 1) * parties)
-        gate[at, :] = jnp.broadcast_to(gates[:, j : j + 1], (parties, LANE))
-        for k in range(2 * tiles):
-            value = wide[pl.ds(j * 2 * tiles + k, parties, stride=size), :]
-            rows[at, k * LANE : (k + 1) * LANE] = value.astype(BF16)
-    outs = start_all([(rows, rows_ref), (gate, gate_ref)], sems, 4)
+        gate[j * parties : (j + 1) * parties, :] = jnp.broadcast_to(gates[:, j : j + 1], (parties, LANE))
+    outs = start_all([(x, rows_ref.at[:, 0:width]), (dy, rows_ref.at[:, width : 2 * width]), (gate, gate_ref)], sems, 4)
     for n, weights in enumerate((own, oth)):
         wait_all(copies[n + 1 : 2 + 2 * n])
-        pre = dot(rows[:, :width], weights[:width, :], ((1,), (0,)))
-        part[:, n * half : n * half + width] = pre.astype(BF16)
-        back = dot(rows[:, width:], weights[width:, :], ((1,), (1,)))
-        part[:, n * half + width : (n + 1) * half] = back.astype(BF16)
-        cols = slice(n * half, (n + 1) * half)
-        outs += start_all([(part.at[:, cols], part_ref.at[:, cols])], sems, 6 + n)
+        for q in range(2):
+            if q == 0:
+                value, at = dot(x[...], weights[:width, :], ((1,), (0,))), n * half
+            else:
+                value, at = dot(dy[...], weights[width:, :], ((1,), (1,))), n * half + width
+            cols = slice(at, at + value.shape[1])
+            part[:, cols] = value.astype(BF16)
+            outs += start_all([(part.at[:, cols], part_ref.at[:, cols])], sems, 7 + 2 * n + q)
     wait_all(outs)
 
 
@@ -318,10 +321,11 @@
     rows = parties * CAP
     flat = got.reshape(parties * size, LANE)
     shapes = (array((rows, 2 * height)), array((rows, 2 * width)), array((rows, LANE), F32))
-    scratch = like(flat) + [(flat.shape, F32)] + like(own, own, shapes[1], shapes[0], shapes[2])
+    half = ((rows, width), BF16)
+    scratch = like(flat) + [(flat.shape, F32)] + like(own, own) + [half, half] + like(shapes[0], shapes[2])
     kernel = functools.partial(gather_kernel, parties, size)
     moved = 4 * own.size + 6 * got.size
-    return call(kernel, shapes, scratch, 6 + CORES, 4 * rows * own.size, moved, flat, own, oth_in, oth_out, limit=SNUG)
+    return call(kernel, shapes, scratch, 7 + 2 * CORES, 4 * rows * own.size, moved, flat, own, oth_in, oth_out, limit=SNUG)
 
 
 def scatter(after, full, own, oth, parties):

time: 139 us -> 139 us (level)
  the two profiles are of different devices: /device:TPU:16 before, /device:TPU:4 now
where the time goes in v9:
time: 139 us; the launch traced here: 138 us
  starting transfers between devices  59 us (42%)
  waiting for transfers between devices  58 us (42%)
  Pallas kernels  20.5 us (15%)
    all_to_all x4, waiting for transfers between devices, exchange(): return lax.all_to_all(x, axes, split_axis=0, concat_axis=0, tiled=True)  53.2 us
    all_to_all x4, starting transfers between devices, exchange(): return lax.all_to_all(x, axes, split_axis=0, concat_axis=0, tiled=True)  48.4 us
    pallas_call x7, Pallas kernels, call(): pl.pallas_call(kernel, out_shape=outs, in_specs=[SMEM if a.shape == (1,)...  20.5 us
    ppermute x5, starting transfers between devices, swap(): return lax.ppermute(x, 'core', [(0, 1), (1, 0)])  10.6 us
    ppermute x5, waiting for transfers between devices, swap(): return lax.ppermute(x, 'core', [(0, 1), (1, 0)])  4.78 us
  transfers between devices with their start and end apart: 9, of which 7 were waited for; matrix products, arithmetic and copies ran while one was open for 0% of the time, Pallas kernels for 6%

profile of v9, /device:TPU:4, one launch (start us, length us, event | category | flops | bytes accessed | tf_op | source)
XLA Modules:
  0.0 138.2 jit_solution(18218506942141863027)
XLA Ops:
  0.6 1.9 %shard_map.103 = bf16[8,8,40,128]{3,2,1,0:T(8,128)(2,1)} custom-call(s32[4,4]{1,0:T(4,128)} %ids_ref.3, bf16[4,4]{1,0:T(4,128)(2,1)} %gates_ref.1, bf16[4,768]{1,0:T(4,128)(2,1)} %tok_ref.1, bf16[4,768]{1,0:T(4,128)(2,1)} %cot_ref.1), custom_call_target="tpu_custom_call" | custom-call | flops 1048576 | bytes 1048576 | tf_op jit(solution)/shard_map/pallas_call | solution.py:276
  2.5 17.3 %all-to-all-start = ((bf16[64,40,128]{2,1,0:T(8,128)(2,1)}), bf16[64,40,128]{2,1,0:T(8,128)(2,1)S(1)}, u32[]{:S(2)}, u32[]{:S(2)}) async-start(bf16[64,40,128]{2,1,0:T(8,128)(2,1)} %bitcast.14), calls=%async_computation | async-start | bytes 1310720 | tf_op jit(solution)/shard_map/all_to_all | solution.py:24
  19.9 3.7 %shard_map.104 = (bf16[1152,768]{1,0:T(8,128)(2,1)}, bf16[768,768]{1,0:T(8,128)(2,1)}, bf16[384,768]{1,0:T(8,128)(2,1)}) custom-call(bf16[64,40,128]{2,1,0:T(8,128)(2,1)} %bitcast.15, bf16[768,768]{1,0:T(8,128)(2,1)} %bitcast.16, bf16[1,768]{1,0:T(2,128)(2,1)} %refs_6_.1, bf16[384,768]{1,0:T(8,128)(2,1)} %bitcast.12, bf16[1,768]{1,0:T(2,128)(2,1)} %refs_8_.1), custom_call_target="tpu_custom_call" | custom-call | flops 3538944 | bytes 3538944 | tf_op jit(solution)/shard_map/pallas_call | solution.py:276
  23.6 1.9 %collective-permute-start = (bf16[768,768]{1,0:T(8,128)(2,1)}, bf16[768,768]{1,0:T(8,128)(2,1)S(1)}, u32[]{:S(2)}, u32[]{:S(2)}) collective-permute-start(bf16[768,768]{1,0:T(8,128)(2,1)} %get-tuple-element.15), channel_id=1, source_target_pairs={{0,8},{8,0},{1,9},{9,1},{2,10},{10,2},{3,11},{11,3},{4,12},{12,4},... | collective-permute-start | bytes 3538952 | tf_op jit(solution)/shard_map/ppermute | solution.py:20
  25.5 2.4 %collective-permute-start.1 = (bf16[384,768]{1,0:T(8,128)(2,1)}, bf16[384,768]{1,0:T(8,128)(2,1)S(1)}, u32[]{:S(2)}, u32[]{:S(2)}) collective-permute-start(bf16[384,768]{1,0:T(8,128)(2,1)} %get-tuple-element.16), channel_id=1, source_target_pairs={{0,8},{8,0},{1,9},{9,1},{2,10},{10,2},{3,11},{11,3},{4,12},{12,4},... | collective-permute-start | bytes 1769480 | tf_op jit(solution)/shard_map/ppermute | solution.py:20
  27.9 1.8 %collective-permute-done.1.oth_out_ref = bf16[384,768]{1,0:T(8,128)(2,1)S(1)} collective-permute-done((bf16[384,768]{1,0:T(8,128)(2,1)}, bf16[384,768]{1,0:T(8,128)(2,1)S(1)}, u32[]{:S(2)}, u32[]{:S(2)}) %collective-permute-start.1) | collective-permute-done | bytes 589856 | tf_op jit(solution)/shard_map/ppermute | solution.py:20
  29.7 0.0 collective-permute-done.oth_in_ref.oth_ref
  29.7 0.0 copy-start.5
  29.7 8.6 %all-to-all-done = bf16[64,40,128]{2,1,0:T(8,128)(2,1)S(1)} async-done(((bf16[64,40,128]{2,1,0:T(8,128)(2,1)}), bf16[64,40,128]{2,1,0:T(8,128)(2,1)S(1)}, u32[]{:S(2)}, u32[]{:S(2)}) %all-to-all-start) | async-done | bytes 655392 | tf_op jit(solution)/shard_map/all_to_all | solution.py:24
  38.3 0.0 copy-done.5
  38.3 3.7 %shard_map.105 = (bf16[192,2304]{1,0:T(8,128)(2,1)}, bf16[192,1536]{1,0:T(8,128)(2,1)S(1)}, f32[192,128]{1,0:T(8,128)S(1)}) custom-call(bf16[2560,128]{1,0:T(8,128)(2,1)S(1)} %bitcast.11, bf16[1152,768]{1,0:T(8,128)(2,1)} %get-tuple-element.14.own_ref, bf16[768,768]{1,0:T(8,128)(2,1)} %copy-done.5, bf16[384,768]{1,0:T(8,128)(2,1)S(1)} %collective-permute-done.1.oth_out_ref), custom_call_target="tpu_custom_call" | custom-call | flops 679477248 | bytes 5505024 | tf_op jit(solution)/shard_map/pallas_call | solution.py:276
  42.1 16.7 %all-to-all-start.1 = ((bf16[8,24,2304]{2,1,0:T(8,128)(2,1)}), bf16[8,24,2304]{2,1,0:T(8,128)(2,1)S(1)}, u32[]{:S(2)}, u32[]{:S(2)}) async-start(bf16[8,24,2304]{2,1,0:T(8,128)(2,1)} %bitcast.5), calls=%async_computation.1 | async-start | bytes 1769472 | tf_op jit(solution)/shard_map/all_to_all | solution.py:24
  58.7 22.7 %all-to-all-done.1.parts_ref = bf16[8,24,2304]{2,1,0:T(8,128)(2,1)S(1)} async-done(((bf16[8,24,2304]{2,1,0:T(8,128)(2,1)}), bf16[8,24,2304]{2,1,0:T(8,128)(2,1)S(1)}, u32[]{:S(2)}, u32[]{:S(2)}) %all-to-all-start.1) | async-done | bytes 884768 | tf_op jit(solution)/shard_map/all_to_all | solution.py:24
  81.5 1.3 shard_map.106
  82.7 3.6 %all-to-all-start.2 = ((bf16[8,24,2304]{2,1,0:T(8,128)(2,1)}), bf16[8,24,2304]{2,1,0:T(8,128)(2,1)S(1)}, u32[]{:S(2)}, u32[]{:S(2)}) async-start(bf16[8,24,2304]{2,1,0:T(8,128)(2,1)} %shard_map.106), calls=%async_computation.2 | async-start | bytes 1769472 | tf_op jit(solution)/shard_map/all_to_all | solution.py:24
  86.3 1.9 %collective-permute-start.2 = (bf16[192,1536]{1,0:T(8,128)(2,1)S(1)}, bf16[192,1536]{1,0:T(8,128)(2,1)S(1)}, u32[]{:S(2)}, u32[]{:S(2)}) collective-permute-start(bf16[192,1536]{1,0:T(8,128)(2,1)S(1)} %get-tuple-element.17.refs_0_), channel_id=1, source_target_pairs={{0,8},{8,0},{1,9},{9,1},{2,10},{10,2},{3,11},{11,3},{4,12},{12,4},... | collective-permute-start | bytes 1769480 | tf_op jit(solution)/shard_map/ppermute | solution.py:20
  88.2 2.0 %collective-permute-done.2.after_ref.refs_1_ = bf16[192,1536]{1,0:T(8,128)(2,1)S(1)} collective-permute-done((bf16[192,1536]{1,0:T(8,128)(2,1)S(1)}, bf16[192,1536]{1,0:T(8,128)(2,1)S(1)}, u32[]{:S(2)}, u32[]{:S(2)}) %collective-permute-start.2) | collective-permute-done | bytes 589856 | tf_op jit(solution)/shard_map/ppermute | solution.py:20
  90.2 18.5 %all-to-all-done.2 = bf16[8,24,2304]{2,1,0:T(8,128)(2,1)S(1)} async-done(((bf16[8,24,2304]{2,1,0:T(8,128)(2,1)}), bf16[8,24,2304]{2,1,0:T(8,128)(2,1)S(1)}, u32[]{:S(2)}, u32[]{:S(2)}) %all-to-all-start.2) | async-done | bytes 884768 | tf_op jit(solution)/shard_map/all_to_all | solution.py:24
  108.7 0.0 copy-start
  108.7 0.0 copy-start.1
  108.7 0.0 copy-start.2
  108.7 0.0 copy-start.3
  108.7 4.4 %shard_map.107 = (bf16[64,2,1152]{2,1,0:T(2,128)(2,1)}, bf16[192,768]{1,0:T(8,128)(2,1)S(1)}, bf16[192,384]{1,0:T(8,128)(2,1)S(1)}) custom-call(bf16[192,1536]{1,0:T(8,128)(2,1)S(1)} %collective-permute-done.2.after_ref.refs_1_, bf16[192,2304]{1,0:T(8,128)(2,1)S(1)} %bitcast.9, bf16[1152,768]{1,0:T(8,128)(2,1)} %get-tuple-element.14.own_ref, ...), custom_call_target="tpu_custom_call" | custom-call | flops 452984832 | bytes 3538944 | tf_op jit(solution)/shard_map/pallas_call | solution.py:276
  113.1 0.0 copy-done
  113.1 10.8 %all-to-all-start.3 = ((bf16[64,2,1152]{2,1,0:T(2,128)(2,1)}), bf16[64,2,1152]{2,1,0:T(2,128)(2,1)S(1)}, u32[]{:S(2)}, u32[]{:S(2)}) async-start(bf16[64,2,1152]{2,1,0:T(2,128)(2,1)} %get-tuple-element.20), calls=%async_computation.3 | async-start | bytes 589824 | tf_op jit(solution)/shard_map/all_to_all | solution.py:24
  123.9 1.9 %collective-permute-start.3 = (bf16[192,768]{1,0:T(8,128)(2,1)S(1)}, bf16[192,768]{1,0:T(8,128)(2,1)S(1)}, u32[]{:S(2)}, u32[]{:S(2)}) collective-permute-start(bf16[192,768]{1,0:T(8,128)(2,1)S(1)} %get-tuple-element.21), channel_id=1, source_target_pairs={{0,8},{8,0},{1,9},{9,1},{2,10},{10,2},{3,11},{11,3},{4,12},{12,4},... | collective-permute-start | bytes 884744 | tf_op jit(solution)/shard_map/ppermute | solution.py:20
  125.8 0.0 copy-start.4
  125.8 2.4 %collective-permute-start.4 = (bf16[192,384]{1,0:T(8,128)(2,1)S(1)}, bf16[192,384]{1,0:T(8,128)(2,1)S(1)}, u32[]{:S(2)}, u32[]{:S(2)}) collective-permute-start(bf16[192,384]{1,0:T(8,128)(2,1)S(1)} %get-tuple-element.22), channel_id=1, source_target_pairs={{0,8},{8,0},{1,9},{9,1},{2,10},{10,2},{3,11},{11,3},{4,12},{12,4},... | collective-permute-start | bytes 442376 | tf_op jit(solution)/shard_map/ppermute | solution.py:20
  128.3 1.0 collective-permute-done.4.refs_4_
  129.2 0.0 collective-permute-done.3.refs_3_
  129.2 0.0 copy-done.1
  129.3 0.0 copy-done.2
  129.3 0.0 copy-done.3
  129.3 4.0 %shard_map.109 = (bf16[768,768]{1,0:T(8,128)(2,1)}, bf16[384,768]{1,0:T(8,128)(2,1)}) custom-call(bf16[192,1536]{1,0:T(8,128)(2,1)S(1)} %get-tuple-element.17.refs_0_, bf16[192,1536]{1,0:T(8,128)(2,1)S(1)} %collective-permute-done.2.after_ref.refs_1_, bf16[192,2304]{1,0:T(8,128)(2,1)} %bitcast.10, bf16[192,768]{1,0:T(8,128)(2,1)S(1)} %collective-permute-done.3.refs_3_, ...), custom_call_target="tpu_custom_call" | custom-call | flops 1048576 | bytes 1048576 | tf_op jit(solution)/shard_map/pallas_call | solution.py:276
  133.2 3.4 %all-to-all-done.3.back_ref = bf16[64,2,1152]{2,1,0:T(2,128)(2,1)S(1)} async-done(((bf16[64,2,1152]{2,1,0:T(2,128)(2,1)}), bf16[64,2,1152]{2,1,0:T(2,128)(2,1)S(1)}, u32[]{:S(2)}, u32[]{:S(2)}) %all-to-all-start.3) | async-done | bytes 294944 | tf_op jit(solution)/shard_map/all_to_all | solution.py:24
  136.6 0.0 copy-done.4
  136.6 1.6 %shard_map.108 = bf16[4,768]{1,0:T(4,128)(2,1)} custom-call(s32[4,4]{1,0:T(4,128)S(1)} %copy-done.4, bf16[64,2,1152]{2,1,0:T(2,128)(2,1)S(1)} %all-to-all-done.3.back_ref), custom_call_target="tpu_custom_call" | custom-call | flops 1048576 | bytes 1048576 | tf_op jit(solution)/shard_map/pallas_call | solution.py:276
Async XLA Ops:
  2.5 35.8 %all-to-all-start = ((bf16[64,40,128]{2,1,0:T(8,128)(2,1)}), bf16[64,40,128]{2,1,0:T(8,128)(2,1)S(1)}, u32[]{:S(2)}, u32[]{:S(2)}) async-start(bf16[64,40,128]{2,1,0:T(8,128)(2,1)} %bitcast.14), calls=%async_computation | async-start | bytes 1310720 | tf_op jit(solution)/shard_map/all_to_all | solution.py:24
  23.6 6.2 %collective-permute-start = (bf16[768,768]{1,0:T(8,128)(2,1)}, bf16[768,768]{1,0:T(8,128)(2,1)S(1)}, u32[]{:S(2)}, u32[]{:S(2)}) collective-permute-start(bf16[768,768]{1,0:T(8,128)(2,1)} %get-tuple-element.15), channel_id=1, source_target_pairs={{0,8},{8,0},{1,9},{9,1},{2,10},{10,2},{3,11},{11,3},{4,12},{12,4},... | collective-permute-start | bytes 3538952 | tf_op jit(solution)/shard_map/ppermute | solution.py:20
  25.5 4.2 %collective-permute-start.1 = (bf16[384,768]{1,0:T(8,128)(2,1)}, bf16[384,768]{1,0:T(8,128)(2,1)S(1)}, u32[]{:S(2)}, u32[]{:S(2)}) collective-permute-start(bf16[384,768]{1,0:T(8,128)(2,1)} %get-tuple-element.16), channel_id=1, source_target_pairs={{0,8},{8,0},{1,9},{9,1},{2,10},{10,2},{3,11},{11,3},{4,12},{12,4},... | collective-permute-start | bytes 1769480 | tf_op jit(solution)/shard_map/ppermute | solution.py:20
  29.7 8.6 %copy-start.5 = (bf16[768,768]{1,0:T(8,128)(2,1)}, bf16[768,768]{1,0:T(8,128)(2,1)S(1)}, u32[]{:S(2)}) copy-start(bf16[768,768]{1,0:T(8,128)(2,1)S(1)} %collective-permute-done.oth_in_ref.oth_ref) | copy-start | bytes 3538948
  42.1 39.4 %all-to-all-start.1 = ((bf16[8,24,2304]{2,1,0:T(8,128)(2,1)}), bf16[8,24,2304]{2,1,0:T(8,128)(2,1)S(1)}, u32[]{:S(2)}, u32[]{:S(2)}) async-start(bf16[8,24,2304]{2,1,0:T(8,128)(2,1)} %bitcast.5), calls=%async_computation.1 | async-start | bytes 1769472 | tf_op jit(solution)/shard_map/all_to_all | solution.py:24
  82.7 25.9 %all-to-all-start.2 = ((bf16[8,24,2304]{2,1,0:T(8,128)(2,1)}), bf16[8,24,2304]{2,1,0:T(8,128)(2,1)S(1)}, u32[]{:S(2)}, u32[]{:S(2)}) async-start(bf16[8,24,2304]{2,1,0:T(8,128)(2,1)} %shard_map.106), calls=%async_computation.2 | async-start | bytes 1769472 | tf_op jit(solution)/shard_map/all_to_all | solution.py:24
  86.3 3.9 %collective-permute-start.2 = (bf16[192,1536]{1,0:T(8,128)(2,1)S(1)}, bf16[192,1536]{1,0:T(8,128)(2,1)S(1)}, u32[]{:S(2)}, u32[]{:S(2)}) collective-permute-start(bf16[192,1536]{1,0:T(8,128)(2,1)S(1)} %get-tuple-element.17.refs_0_), channel_id=1, source_target_pairs={{0,8},{8,0},{1,9},{9,1},{2,10},{10,2},{3,11},{11,3},{4,12},{12,4},... | collective-permute-start | bytes 1769480 | tf_op jit(solution)/shard_map/ppermute | solution.py:20
  108.7 4.4 %copy-start = (bf16[8,24,2304]{2,1,0:T(8,128)(2,1)}, bf16[8,24,2304]{2,1,0:T(8,128)(2,1)S(1)}, u32[]{:S(2)}) copy-start(bf16[8,24,2304]{2,1,0:T(8,128)(2,1)S(1)} %all-to-all-done.2) | copy-start | bytes 2654212
  108.7 20.6 %copy-start.1 = (bf16[1,384,768]{2,1,0:T(8,128)(2,1)S(1)}, bf16[1,384,768]{2,1,0:T(8,128)(2,1)}, u32[]{:S(2)}) copy-start(bf16[1,384,768]{2,1,0:T(8,128)(2,1)} %param.14) | copy-start | bytes 1769476
  108.7 20.6 %copy-start.2 = (bf16[1,768]{1,0:T(2,128)(2,1)S(1)}, bf16[1,768]{1,0:T(2,128)(2,1)}, u32[]{:S(2)}) copy-start(bf16[1,768]{1,0:T(2,128)(2,1)} %refs_6_.1) | copy-start | bytes 4612
  108.7 20.6 %copy-start.3 = (bf16[1,768]{1,0:T(2,128)(2,1)S(1)}, bf16[1,768]{1,0:T(2,128)(2,1)}, u32[]{:S(2)}) copy-start(bf16[1,768]{1,0:T(2,128)(2,1)} %refs_8_.1) | copy-start | bytes 4612
  113.1 23.5 %all-to-all-start.3 = ((bf16[64,2,1152]{2,1,0:T(2,128)(2,1)}), bf16[64,2,1152]{2,1,0:T(2,128)(2,1)S(1)}, u32[]{:S(2)}, u32[]{:S(2)}) async-start(bf16[64,2,1152]{2,1,0:T(2,128)(2,1)} %get-tuple-element.20), calls=%async_computation.3 | async-start | bytes 589824 | tf_op jit(solution)/shard_map/all_to_all | solution.py:24
  123.9 5.3 %collective-permute-start.3 = (bf16[192,768]{1,0:T(8,128)(2,1)S(1)}, bf16[192,768]{1,0:T(8,128)(2,1)S(1)}, u32[]{:S(2)}, u32[]{:S(2)}) collective-permute-start(bf16[192,768]{1,0:T(8,128)(2,1)S(1)} %get-tuple-element.21), channel_id=1, source_target_pairs={{0,8},{8,0},{1,9},{9,1},{2,10},{10,2},{3,11},{11,3},{4,12},{12,4},... | collective-permute-start | bytes 884744 | tf_op jit(solution)/shard_map/ppermute | solution.py:20
  125.8 10.8 %copy-start.4 = (s32[4,4]{1,0:T(4,128)S(1)}, s32[4,4]{1,0:T(4,128)}, u32[]{:S(2)}) copy-start(s32[4,4]{1,0:T(4,128)} %ids_ref.3) | copy-start | bytes 196
  125.8 3.4 %collective-permute-start.4 = (bf16[192,384]{1,0:T(8,128)(2,1)S(1)}, bf16[192,384]{1,0:T(8,128)(2,1)S(1)}, u32[]{:S(2)}, u32[]{:S(2)}) collective-permute-start(bf16[192,384]{1,0:T(8,128)(2,1)S(1)} %get-tuple-element.22), channel_id=1, source_target_pairs={{0,8},{8,0},{1,9},{9,1},{2,10},{10,2},{3,11},{11,3},{4,12},{12,4},... | collective-permute-start | bytes 442376 | tf_op jit(solution)/shard_map/ppermute | solution.py:20

commit v10 on v8

--- a/solution.py
+++ b/solution.py
@@ -175,10 +175,9 @@
     wait_all(outs)
 
 
-def place(n, ref):
-    tiles = ref.shape[2] // LANE
-    at = n % tiles * LANE
-    return n // tiles, slice(at, at + LANE)
+def place(j, k):
+    at = (k // 2 * CAP + j) * LANE
+    return k % 2, slice(at, at + LANE)
 
 
 def scatter_kernel(
@@ -187,8 +186,8 @@
     del after_ref
     width = own.shape[0]
     hidden = own.shape[1]
-    tiles = width // LANE
     step = width // PIECES
+    span = out.shape[2] // PIECES
     copies = start_all(
         [
             (full_ref.at[:, 0:hidden], dh.at[0]),
@@ -209,10 +208,12 @@
         dx = dot(dh[0], own[at, :], ((1,), (1,))) + dot(dh[1], oth[at, :], ((1,), (1,)))
         for j in range(CAP):
             for k in range(step // LANE):
-                row, cols = place(j * tiles + p * (step // LANE) + k, wide)
+                row, cols = place(j, p * (step // LANE) + k)
                 wide[:, row, cols] = dx[j * parties : (j + 1) * parties, k * LANE : (k + 1) * LANE]
-    out[...] = wide[...].astype(BF16)
-    wait_all(outs + start_all([(out, out_ref)], sems, 5 + 2 * PIECES))
+        cols = slice(p * span, (p + 1) * span)
+        out[:, :, cols] = wide[:, :, cols].astype(BF16)
+        outs += start_all([(out.at[:, :, cols], out_ref.at[:, :, cols])], sems, 5 + 2 * PIECES + p)
+    wait_all(outs)
 
 
 def grads_kernel(step, *refs):
@@ -252,7 +253,7 @@
     for k in range(tiles):
         totals = [jnp.zeros((1, LANE), F32) for _ in range(tok_rows)]
         for j in range(CAP):
-            row, cols = place(j * tiles + k, wide)
+            row, cols = place(j, k)
             value = wide[:, row, cols]
             value = jnp.sum(value.reshape(n_expert, n_y, LANE), axis=1)
             for i in range(tok_rows):
@@ -333,7 +334,7 @@
     scratch = [((2, rows, hidden), BF16)] + like(shapes[2], oth, oth) + [(flat.shape, F32), (flat.shape, BF16)]
     kernel = functools.partial(scatter_kernel, parties, height)
     flops, moved = 4 * rows * width * hidden, 4 * own.size
-    return call(kernel, shapes, scratch, 6 + 2 * PIECES, flops, moved, after, full, own, oth, limit=SNUG)
+    return call(kernel, shapes, scratch, 5 + 3 * PIECES, flops, moved, after, full, own, oth, limit=SNUG)
 
 
 def weight_grads(mine, theirs, full, dh, act, w_in, scale_in, w_out, scale_out):

time: 139 us -> 139 us (level)
  the two profiles are of different devices: /device:TPU:16 before, /device:TPU:4 now
where the time goes in v10:
time: 139 us; the launch traced here: 138 us
  starting transfers between devices  59 us (42%)
  waiting for transfers between devices  57.9 us (42%)
  Pallas kernels  20.6 us (15%)
    all_to_all x4, waiting for transfers between devices, exchange(): return lax.all_to_all(x, axes, split_axis=0, concat_axis=0, tiled=True)  53.2 us
    all_to_all x4, starting transfers between devices, exchange(): return lax.all_to_all(x, axes, split_axis=0, concat_axis=0, tiled=True)  48.4 us
    pallas_call x7, Pallas kernels, call(): pl.pallas_call(kernel, out_shape=outs, in_specs=[SMEM if a.shape == (1,)...  20.6 us
    ppermute x5, starting transfers between devices, swap(): return lax.ppermute(x, 'core', [(0, 1), (1, 0)])  10.6 us
    ppermute x5, waiting for transfers between devices, swap(): return lax.ppermute(x, 'core', [(0, 1), (1, 0)])  4.78 us
  transfers between devices with their start and end apart: 9, of which 7 were waited for; matrix products, arithmetic and copies ran while one was open for 0% of the time, Pallas kernels for 6%

profile of v10, /device:TPU:4, one launch (start us, length us, event | category | flops | bytes accessed | tf_op | source)
XLA Modules:
  0.0 138.3 jit_solution(12708364194524846458)
XLA Ops:
  0.6 1.9 %shard_map.103 = bf16[8,8,40,128]{3,2,1,0:T(8,128)(2,1)} custom-call(s32[4,4]{1,0:T(4,128)} %ids_ref.3, bf16[4,4]{1,0:T(4,128)(2,1)} %gates_ref.1, bf16[4,768]{1,0:T(4,128)(2,1)} %tok_ref.1, bf16[4,768]{1,0:T(4,128)(2,1)} %cot_ref.1), custom_call_target="tpu_custom_call" | custom-call | flops 1048576 | bytes 1048576 | tf_op jit(solution)/shard_map/pallas_call | solution.py:274
  2.5 17.3 %all-to-all-start = ((bf16[64,40,128]{2,1,0:T(8,128)(2,1)}), bf16[64,40,128]{2,1,0:T(8,128)(2,1)S(1)}, u32[]{:S(2)}, u32[]{:S(2)}) async-start(bf16[64,40,128]{2,1,0:T(8,128)(2,1)} %bitcast.14), calls=%async_computation | async-start | bytes 1310720 | tf_op jit(solution)/shard_map/all_to_all | solution.py:24
  19.9 3.7 %shard_map.104 = (bf16[1152,768]{1,0:T(8,128)(2,1)}, bf16[768,768]{1,0:T(8,128)(2,1)}, bf16[384,768]{1,0:T(8,128)(2,1)}) custom-call(bf16[64,40,128]{2,1,0:T(8,128)(2,1)} %bitcast.15, bf16[768,768]{1,0:T(8,128)(2,1)} %bitcast.16, bf16[1,768]{1,0:T(2,128)(2,1)} %refs_6_.1, bf16[384,768]{1,0:T(8,128)(2,1)} %bitcast.12, bf16[1,768]{1,0:T(2,128)(2,1)} %refs_8_.1), custom_call_target="tpu_custom_call" | custom-call | flops 3538944 | bytes 3538944 | tf_op jit(solution)/shard_map/pallas_call | solution.py:274
  23.6 1.9 %collective-permute-start = (bf16[768,768]{1,0:T(8,128)(2,1)}, bf16[768,768]{1,0:T(8,128)(2,1)S(1)}, u32[]{:S(2)}, u32[]{:S(2)}) collective-permute-start(bf16[768,768]{1,0:T(8,128)(2,1)} %get-tuple-element.15), channel_id=1, source_target_pairs={{0,8},{8,0},{1,9},{9,1},{2,10},{10,2},{3,11},{11,3},{4,12},{12,4},... | collective-permute-start | bytes 3538952 | tf_op jit(solution)/shard_map/ppermute | solution.py:20
  25.5 2.4 %collective-permute-start.1 = (bf16[384,768]{1,0:T(8,128)(2,1)}, bf16[384,768]{1,0:T(8,128)(2,1)S(1)}, u32[]{:S(2)}, u32[]{:S(2)}) collective-permute-start(bf16[384,768]{1,0:T(8,128)(2,1)} %get-tuple-element.16), channel_id=1, source_target_pairs={{0,8},{8,0},{1,9},{9,1},{2,10},{10,2},{3,11},{11,3},{4,12},{12,4},... | collective-permute-start | bytes 1769480 | tf_op jit(solution)/shard_map/ppermute | solution.py:20
  27.9 1.8 %collective-permute-done.1.oth_out_ref = bf16[384,768]{1,0:T(8,128)(2,1)S(1)} collective-permute-done((bf16[384,768]{1,0:T(8,128)(2,1)}, bf16[384,768]{1,0:T(8,128)(2,1)S(1)}, u32[]{:S(2)}, u32[]{:S(2)}) %collective-permute-start.1) | collective-permute-done | bytes 589856 | tf_op jit(solution)/shard_map/ppermute | solution.py:20
  29.7 0.0 collective-permute-done.oth_in_ref.oth_ref
  29.7 0.0 copy-start.5
  29.7 8.6 %all-to-all-done = bf16[64,40,128]{2,1,0:T(8,128)(2,1)S(1)} async-done(((bf16[64,40,128]{2,1,0:T(8,128)(2,1)}), bf16[64,40,128]{2,1,0:T(8,128)(2,1)S(1)}, u32[]{:S(2)}, u32[]{:S(2)}) %all-to-all-start) | async-done | bytes 655392 | tf_op jit(solution)/shard_map/all_to_all | solution.py:24
  38.3 0.0 copy-done.5
  38.3 3.8 %shard_map.105 = (bf16[192,2304]{1,0:T(8,128)(2,1)}, bf16[192,1536]{1,0:T(8,128)(2,1)S(1)}, f32[192,128]{1,0:T(8,128)S(1)}) custom-call(bf16[2560,128]{1,0:T(8,128)(2,1)S(1)} %bitcast.11, bf16[1152,768]{1,0:T(8,128)(2,1)} %get-tuple-element.14.own_ref, bf16[768,768]{1,0:T(8,128)(2,1)} %copy-done.5, bf16[384,768]{1,0:T(8,128)(2,1)S(1)} %collective-permute-done.1.oth_out_ref), custom_call_target="tpu_custom_call" | custom-call | flops 679477248 | bytes 5505024 | tf_op jit(solution)/shard_map/pallas_call | solution.py:274
  42.2 16.7 %all-to-all-start.1 = ((bf16[8,24,2304]{2,1,0:T(8,128)(2,1)}), bf16[8,24,2304]{2,1,0:T(8,128)(2,1)S(1)}, u32[]{:S(2)}, u32[]{:S(2)}) async-start(bf16[8,24,2304]{2,1,0:T(8,128)(2,1)} %bitcast.5), calls=%async_computation.1 | async-start | bytes 1769472 | tf_op jit(solution)/shard_map/all_to_all | solution.py:24
  58.8 22.7 %all-to-all-done.1.parts_ref = bf16[8,24,2304]{2,1,0:T(8,128)(2,1)S(1)} async-done(((bf16[8,24,2304]{2,1,0:T(8,128)(2,1)}), bf16[8,24,2304]{2,1,0:T(8,128)(2,1)S(1)}, u32[]{:S(2)}, u32[]{:S(2)}) %all-to-all-start.1) | async-done | bytes 884768 | tf_op jit(solution)/shard_map/all_to_all | solution.py:24
  81.5 1.3 shard_map.106
  82.8 3.6 %all-to-all-start.2 = ((bf16[8,24,2304]{2,1,0:T(8,128)(2,1)}), bf16[8,24,2304]{2,1,0:T(8,128)(2,1)S(1)}, u32[]{:S(2)}, u32[]{:S(2)}) async-start(bf16[8,24,2304]{2,1,0:T(8,128)(2,1)} %shard_map.106), calls=%async_computation.2 | async-start | bytes 1769472 | tf_op jit(solution)/shard_map/all_to_all | solution.py:24
  86.4 1.9 %collective-permute-start.2 = (bf16[192,1536]{1,0:T(8,128)(2,1)S(1)}, bf16[192,1536]{1,0:T(8,128)(2,1)S(1)}, u32[]{:S(2)}, u32[]{:S(2)}) collective-permute-start(bf16[192,1536]{1,0:T(8,128)(2,1)S(1)} %get-tuple-element.17.refs_0_), channel_id=1, source_target_pairs={{0,8},{8,0},{1,9},{9,1},{2,10},{10,2},{3,11},{11,3},{4,12},{12,4},... | collective-permute-start | bytes 1769480 | tf_op jit(solution)/shard_map/ppermute | solution.py:20
  88.3 2.0 %collective-permute-done.2.after_ref.refs_1_ = bf16[192,1536]{1,0:T(8,128)(2,1)S(1)} collective-permute-done((bf16[192,1536]{1,0:T(8,128)(2,1)S(1)}, bf16[192,1536]{1,0:T(8,128)(2,1)S(1)}, u32[]{:S(2)}, u32[]{:S(2)}) %collective-permute-start.2) | collective-permute-done | bytes 589856 | tf_op jit(solution)/shard_map/ppermute | solution.py:20
  90.3 18.5 %all-to-all-done.2 = bf16[8,24,2304]{2,1,0:T(8,128)(2,1)S(1)} async-done(((bf16[8,24,2304]{2,1,0:T(8,128)(2,1)}), bf16[8,24,2304]{2,1,0:T(8,128)(2,1)S(1)}, u32[]{:S(2)}, u32[]{:S(2)}) %all-to-all-start.2) | async-done | bytes 884768 | tf_op jit(solution)/shard_map/all_to_all | solution.py:24
  108.8 0.0 copy-start
  108.8 0.0 copy-start.1
  108.8 0.0 copy-start.2
  108.8 0.0 copy-start.3
  108.8 4.4 %shard_map.107 = (bf16[64,2,1152]{2,1,0:T(2,128)(2,1)}, bf16[192,768]{1,0:T(8,128)(2,1)S(1)}, bf16[192,384]{1,0:T(8,128)(2,1)S(1)}) custom-call(bf16[192,1536]{1,0:T(8,128)(2,1)S(1)} %collective-permute-done.2.after_ref.refs_1_, bf16[192,2304]{1,0:T(8,128)(2,1)S(1)} %bitcast.9, bf16[1152,768]{1,0:T(8,128)(2,1)} %get-tuple-element.14.own_ref, ...), custom_call_target="tpu_custom_call" | custom-call | flops 452984832 | bytes 3538944 | tf_op jit(solution)/shard_map/pallas_call | solution.py:274
  113.1 0.0 copy-done
  113.1 10.8 %all-to-all-start.3 = ((bf16[64,2,1152]{2,1,0:T(2,128)(2,1)}), bf16[64,2,1152]{2,1,0:T(2,128)(2,1)S(1)}, u32[]{:S(2)}, u32[]{:S(2)}) async-start(bf16[64,2,1152]{2,1,0:T(2,128)(2,1)} %get-tuple-element.20), calls=%async_computation.3 | async-start | bytes 589824 | tf_op jit(solution)/shard_map/all_to_all | solution.py:24
  124.0 1.9 %collective-permute-start.3 = (bf16[192,768]{1,0:T(8,128)(2,1)S(1)}, bf16[192,768]{1,0:T(8,128)(2,1)S(1)}, u32[]{:S(2)}, u32[]{:S(2)}) collective-permute-start(bf16[192,768]{1,0:T(8,128)(2,1)S(1)} %get-tuple-element.21), channel_id=1, source_target_pairs={{0,8},{8,0},{1,9},{9,1},{2,10},{10,2},{3,11},{11,3},{4,12},{12,4},... | collective-permute-start | bytes 884744 | tf_op jit(solution)/shard_map/ppermute | solution.py:20
  125.9 0.0 copy-start.4
  125.9 2.4 %collective-permute-start.4 = (bf16[192,384]{1,0:T(8,128)(2,1)S(1)}, bf16[192,384]{1,0:T(8,128)(2,1)S(1)}, u32[]{:S(2)}, u32[]{:S(2)}) collective-permute-start(bf16[192,384]{1,0:T(8,128)(2,1)S(1)} %get-tuple-element.22), channel_id=1, source_target_pairs={{0,8},{8,0},{1,9},{9,1},{2,10},{10,2},{3,11},{11,3},{4,12},{12,4},... | collective-permute-start | bytes 442376 | tf_op jit(solution)/shard_map/ppermute | solution.py:20
  128.3 1.0 collective-permute-done.4.refs_4_
  129.3 0.0 collective-permute-done.3.refs_3_
  129.3 0.0 copy-done.1
  129.3 0.0 copy-done.2
  129.3 0.0 copy-done.3
  129.3 4.0 %shard_map.109 = (bf16[768,768]{1,0:T(8,128)(2,1)}, bf16[384,768]{1,0:T(8,128)(2,1)}) custom-call(bf16[192,1536]{1,0:T(8,128)(2,1)S(1)} %get-tuple-element.17.refs_0_, bf16[192,1536]{1,0:T(8,128)(2,1)S(1)} %collective-permute-done.2.after_ref.refs_1_, bf16[192,2304]{1,0:T(8,128)(2,1)} %bitcast.10, bf16[192,768]{1,0:T(8,128)(2,1)S(1)} %collective-permute-done.3.refs_3_, ...), custom_call_target="tpu_custom_call" | custom-call | flops 1048576 | bytes 1048576 | tf_op jit(solution)/shard_map/pallas_call | solution.py:274
  133.3 3.4 %all-to-all-done.3.back_ref = bf16[64,2,1152]{2,1,0:T(2,128)(2,1)S(1)} async-done(((bf16[64,2,1152]{2,1,0:T(2,128)(2,1)}), bf16[64,2,1152]{2,1,0:T(2,128)(2,1)S(1)}, u32[]{:S(2)}, u32[]{:S(2)}) %all-to-all-start.3) | async-done | bytes 294944 | tf_op jit(solution)/shard_map/all_to_all | solution.py:24
  136.7 0.0 copy-done.4
  136.7 1.6 %shard_map.108 = bf16[4,768]{1,0:T(4,128)(2,1)} custom-call(s32[4,4]{1,0:T(4,128)S(1)} %copy-done.4, bf16[64,2,1152]{2,1,0:T(2,128)(2,1)S(1)} %all-to-all-done.3.back_ref), custom_call_target="tpu_custom_call" | custom-call | flops 1048576 | bytes 1048576 | tf_op jit(solution)/shard_map/pallas_call | solution.py:274
Async XLA Ops:
  2.5 35.8 %all-to-all-start = ((bf16[64,40,128]{2,1,0:T(8,128)(2,1)}), bf16[64,40,128]{2,1,0:T(8,128)(2,1)S(1)}, u32[]{:S(2)}, u32[]{:S(2)}) async-start(bf16[64,40,128]{2,1,0:T(8,128)(2,1)} %bitcast.14), calls=%async_computation | async-start | bytes 1310720 | tf_op jit(solution)/shard_map/all_to_all | solution.py:24
  23.6 6.2 %collective-permute-start = (bf16[768,768]{1,0:T(8,128)(2,1)}, bf16[768,768]{1,0:T(8,128)(2,1)S(1)}, u32[]{:S(2)}, u32[]{:S(2)}) collective-permute-start(bf16[768,768]{1,0:T(8,128)(2,1)} %get-tuple-element.15), channel_id=1, source_target_pairs={{0,8},{8,0},{1,9},{9,1},{2,10},{10,2},{3,11},{11,3},{4,12},{12,4},... | collective-permute-start | bytes 3538952 | tf_op jit(solution)/shard_map/ppermute | solution.py:20
  25.5 4.2 %collective-permute-start.1 = (bf16[384,768]{1,0:T(8,128)(2,1)}, bf16[384,768]{1,0:T(8,128)(2,1)S(1)}, u32[]{:S(2)}, u32[]{:S(2)}) collective-permute-start(bf16[384,768]{1,0:T(8,128)(2,1)} %get-tuple-element.16), channel_id=1, source_target_pairs={{0,8},{8,0},{1,9},{9,1},{2,10},{10,2},{3,11},{11,3},{4,12},{12,4},... | collective-permute-start | bytes 1769480 | tf_op jit(solution)/shard_map/ppermute | solution.py:20
  29.7 8.6 %copy-start.5 = (bf16[768,768]{1,0:T(8,128)(2,1)}, bf16[768,768]{1,0:T(8,128)(2,1)S(1)}, u32[]{:S(2)}) copy-start(bf16[768,768]{1,0:T(8,128)(2,1)S(1)} %collective-permute-done.oth_in_ref.oth_ref) | copy-start | bytes 3538948
  42.2 39.4 %all-to-all-start.1 = ((bf16[8,24,2304]{2,1,0:T(8,128)(2,1)}), bf16[8,24,2304]{2,1,0:T(8,128)(2,1)S(1)}, u32[]{:S(2)}, u32[]{:S(2)}) async-start(bf16[8,24,2304]{2,1,0:T(8,128)(2,1)} %bitcast.5), calls=%async_computation.1 | async-start | bytes 1769472 | tf_op jit(solution)/shard_map/all_to_all | solution.py:24
  82.8 25.9 %all-to-all-start.2 = ((bf16[8,24,2304]{2,1,0:T(8,128)(2,1)}), bf16[8,24,2304]{2,1,0:T(8,128)(2,1)S(1)}, u32[]{:S(2)}, u32[]{:S(2)}) async-start(bf16[8,24,2304]{2,1,0:T(8,128)(2,1)} %shard_map.106), calls=%async_computation.2 | async-start | bytes 1769472 | tf_op jit(solution)/shard_map/all_to_all | solution.py:24
  86.4 3.9 %collective-permute-start.2 = (bf16[192,1536]{1,0:T(8,128)(2,1)S(1)}, bf16[192,1536]{1,0:T(8,128)(2,1)S(1)}, u32[]{:S(2)}, u32[]{:S(2)}) collective-permute-start(bf16[192,1536]{1,0:T(8,128)(2,1)S(1)} %get-tuple-element.17.refs_0_), channel_id=1, source_target_pairs={{0,8},{8,0},{1,9},{9,1},{2,10},{10,2},{3,11},{11,3},{4,12},{12,4},... | collective-permute-start | bytes 1769480 | tf_op jit(solution)/shard_map/ppermute | solution.py:20
  108.8 4.4 %copy-start = (bf16[8,24,2304]{2,1,0:T(8,128)(2,1)}, bf16[8,24,2304]{2,1,0:T(8,128)(2,1)S(1)}, u32[]{:S(2)}) copy-start(bf16[8,24,2304]{2,1,0:T(8,128)(2,1)S(1)} %all-to-all-done.2) | copy-start | bytes 2654212
  108.8 20.6 %copy-start.1 = (bf16[1,384,768]{2,1,0:T(8,128)(2,1)S(1)}, bf16[1,384,768]{2,1,0:T(8,128)(2,1)}, u32[]{:S(2)}) copy-start(bf16[1,384,768]{2,1,0:T(8,128)(2,1)} %param.14) | copy-start | bytes 1769476
  108.8 20.6 %copy-start.2 = (bf16[1,768]{1,0:T(2,128)(2,1)S(1)}, bf16[1,768]{1,0:T(2,128)(2,1)}, u32[]{:S(2)}) copy-start(bf16[1,768]{1,0:T(2,128)(2,1)} %refs_6_.1) | copy-start | bytes 4612
  108.8 20.6 %copy-start.3 = (bf16[1,768]{1,0:T(2,128)(2,1)S(1)}, bf16[1,768]{1,0:T(2,128)(2,1)}, u32[]{:S(2)}) copy-start(bf16[1,768]{1,0:T(2,128)(2,1)} %refs_8_.1) | copy-start | bytes 4612
  113.1 23.5 %all-to-all-start.3 = ((bf16[64,2,1152]{2,1,0:T(2,128)(2,1)}), bf16[64,2,1152]{2,1,0:T(2,128)(2,1)S(1)}, u32[]{:S(2)}, u32[]{:S(2)}) async-start(bf16[64,2,1152]{2,1,0:T(2,128)(2,1)} %get-tuple-element.20), calls=%async_computation.3 | async-start | bytes 589824 | tf_op jit(solution)/shard_map/all_to_all | solution.py:24
  124.0 5.3 %collective-permute-start.3 = (bf16[192,768]{1,0:T(8,128)(2,1)S(1)}, bf16[192,768]{1,0:T(8,128)(2,1)S(1)}, u32[]{:S(2)}, u32[]{:S(2)}) collective-permute-start(bf16[192,768]{1,0:T(8,128)(2,1)S(1)} %get-tuple-element.21), channel_id=1, source_target_pairs={{0,8},{8,0},{1,9},{9,1},{2,10},{10,2},{3,11},{11,3},{4,12},{12,4},... | collective-permute-start | bytes 884744 | tf_op jit(solution)/shard_map/ppermute | solution.py:20
  125.9 10.8 %copy-start.4 = (s32[4,4]{1,0:T(4,128)S(1)}, s32[4,4]{1,0:T(4,128)}, u32[]{:S(2)}) copy-start(s32[4,4]{1,0:T(4,128)} %ids_ref.3) | copy-start | bytes 196
  125.9 3.4 %collective-permute-start.4 = (bf16[192,384]{1,0:T(8,128)(2,1)S(1)}, bf16[192,384]{1,0:T(8,128)(2,1)S(1)}, u32[]{:S(2)}, u32[]{:S(2)}) collective-permute-start(bf16[192,384]{1,0:T(8,128)(2,1)S(1)} %get-tuple-element.22), channel_id=1, source_target_pairs={{0,8},{8,0},{1,9},{9,1},{2,10},{10,2},{3,11},{11,3},{4,12},{12,4},... | collective-permute-start | bytes 442376 | tf_op jit(solution)/shard_map/ppermute | solution.py:20

commit v11 on v10

--- a/solution.py
+++ b/solution.py
@@ -181,31 +181,23 @@
 
 
 def scatter_kernel(
-    parties, offset, after_ref, full_ref, own_ref, oth_ref, out_ref, dh_ref, act_ref, dh, act, own, oth, wide, out, sems
+    parties, offset, after_ref, full, own_ref, oth_ref, out_ref, dh_ref, act_ref, own, oth, wide, out, sems
 ):
     del after_ref
     width = own.shape[0]
     hidden = own.shape[1]
     step = width // PIECES
     span = out.shape[2] // PIECES
-    copies = start_all(
-        [
-            (full_ref.at[:, 0:hidden], dh.at[0]),
-            (full_ref.at[:, offset : offset + hidden], dh.at[1]),
-            (full_ref.at[:, offset + hidden : 2 * offset], act),
-        ],
-        sems,
-    )
     spans = [slice(p * step, (p + 1) * step) for p in range(PIECES)]
     pieces = [
         start_all([(own_ref.at[at, :], own.at[at, :]), (oth_ref.at[at, :], oth.at[at, :])], sems, 3 + 2 * p)
         for p, at in enumerate(spans)
     ]
-    wait_all(copies)
-    outs = start_all([(dh.at[1], dh_ref), (act, act_ref)], sems, 3 + 2 * PIECES)
+    dh, act = full.at[:, offset : offset + hidden], full.at[:, offset + hidden : 2 * offset]
+    outs = start_all([(dh, dh_ref), (act, act_ref)], sems, 3 + 2 * PIECES)
     for p, at in enumerate(spans):
         wait_all(pieces[p])
-        dx = dot(dh[0], own[at, :], ((1,), (1,))) + dot(dh[1], oth[at, :], ((1,), (1,)))
+        dx = dot(full[:, 0:hidden], own[at, :], ((1,), (1,))) + dot(dh[...], oth[at, :], ((1,), (1,)))
         for j in range(CAP):
             for k in range(step // LANE):
                 row, cols = place(j, p * (step // LANE) + k)
@@ -263,6 +255,7 @@
 
 
 ANY = pl.BlockSpec(memory_space=pl.ANY)
+VM = pl.BlockSpec(memory_space=pltpu.VMEM)
 SMEM = pl.BlockSpec(memory_space=pltpu.SMEM)
 
 
@@ -270,11 +263,11 @@
     return jax.ShapeDtypeStruct(shape, dtype)
 
 
-def call(kernel, outs, scratch, n_sems, flops, moved, *args, limit=FULL):
+def call(kernel, outs, scratch, n_sems, flops, moved, *args, limit=FULL, resident=()):
     return pl.pallas_call(
         kernel,
         out_shape=outs,
-        in_specs=[SMEM if a.shape == (1,) else ANY for a in args],
+        in_specs=[SMEM if a.shape == (1,) else VM if n in resident else ANY for n, a in enumerate(args)],
         out_specs=jax.tree.map(lambda _: ANY, outs),
         scratch_shapes=[pltpu.VMEM(*s) for s in scratch] + [pltpu.SemaphoreType.DMA((n_sems,))],
         compiler_params=pltpu.CompilerParams(vmem_limit_bytes=limit),
@@ -331,10 +324,10 @@
     hidden = width
     flat = array((parties, 2, CAP * width // 2))
     shapes = (flat, array((rows, hidden)), array((rows, height - width)))
-    scratch = [((2, rows, hidden), BF16)] + like(shapes[2], oth, oth) + [(flat.shape, F32), (flat.shape, BF16)]
+    scratch = like(oth, oth) + [(flat.shape, F32), (flat.shape, BF16)]
     kernel = functools.partial(scatter_kernel, parties, height)
     flops, moved = 4 * rows * width * hidden, 4 * own.size
-    return call(kernel, shapes, scratch, 5 + 3 * PIECES, flops, moved, after, full, own, oth, limit=SNUG)
+    return call(kernel, shapes, scratch, 5 + 3 * PIECES, flops, moved, after, full, own, oth, limit=SNUG, resident=(1,))
 
 
 def weight_grads(mine, theirs, full, dh, act, w_in, scale_in, w_out, scale_out):

time: 139 us -> 139 us (level)
  the two profiles are of different devices: /device:TPU:4 before, /device:TPU:16 now
where the time goes in v11:
time: 139 us; the launch traced here: 138 us
  starting transfers between devices  60.9 us (44%)
  waiting for transfers between devices  56.2 us (40%)
  Pallas kernels  20.5 us (15%)
    all_to_all x4, waiting for transfers between devices, exchange(): return lax.all_to_all(x, axes, split_axis=0, concat_axis=0, tiled=True)  51.4 us
    all_to_all x4, starting transfers between devices, exchange(): return lax.all_to_all(x, axes, split_axis=0, concat_axis=0, tiled=True)  50.3 us
    pallas_call x7, Pallas kernels, call(): pl.pallas_call(kernel, out_shape=outs, in_specs=[SMEM if a.shape == (1,)...  20.5 us
    ppermute x5, starting transfers between devices, swap(): return lax.ppermute(x, 'core', [(0, 1), (1, 0)])  10.6 us
    ppermute x5, waiting for transfers between devices, swap(): return lax.ppermute(x, 'core', [(0, 1), (1, 0)])  4.78 us
  transfers between devices with their start and end apart: 9, of which 7 were waited for; matrix products, arithmetic and copies ran while one was open for 0% of the time, Pallas kernels for 6%

profile of v11, /device:TPU:16, one launch (start us, length us, event | category | flops | bytes accessed | tf_op | source)
XLA Modules:
  0.0 138.4 jit_solution(6798485413060919750)
XLA Ops:
  0.6 1.9 %shard_map.103 = bf16[8,8,40,128]{3,2,1,0:T(8,128)(2,1)} custom-call(s32[4,4]{1,0:T(4,128)} %ids_ref.3, bf16[4,4]{1,0:T(4,128)(2,1)} %gates_ref.1, bf16[4,768]{1,0:T(4,128)(2,1)} %tok_ref.1, bf16[4,768]{1,0:T(4,128)(2,1)} %cot_ref.1), custom_call_target="tpu_custom_call" | custom-call | flops 1048576 | bytes 1048576 | tf_op jit(solution)/shard_map/pallas_call | solution.py:267
  2.5 17.1 %all-to-all-start = ((bf16[64,40,128]{2,1,0:T(8,128)(2,1)}), bf16[64,40,128]{2,1,0:T(8,128)(2,1)S(1)}, u32[]{:S(2)}, u32[]{:S(2)}) async-start(bf16[64,40,128]{2,1,0:T(8,128)(2,1)} %bitcast.14), calls=%async_computation | async-start | bytes 1310720 | tf_op jit(solution)/shard_map/all_to_all | solution.py:24
  19.6 3.7 %shard_map.104 = (bf16[1152,768]{1,0:T(8,128)(2,1)}, bf16[768,768]{1,0:T(8,128)(2,1)}, bf16[384,768]{1,0:T(8,128)(2,1)}) custom-call(bf16[64,40,128]{2,1,0:T(8,128)(2,1)} %bitcast.15, bf16[768,768]{1,0:T(8,128)(2,1)} %bitcast.16, bf16[1,768]{1,0:T(2,128)(2,1)} %refs_6_.1, bf16[384,768]{1,0:T(8,128)(2,1)} %bitcast.12, bf16[1,768]{1,0:T(2,128)(2,1)} %refs_8_.1), custom_call_target="tpu_custom_call" | custom-call | flops 3538944 | bytes 3538944 | tf_op jit(solution)/shard_map/pallas_call | solution.py:267
  23.3 1.9 %collective-permute-start = (bf16[768,768]{1,0:T(8,128)(2,1)}, bf16[768,768]{1,0:T(8,128)(2,1)S(1)}, u32[]{:S(2)}, u32[]{:S(2)}) collective-permute-start(bf16[768,768]{1,0:T(8,128)(2,1)} %get-tuple-element.15), channel_id=1, source_target_pairs={{0,8},{8,0},{1,9},{9,1},{2,10},{10,2},{3,11},{11,3},{4,12},{12,4},... | collective-permute-start | bytes 3538952 | tf_op jit(solution)/shard_map/ppermute | solution.py:20
  25.2 2.4 %collective-permute-start.1 = (bf16[384,768]{1,0:T(8,128)(2,1)}, bf16[384,768]{1,0:T(8,128)(2,1)S(1)}, u32[]{:S(2)}, u32[]{:S(2)}) collective-permute-start(bf16[384,768]{1,0:T(8,128)(2,1)} %get-tuple-element.16), channel_id=1, source_target_pairs={{0,8},{8,0},{1,9},{9,1},{2,10},{10,2},{3,11},{11,3},{4,12},{12,4},... | collective-permute-start | bytes 1769480 | tf_op jit(solution)/shard_map/ppermute | solution.py:20
  27.6 1.8 %collective-permute-done.1.oth_out_ref = bf16[384,768]{1,0:T(8,128)(2,1)S(1)} collective-permute-done((bf16[384,768]{1,0:T(8,128)(2,1)}, bf16[384,768]{1,0:T(8,128)(2,1)S(1)}, u32[]{:S(2)}, u32[]{:S(2)}) %collective-permute-start.1) | collective-permute-done | bytes 589856 | tf_op jit(solution)/shard_map/ppermute | solution.py:20
  29.5 0.0 collective-permute-done.oth_in_ref.oth_ref
  29.5 0.0 copy-start.5
  29.5 7.8 %all-to-all-done = bf16[64,40,128]{2,1,0:T(8,128)(2,1)S(1)} async-done(((bf16[64,40,128]{2,1,0:T(8,128)(2,1)}), bf16[64,40,128]{2,1,0:T(8,128)(2,1)S(1)}, u32[]{:S(2)}, u32[]{:S(2)}) %all-to-all-start) | async-done | bytes 655392 | tf_op jit(solution)/shard_map/all_to_all | solution.py:24
  37.3 0.0 copy-done.5
  37.3 3.8 %shard_map.105 = (bf16[192,2304]{1,0:T(8,128)(2,1)}, bf16[192,1536]{1,0:T(8,128)(2,1)S(1)}, f32[192,128]{1,0:T(8,128)S(1)}) custom-call(bf16[2560,128]{1,0:T(8,128)(2,1)S(1)} %bitcast.11, bf16[1152,768]{1,0:T(8,128)(2,1)} %get-tuple-element.14.own_ref, bf16[768,768]{1,0:T(8,128)(2,1)} %copy-done.5, bf16[384,768]{1,0:T(8,128)(2,1)S(1)} %collective-permute-done.1.oth_out_ref), custom_call_target="tpu_custom_call" | custom-call | flops 679477248 | bytes 5505024 | tf_op jit(solution)/shard_map/pallas_call | solution.py:267
  41.1 16.5 %all-to-all-start.1 = ((bf16[8,24,2304]{2,1,0:T(8,128)(2,1)}), bf16[8,24,2304]{2,1,0:T(8,128)(2,1)S(1)}, u32[]{:S(2)}, u32[]{:S(2)}) async-start(bf16[8,24,2304]{2,1,0:T(8,128)(2,1)} %bitcast.5), calls=%async_computation.1 | async-start | bytes 1769472 | tf_op jit(solution)/shard_map/all_to_all | solution.py:24
  57.6 21.9 %all-to-all-done.1.parts_ref = bf16[8,24,2304]{2,1,0:T(8,128)(2,1)S(1)} async-done(((bf16[8,24,2304]{2,1,0:T(8,128)(2,1)}), bf16[8,24,2304]{2,1,0:T(8,128)(2,1)S(1)}, u32[]{:S(2)}, u32[]{:S(2)}) %all-to-all-start.1) | async-done | bytes 884768 | tf_op jit(solution)/shard_map/all_to_all | solution.py:24
  79.5 1.3 shard_map.106
  80.8 3.6 %all-to-all-start.2 = ((bf16[8,24,2304]{2,1,0:T(8,128)(2,1)}), bf16[8,24,2304]{2,1,0:T(8,128)(2,1)S(1)}, u32[]{:S(2)}, u32[]{:S(2)}) async-start(bf16[8,24,2304]{2,1,0:T(8,128)(2,1)} %shard_map.106), calls=%async_computation.2 | async-start | bytes 1769472 | tf_op jit(solution)/shard_map/all_to_all | solution.py:24
  84.3 1.9 %collective-permute-start.2 = (bf16[192,1536]{1,0:T(8,128)(2,1)S(1)}, bf16[192,1536]{1,0:T(8,128)(2,1)S(1)}, u32[]{:S(2)}, u32[]{:S(2)}) collective-permute-start(bf16[192,1536]{1,0:T(8,128)(2,1)S(1)} %get-tuple-element.17.refs_0_), channel_id=1, source_target_pairs={{0,8},{8,0},{1,9},{9,1},{2,10},{10,2},{3,11},{11,3},{4,12},{12,4},... | collective-permute-start | bytes 1769480 | tf_op jit(solution)/shard_map/ppermute | solution.py:20
  86.3 2.0 %collective-permute-done.2.after_ref.refs_1_ = bf16[192,1536]{1,0:T(8,128)(2,1)S(1)} collective-permute-done((bf16[192,1536]{1,0:T(8,128)(2,1)S(1)}, bf16[192,1536]{1,0:T(8,128)(2,1)S(1)}, u32[]{:S(2)}, u32[]{:S(2)}) %collective-permute-start.2) | collective-permute-done | bytes 589856 | tf_op jit(solution)/shard_map/ppermute | solution.py:20
  88.2 18.1 %all-to-all-done.2 = bf16[8,24,2304]{2,1,0:T(8,128)(2,1)S(1)} async-done(((bf16[8,24,2304]{2,1,0:T(8,128)(2,1)}), bf16[8,24,2304]{2,1,0:T(8,128)(2,1)S(1)}, u32[]{:S(2)}, u32[]{:S(2)}) %all-to-all-start.2) | async-done | bytes 884768 | tf_op jit(solution)/shard_map/all_to_all | solution.py:24
  106.3 0.0 copy-start
  106.3 0.0 copy-start.1
  106.3 0.0 copy-start.2
  106.3 0.0 copy-start.3
  106.3 4.3 %shard_map.107 = (bf16[64,2,1152]{2,1,0:T(2,128)(2,1)}, bf16[192,768]{1,0:T(8,128)(2,1)S(1)}, bf16[192,384]{1,0:T(8,128)(2,1)S(1)}) custom-call(bf16[192,1536]{1,0:T(8,128)(2,1)S(1)} %collective-permute-done.2.after_ref.refs_1_, bf16[192,2304]{1,0:T(8,128)(2,1)S(1)} %bitcast.9, bf16[1152,768]{1,0:T(8,128)(2,1)} %get-tuple-element.14.own_ref, ...), custom_call_target="tpu_custom_call" | custom-call | flops 452984832 | bytes 3538944 | tf_op jit(solution)/shard_map/pallas_call | solution.py:267
  110.6 0.0 copy-done
  110.6 13.1 %all-to-all-start.3 = ((bf16[64,2,1152]{2,1,0:T(2,128)(2,1)}), bf16[64,2,1152]{2,1,0:T(2,128)(2,1)S(1)}, u32[]{:S(2)}, u32[]{:S(2)}) async-start(bf16[64,2,1152]{2,1,0:T(2,128)(2,1)} %get-tuple-element.20), calls=%async_computation.3 | async-start | bytes 589824 | tf_op jit(solution)/shard_map/all_to_all | solution.py:24
  123.7 1.9 %collective-permute-start.3 = (bf16[192,768]{1,0:T(8,128)(2,1)S(1)}, bf16[192,768]{1,0:T(8,128)(2,1)S(1)}, u32[]{:S(2)}, u32[]{:S(2)}) collective-permute-start(bf16[192,768]{1,0:T(8,128)(2,1)S(1)} %get-tuple-element.21), channel_id=1, source_target_pairs={{0,8},{8,0},{1,9},{9,1},{2,10},{10,2},{3,11},{11,3},{4,12},{12,4},... | collective-permute-start | bytes 884744 | tf_op jit(solution)/shard_map/ppermute | solution.py:20
  125.7 0.0 copy-start.4
  125.7 2.4 %collective-permute-start.4 = (bf16[192,384]{1,0:T(8,128)(2,1)S(1)}, bf16[192,384]{1,0:T(8,128)(2,1)S(1)}, u32[]{:S(2)}, u32[]{:S(2)}) collective-permute-start(bf16[192,384]{1,0:T(8,128)(2,1)S(1)} %get-tuple-element.22), channel_id=1, source_target_pairs={{0,8},{8,0},{1,9},{9,1},{2,10},{10,2},{3,11},{11,3},{4,12},{12,4},... | collective-permute-start | bytes 442376 | tf_op jit(solution)/shard_map/ppermute | solution.py:20
  128.1 1.0 collective-permute-done.4.refs_4_
  129.1 0.0 collective-permute-done.3.refs_3_
  129.1 0.0 copy-done.1
  129.1 0.0 copy-done.2
  129.1 0.0 copy-done.3
  129.1 4.0 %shard_map.109 = (bf16[768,768]{1,0:T(8,128)(2,1)}, bf16[384,768]{1,0:T(8,128)(2,1)}) custom-call(bf16[192,1536]{1,0:T(8,128)(2,1)S(1)} %get-tuple-element.17.refs_0_, bf16[192,1536]{1,0:T(8,128)(2,1)S(1)} %collective-permute-done.2.after_ref.refs_1_, bf16[192,2304]{1,0:T(8,128)(2,1)} %bitcast.10, bf16[192,768]{1,0:T(8,128)(2,1)S(1)} %collective-permute-done.3.refs_3_, ...), custom_call_target="tpu_custom_call" | custom-call | flops 1048576 | bytes 1048576 | tf_op jit(solution)/shard_map/pallas_call | solution.py:267
  133.1 3.7 %all-to-all-done.3.back_ref = bf16[64,2,1152]{2,1,0:T(2,128)(2,1)S(1)} async-done(((bf16[64,2,1152]{2,1,0:T(2,128)(2,1)}), bf16[64,2,1152]{2,1,0:T(2,128)(2,1)S(1)}, u32[]{:S(2)}, u32[]{:S(2)}) %all-to-all-start.3) | async-done | bytes 294944 | tf_op jit(solution)/shard_map/all_to_all | solution.py:24
  136.8 0.0 copy-done.4
  136.8 1.6 %shard_map.108 = bf16[4,768]{1,0:T(4,128)(2,1)} custom-call(s32[4,4]{1,0:T(4,128)S(1)} %copy-done.4, bf16[64,2,1152]{2,1,0:T(2,128)(2,1)S(1)} %all-to-all-done.3.back_ref), custom_call_target="tpu_custom_call" | custom-call | flops 1048576 | bytes 1048576 | tf_op jit(solution)/shard_map/pallas_call | solution.py:267
Async XLA Ops:
  2.5 34.7 %all-to-all-start = ((bf16[64,40,128]{2,1,0:T(8,128)(2,1)}), bf16[64,40,128]{2,1,0:T(8,128)(2,1)S(1)}, u32[]{:S(2)}, u32[]{:S(2)}) async-start(bf16[64,40,128]{2,1,0:T(8,128)(2,1)} %bitcast.14), calls=%async_computation | async-start | bytes 1310720 | tf_op jit(solution)/shard_map/all_to_all | solution.py:24
  23.3 6.2 %collective-permute-start = (bf16[768,768]{1,0:T(8,128)(2,1)}, bf16[768,768]{1,0:T(8,128)(2,1)S(1)}, u32[]{:S(2)}, u32[]{:S(2)}) collective-permute-start(bf16[768,768]{1,0:T(8,128)(2,1)} %get-tuple-element.15), channel_id=1, source_target_pairs={{0,8},{8,0},{1,9},{9,1},{2,10},{10,2},{3,11},{11,3},{4,12},{12,4},... | collective-permute-start | bytes 3538952 | tf_op jit(solution)/shard_map/ppermute | solution.py:20
  25.2 4.2 %collective-permute-start.1 = (bf16[384,768]{1,0:T(8,128)(2,1)}, bf16[384,768]{1,0:T(8,128)(2,1)S(1)}, u32[]{:S(2)}, u32[]{:S(2)}) collective-permute-start(bf16[384,768]{1,0:T(8,128)(2,1)} %get-tuple-element.16), channel_id=1, source_target_pairs={{0,8},{8,0},{1,9},{9,1},{2,10},{10,2},{3,11},{11,3},{4,12},{12,4},... | collective-permute-start | bytes 1769480 | tf_op jit(solution)/shard_map/ppermute | solution.py:20
  29.5 7.8 %copy-start.5 = (bf16[768,768]{1,0:T(8,128)(2,1)}, bf16[768,768]{1,0:T(8,128)(2,1)S(1)}, u32[]{:S(2)}) copy-start(bf16[768,768]{1,0:T(8,128)(2,1)S(1)} %collective-permute-done.oth_in_ref.oth_ref) | copy-start | bytes 3538948
  41.1 38.4 %all-to-all-start.1 = ((bf16[8,24,2304]{2,1,0:T(8,128)(2,1)}), bf16[8,24,2304]{2,1,0:T(8,128)(2,1)S(1)}, u32[]{:S(2)}, u32[]{:S(2)}) async-start(bf16[8,24,2304]{2,1,0:T(8,128)(2,1)} %bitcast.5), calls=%async_computation.1 | async-start | bytes 1769472 | tf_op jit(solution)/shard_map/all_to_all | solution.py:24
  80.8 25.5 %all-to-all-start.2 = ((bf16[8,24,2304]{2,1,0:T(8,128)(2,1)}), bf16[8,24,2304]{2,1,0:T(8,128)(2,1)S(1)}, u32[]{:S(2)}, u32[]{:S(2)}) async-start(bf16[8,24,2304]{2,1,0:T(8,128)(2,1)} %shard_map.106), calls=%async_computation.2 | async-start | bytes 1769472 | tf_op jit(solution)/shard_map/all_to_all | solution.py:24
  84.3 3.9 %collective-permute-start.2 = (bf16[192,1536]{1,0:T(8,128)(2,1)S(1)}, bf16[192,1536]{1,0:T(8,128)(2,1)S(1)}, u32[]{:S(2)}, u32[]{:S(2)}) collective-permute-start(bf16[192,1536]{1,0:T(8,128)(2,1)S(1)} %get-tuple-element.17.refs_0_), channel_id=1, source_target_pairs={{0,8},{8,0},{1,9},{9,1},{2,10},{10,2},{3,11},{11,3},{4,12},{12,4},... | collective-permute-start | bytes 1769480 | tf_op jit(solution)/shard_map/ppermute | solution.py:20
  106.3 4.3 %copy-start = (bf16[8,24,2304]{2,1,0:T(8,128)(2,1)}, bf16[8,24,2304]{2,1,0:T(8,128)(2,1)S(1)}, u32[]{:S(2)}) copy-start(bf16[8,24,2304]{2,1,0:T(8,128)(2,1)S(1)} %all-to-all-done.2) | copy-start | bytes 2654212
  106.3 22.8 %copy-start.1 = (bf16[1,384,768]{2,1,0:T(8,128)(2,1)S(1)}, bf16[1,384,768]{2,1,0:T(8,128)(2,1)}, u32[]{:S(2)}) copy-start(bf16[1,384,768]{2,1,0:T(8,128)(2,1)} %param.14) | copy-start | bytes 1769476
  106.3 22.8 %copy-start.2 = (bf16[1,768]{1,0:T(2,128)(2,1)S(1)}, bf16[1,768]{1,0:T(2,128)(2,1)}, u32[]{:S(2)}) copy-start(bf16[1,768]{1,0:T(2,128)(2,1)} %refs_6_.1) | copy-start | bytes 4612
  106.3 22.8 %copy-start.3 = (bf16[1,768]{1,0:T(2,128)(2,1)S(1)}, bf16[1,768]{1,0:T(2,128)(2,1)}, u32[]{:S(2)}) copy-start(bf16[1,768]{1,0:T(2,128)(2,1)} %refs_8_.1) | copy-start | bytes 4612
  110.6 26.1 %all-to-all-start.3 = ((bf16[64,2,1152]{2,1,0:T(2,128)(2,1)}), bf16[64,2,1152]{2,1,0:T(2,128)(2,1)S(1)}, u32[]{:S(2)}, u32[]{:S(2)}) async-start(bf16[64,2,1152]{2,1,0:T(2,128)(2,1)} %get-tuple-element.20), calls=%async_computation.3 | async-start | bytes 589824 | tf_op jit(solution)/shard_map/all_to_all | solution.py:24
  123.7 5.3 %collective-permute-start.3 = (bf16[192,768]{1,0:T(8,128)(2,1)S(1)}, bf16[192,768]{1,0:T(8,128)(2,1)S(1)}, u32[]{:S(2)}, u32[]{:S(2)}) collective-permute-start(bf16[192,768]{1,0:T(8,128)(2,1)S(1)} %get-tuple-element.21), channel_id=1, source_target_pairs={{0,8},{8,0},{1,9},{9,1},{2,10},{10,2},{3,11},{11,3},{4,12},{12,4},... | collective-permute-start | bytes 884744 | tf_op jit(solution)/shard_map/ppermute | solution.py:20
  125.7 11.1 %copy-start.4 = (s32[4,4]{1,0:T(4,128)S(1)}, s32[4,4]{1,0:T(4,128)}, u32[]{:S(2)}) copy-start(s32[4,4]{1,0:T(4,128)} %ids_ref.3) | copy-start | bytes 196
  125.7 3.4 %collective-permute-start.4 = (bf16[192,384]{1,0:T(8,128)(2,1)S(1)}, bf16[192,384]{1,0:T(8,128)(2,1)S(1)}, u32[]{:S(2)}, u32[]{:S(2)}) collective-permute-start(bf16[192,384]{1,0:T(8,128)(2,1)S(1)} %get-tuple-element.22), channel_id=1, source_target_pairs={{0,8},{8,0},{1,9},{9,1},{2,10},{10,2},{3,11},{11,3},{4,12},{12,4},... | collective-permute-start | bytes 442376 | tf_op jit(solution)/shard_map/ppermute | solution.py:20
